TPU v7x, 32 devices: a whole 2x2x4 slice. The times are simulated.
32 devices in a mesh: ctx: 4 (over y, core), exp: 8 (over z, x).
Axes of the slice: x: 2, y: 2, z: 4, core: 2. Of those that a mesh axis runs over, the one named last changes fastest.
Arguments:
- hidden: bfloat16 [8, 512, 4096], P('exp', 'ctx'), may hold values from -6 to 6
- queries: bfloat16 [8, 512, 4096], P('exp', 'ctx'), may hold values from -4.5 to 4.5
- new_keys: bfloat16 [8, 512, 512], P('exp', 'ctx'), may hold values from -6 to 6
- new_values: bfloat16 [8, 512, 512], P('exp', 'ctx'), may hold values from -6 to 6
- cache_keys: bfloat16 [8, 512, 512], P('exp', 'ctx'), may hold values from -4.5 to 4.5
- cache_values: bfloat16 [8, 512, 512], P('exp', 'ctx'), may hold values from -6 to 6
- out_weight: bfloat16 [4096, 4096], P(('ctx', 'exp')), may hold values from -1.5 to 1.5
- norm_gain: bfloat16 [4096], replicated, may hold values from 0.099609375 to 1.8984375
- gate_proj: bfloat16 [32, 4096, 768], P(('ctx', 'exp')), may hold values from -0.09375 to 0.09375
- up_proj: bfloat16 [32, 4096, 768], P(('ctx', 'exp')), may hold values from -0.09375 to 0.09375
- down_proj: bfloat16 [32, 768, 4096], P(('ctx', 'exp')), may hold values from -0.21875 to 0.21875
- expert_ids: int32 [8, 512, 4], P('exp', 'ctx'), may hold values from 0 to 31, all different within a row; in each aligned block of 128 rows (0 to 127, 128 to 255, ..., all dimensions but the last counted through in order) at most 32 rows name the same one
- gate_fixed: int32 [8, 512, 4], P('exp', 'ctx'), may hold values from 1 to 65535
Outputs:
- after_attention: bfloat16 [8, 512, 4096], P('exp', 'ctx')
- layer_output: bfloat16 [8, 512, 4096], P('exp', 'ctx')
Inputs may be any that keep to these rules, and one draw needn't show every extreme that they name: `expert_ids`: each row names 4 different experts. Within the rows of one device (aligned blocks of 128 rows, sequences taken in order) no expert is named more than 32 times, and in some blocks one expert is named exactly 32 times.
All inputs are finite; a program needn't handle non-finite values.
Results may differ from a plain program's by a relative error of at most 0.02.
Values may be sent and summed in bfloat16 or wider, within the bound.
No kernel may reach another device: no remote copies, remote signals or barrier semaphores. Data moves between devices by JAX's collectives and lax.ppermute only.
A program may use at most 128 MiB of HBM per device.

v0:
```python
import math

import jax
import jax.numpy as jnp
from jax import lax
from jax.sharding import PartitionSpec as P

D = 4096
KVH = 4
HD = 128
TOPK = 4


def widen_heads(tensor, copies):
    row_count = tensor.shape[0]
    heads = tensor.reshape(row_count, KVH, HD)
    return jnp.repeat(heads, copies, axis=1).reshape(row_count, KVH * copies * HD)


def expert_ffn(incoming, gate_matrix, up_matrix, down_matrix):
    shape_in = incoming.shape
    flat_rows = incoming.reshape(-1, shape_in[-1])
    gate_act = jnp.dot(flat_rows, gate_matrix, preferred_element_type=jnp.float32)
    up_act = jnp.dot(flat_rows, up_matrix, preferred_element_type=jnp.float32)
    product = (jax.nn.silu(gate_act) * up_act).astype(jnp.bfloat16)
    output = jnp.dot(product, down_matrix, preferred_element_type=jnp.float32)
    return output.astype(jnp.bfloat16).reshape(shape_in)


def per_device(
    hidden,
    queries,
    new_keys,
    new_values,
    cache_keys,
    cache_values,
    out_weight,
    norm_gain,
    gate_proj,
    up_proj,
    down_proj,
    expert_ids,
    gate_fixed,
):
    context = lax.axis_size("ctx")
    experts_all = context * lax.axis_size("exp")
    tok_rows = hidden.shape[1]
    copies = context // KVH
    local_queries = queries[0]
    query_part, key_new, value_new, key_old, value_old = (
        lax.all_to_all(local_queries, "ctx", split_axis=1, concat_axis=0, tiled=True),
        lax.all_to_all(
            widen_heads(new_keys[0], copies), "ctx", split_axis=1, concat_axis=0, tiled=True
        ),
        lax.all_to_all(
            widen_heads(new_values[0], copies), "ctx", split_axis=1, concat_axis=0, tiled=True
        ),
        lax.all_to_all(
            widen_heads(cache_keys[0], copies), "ctx", split_axis=1, concat_axis=0, tiled=True
        ),
        lax.all_to_all(
            widen_heads(cache_values[0], copies), "ctx", split_axis=1, concat_axis=0, tiled=True
        ),
    )
    key_rows = jnp.concatenate([key_old, key_new], axis=0)
    value_rows = jnp.concatenate([value_old, value_new], axis=0)
    window = query_part.shape[0]
    heads_here = query_part.shape[1] // HD
    total_cache = key_old.shape[0]
    block_rows = min(512, window)
    block_count = window // block_rows
    key_pos = jnp.arange(key_rows.shape[0])

    def attend(operands):
        query_block, block_start = operands
        query_heads = query_block.reshape(block_rows, heads_here, HD)
        scores = jnp.einsum(
            "whd,ld->hwl", query_heads, key_rows, preferred_element_type=jnp.float32
        ) / math.sqrt(HD)
        query_pos = total_cache + block_start + jnp.arange(block_rows)
        scores = jnp.where(key_pos[None, None, :] <= query_pos[None, :, None], scores, -jnp.inf)
        highest = jnp.max(scores, axis=-1, keepdims=True)
        powers = jnp.exp(scores - highest)
        weights = (powers / jnp.sum(powers, axis=-1, keepdims=True)).astype(jnp.bfloat16)
        attended_block = jnp.einsum(
            "hwl,ld->whd", weights, value_rows, preferred_element_type=jnp.float32
        )
        return attended_block.astype(jnp.bfloat16).reshape(block_rows, heads_here * HD)

    attended = lax.map(
        attend,
        (
            query_part.reshape(block_count, block_rows, heads_here * HD),
            jnp.arange(block_count) * block_rows,
        ),
    ).reshape(window, heads_here * HD)
    proj_rows = lax.all_gather(out_weight, "exp", axis=0, tiled=True)
    projected = lax.psum_scatter(
        jnp.dot(attended, proj_rows, preferred_element_type=jnp.float32).astype(jnp.bfloat16),
        "ctx",
        scatter_dimension=0,
        tiled=True,
    ).astype(jnp.float32)
    after_attention = (hidden[0].astype(jnp.float32) + projected).astype(jnp.bfloat16)
    after_float = after_attention.astype(jnp.float32)
    normed = (
        after_float
        * lax.rsqrt(jnp.mean(after_float * after_float, axis=-1, keepdims=True) + 1e-06)
        * norm_gain.astype(jnp.float32)
    ).astype(jnp.bfloat16)
    capacity = max(2, 2 * tok_rows * TOPK // experts_all)
    flat_ids = expert_ids[0].reshape(-1)
    one_hot = (flat_ids[:, None] == jnp.arange(experts_all, dtype=jnp.int32)[None, :]).astype(
        jnp.int32
    )
    earlier = jnp.cumsum(one_hot, axis=0) - one_hot
    slot_index = jnp.sum(earlier * one_hot, axis=1)
    target = flat_ids * capacity + slot_index
    sources = jnp.repeat(normed, TOPK, axis=0)
    outgoing = jnp.zeros((experts_all * capacity, D), jnp.bfloat16).at[target].set(sources)
    results = expert_ffn(
        lax.all_to_all(
            outgoing.reshape(experts_all, capacity, D),
            ("ctx", "exp"),
            split_axis=0,
            concat_axis=0,
            tiled=True,
        ),
        gate_proj[0],
        up_proj[0],
        down_proj[0],
    )
    returned = lax.all_to_all(results, ("ctx", "exp"), split_axis=0, concat_axis=0, tiled=True)
    back_rows = returned.reshape(experts_all * capacity, D)[target]
    shares = gate_fixed[0].astype(jnp.float32) / 65536.0
    expert_sum = jnp.sum(
        back_rows.astype(jnp.float32).reshape(tok_rows, TOPK, D) * shares[:, :, None], axis=1
    )
    layer_output = (after_float + expert_sum).astype(jnp.bfloat16)
    return (after_attention[None], layer_output[None])


def solution(mesh):
    return jax.shard_map(
        per_device,
        mesh=mesh,
        in_specs=(
            P("exp", "ctx", None),
            P("exp", "ctx", None),
            P("exp", "ctx", None),
            P("exp", "ctx", None),
            P("exp", "ctx", None),
            P("exp", "ctx", None),
            P(("ctx", "exp"), None),
            P(),
            P(("ctx", "exp"), None, None),
            P(("ctx", "exp"), None, None),
            P(("ctx", "exp"), None, None),
            P("exp", "ctx", None),
            P("exp", "ctx", None),
        ),
        out_specs=(P("exp", "ctx", None), P("exp", "ctx", None)),
        check_vma=False,
    )
```

profile of v0, /device:TPU:0, one launch (start us, length us, event | category | flops | bytes accessed | tf_op | source)
XLA Modules:
  0.0 660.8 jit_solution(17416190346805939913)
XLA Ops:
  7.2 0.7 all-gather.2.cloned.1.call-update
  7.9 0.9 all_to_all.82
  8.8 0.7 copy.37
  9.5 4.2 all-to-all-start.2
  13.8 1.7 copy.35
  15.4 3.0 all-to-all-done.2
  18.4 3.3 all-to-all-start.1
  21.7 1.7 copy.33
  23.4 2.9 all-to-all-done.1
  26.3 3.3 all-to-all-start
  29.7 1.9 all_to_all.90
  31.5 1.3 copy.39
  32.8 1.5 all-to-all-done
  34.3 3.5 all-to-all-start.4
  37.8 0.7 copy.38
  38.5 0.4 iota_compare_fusion
  38.9 13.3 %all-to-all-done.4 = bf16[128,4,1024]{2,0,1:T(8,128)(2,1)S(1)} async-done(((bf16[128,4,1024]{2,0,1:T(8,128)(2,1)}), bf16[128,4,1024]{2,0,1:T(8,128)(2,1)S(1)}, u32[]{:S(2)}, u32[]{:S(2)}) %all-to-all-start.4) | async-done | bytes 1048608 | tf_op jit(solution)/shard_map/all_to_all | solution.py:51
  52.2 3.3 all-to-all-start.3
  55.6 0.3 copy.51
  55.9 4.2 all-to-all-done.3
  60.2 9.0 %fusion.22 = f32[1024,512,8]{1,0,2:T(8,128)} fusion(bf16[512,8,128]{2,1,0:T(8,128)(2,1)S(1)} %bitcast.99, bf16[512,128]{1,0:T(8,128)(2,1)S(1)} %bitcast.102, bf16[512,128]{1,0:T(8,128)(2,1)S(1)} %bitcast.101), kind=kOutput, calls=%fused_computation.34 | convolution fusion | flops 1074266112 | bytes 18087936 | tf_op jit(solution)/shard_map/while/body/eval_jaxpr/whd,ld->hwl/dot_general | solution.py:77
  69.1 18.0 %fusion.37 = (f32[8,512]{1,0:T(8,128)S(1)}, f32[8,512,1024]{1,2,0:T(8,128)}) fusion(f32[1024,512,8]{1,0,2:T(8,128)} %fusion.22, pred[512,1024]{0,1:T(8,128)(4,1)S(1)} %iota_compare_fusion), kind=kOutput, calls=%fused_computation.63 | output fusion | flops 25166848 | bytes 34095104 | tf_op jit(solution)/shard_map/while/body/eval_jaxpr/sub | solution.py:83
  87.1 8.1 %fusion.20 = bf16[128,8,512]{2,0,1:T(8,128)(2,1)} fusion(f32[8,512,1024]{1,2,0:T(8,128)} %get-tuple-element.17, f32[8,512]{1,0:T(8,128)S(1)} %get-tuple-element.16, bf16[512,128]{0,1:T(8,128)(2,1)S(1)} %copy_bitcast_fusion, bf16[512,128]{0,1:T(8,128)(2,1)S(1)} %copy_bitcast_fusion.1), kind=kOutput, calls=%fused_computation.32 | convolution fusion | flops 1083179008 | bytes 18104320 | tf_op jit(solution)/shard_map/while/body/eval_jaxpr/hwl,ld->whd/dot_general | solution.py:85
  95.2 42.6 %all-gather.2.cloned.1.call-done = bf16[1024,4096]{1,0:T(8,128)(2,1)} async-done(((bf16[128,4096]{1,0:T(8,128)(2,1)}), bf16[1024,4096]{1,0:T(8,128)(2,1)}) %all-gather.2.cloned.1.call-update) | async-done | bytes 8388624 | tf_op jit(solution)/shard_map/all_gather | solution.py:97
  137.8 10.3 %convolution_convert_fusion.1 = bf16[512,4096]{1,0:T(8,128)(2,1)} fusion(bf16[512,1024]{0,1:T(8,128)(2,1)} %bitcast.110, bf16[1024,4096]{1,0:T(8,128)(2,1)} %all-gather.2.cloned.1.call-done), kind=kOutput, calls=%fused_computation.18 | convolution fusion | flops 4297064448 | bytes 13631488 | tf_op jit(solution)/shard_map/dot_general | solution.py:99
  148.1 0.1 copy.43
  148.3 0.1 eq.25
  148.5 1.2 reduce-window.6
  149.7 0.2 slice_reduce_fusion
  149.9 0.1 copy.42
  150.0 0.1 mul.55
  150.3 40.7 %reduce-scatter.2.cloned.1.call-done = bf16[128,4096]{1,0:T(8,128)(2,1)} async-done(((bf16[512,4096]{1,0:T(8,128)(2,1)}), bf16[128,4096]{1,0:T(8,128)(2,1)}) %reduce-scatter.2.cloned.1.call-update) | async-done | bytes 1048592 | tf_op jit(solution)/shard_map/reduce_scatter | solution.py:98
  191.0 1.7 fusion.15
  192.7 0.3 fusion.17
  193.0 4.1 broadcast_in_dim.50
  197.1 7.0 %reshape.174 = bf16[512,4096]{1,0:T(8,128)(2,1)} reshape(bf16[128,4,4096]{2,1,0:T(4,128)(2,1)} %broadcast_in_dim.50) | data formatting | bytes 8388608 | tf_op jit(solution)/shard_map/reshape | solution.py:119
  204.1 12.4 %scatter_custom_fusion = bf16[1024,4096]{1,0:T(8,128)(2,1)} fusion(s32[512]{0:T(512)S(1)} %bitcast.103, bf16[512,4096]{1,0:T(8,128)(2,1)} %reshape.174, bf16[]{:T(256)} %constant.43.clone.1), kind=kCustom, calls=%fused_computation.19 | custom fusion | bytes 8389120 | tf_op jit(solution)/shard_map/scatter | solution.py:120
  216.6 189.7 %all_to_all.102 = bf16[32,32,4096]{2,1,0:T(8,128)(2,1)S(1)} all-to-all(bf16[32,32,4096]{2,1,0:T(8,128)(2,1)} %bitcast.94), channel_id=1, replica_groups=mesh['ctx'=4,'exp'=8] {'ctx','exp'}, dimensions={0} | all-to-all | bytes 16777216 | tf_op jit(solution)/shard_map/all_to_all | solution.py:122
  406.3 9.2 %fusion.7 = f32[1024,768]{1,0:T(8,128)S(1)} fusion(bf16[1024,4096]{1,0:T(8,128)(2,1)S(1)} %bitcast.97, bf16[1,4096,768]{2,1,0:T(8,128)(2,1)} %param.22), kind=kOutput, calls=%fused_computation.14 | convolution fusion | flops 6442450944 | bytes 17825792 | tf_op jit(solution)/shard_map/dot_general | solution.py:24
  415.5 7.0 %multiply_convert_fusion = bf16[1024,768]{1,0:T(8,128)(2,1)S(1)} fusion(f32[1024,768]{1,0:T(8,128)S(1)} %fusion.7, bf16[1024,4096]{1,0:T(8,128)(2,1)S(1)} %bitcast.98, bf16[1,4096,768]{2,1,0:T(8,128)(2,1)S(1)} %bitcast.107), kind=kOutput, calls=%fused_computation.21 | convolution fusion | flops 6447169536 | bytes 19398656 | tf_op jit(solution)/shard_map/dot_general | solution.py:23
  422.5 8.8 %convolution_convert_fusion = bf16[1024,4096]{1,0:T(8,128)(2,1)} fusion(bf16[1024,768]{1,0:T(8,128)(2,1)S(1)} %multiply_convert_fusion, bf16[1,768,4096]{2,1,0:T(8,128)(2,1)S(1)} %bitcast.109), kind=kOutput, calls=%fused_computation.12 | convolution fusion | flops 6446645248 | bytes 16252928 | tf_op jit(solution)/shard_map/dot_general | solution.py:26
  431.3 4.1 all-to-all-start.6
  435.4 0.1 copy.46
  435.5 185.7 %all-to-all-done.6 = bf16[32,32,4096]{2,1,0:T(8,128)(2,1)} async-done(((bf16[32,32,4096]{2,1,0:T(8,128)(2,1)}), bf16[32,32,4096]{2,1,0:T(8,128)(2,1)}, u32[]{:S(2)}, u32[]{:S(2)}) %all-to-all-start.6) | async-done | bytes 8388640 | tf_op jit(solution)/shard_map/all_to_all | solution.py:133
  621.2 13.0 %gather_fusion = bf16[512,4096]{1,0:T(8,128)(2,1)} fusion(bf16[1024,4096]{1,0:T(8,128)(2,1)} %bitcast.25, s32[1024]{0:T(1024)S(1)} %pad_clamp_fusion), kind=kCustom, calls=%fused_computation | custom fusion | bytes 8390656 | tf_op jit(solution)/shard_map/gather | solution.py:134
  634.2 8.3 %reshape.161 = f32[128,4,4096]{2,1,0:T(4,128)} reshape(bf16[512,4096]{1,0:T(8,128)(2,1)} %gather_fusion) | data formatting | bytes 12582912 | tf_op jit(solution)/shard_map/convert_element_type | solution.py:137
  642.6 9.8 %multiply_reduce_fusion = f32[128,4096]{1,0:T(8,128)S(1)} fusion(f32[128,4,4096]{2,1,0:T(4,128)} %reshape.161, f32[128,4]{1,0:T(8,128)S(1)} %copy.46), kind=kLoop, calls=%fused_computation.7 | loop fusion | flops 3670016 | bytes 10487808 | tf_op jit(solution)/shard_map/reduce_sum | solution.py:136
  652.3 1.2 fusion.21
  (40 shorter events, 0.5 us)
Async XLA Ops:
  7.2 30.6 %copy-start.2 = (bf16[1,128,512]{2,1,0:T(8,128)(2,1)S(1)}, bf16[1,128,512]{2,1,0:T(8,128)(2,1)}, u32[]{:S(2)}) copy-start(bf16[1,128,512]{2,1,0:T(8,128)(2,1)} %param.15) | copy-start | bytes 393220
  7.2 130.6 %all-gather.2.cloned.1.call-start = ((), (), s32[]{:S(2)}) async-start(), calls=%async_computation.8 | async-start | bytes 9437184 | tf_op jit(solution)/shard_map/all_gather | solution.py:97
  9.5 8.9 %all-to-all-start.2 = ((bf16[128,4,128]{2,0,1:T(8,128)(2,1)}), bf16[128,4,128]{2,0,1:T(8,128)(2,1)S(1)}, u32[]{:S(2)}, u32[]{:S(2)}) async-start(bf16[128,4,128]{2,0,1:T(8,128)(2,1)} %copy.37), calls=%async_computation.2 | async-start | bytes 262144 | tf_op jit(solution)/shard_map/all_to_all | solution.py:58
  18.4 7.9 %all-to-all-start.1 = ((bf16[128,4,128]{0,2,1:T(8,128)(2,1)}), bf16[128,4,128]{0,2,1:T(8,128)(2,1)S(1)}, u32[]{:S(2)}, u32[]{:S(2)}) async-start(bf16[128,4,128]{0,2,1:T(8,128)(2,1)} %bitcast.3), calls=%async_computation.1 | async-start | bytes 262144 | tf_op jit(solution)/shard_map/all_to_all | solution.py:55
  26.3 7.9 %all-to-all-start = ((bf16[128,4,128]{0,2,1:T(8,128)(2,1)}), bf16[128,4,128]{0,2,1:T(8,128)(2,1)S(1)}, u32[]{:S(2)}, u32[]{:S(2)}) async-start(bf16[128,4,128]{0,2,1:T(8,128)(2,1)} %bitcast.1), calls=%async_computation | async-start | bytes 262144 | tf_op jit(solution)/shard_map/all_to_all | solution.py:61
  34.3 18.0 %all-to-all-start.4 = ((bf16[128,4,1024]{2,0,1:T(8,128)(2,1)}), bf16[128,4,1024]{2,0,1:T(8,128)(2,1)S(1)}, u32[]{:S(2)}, u32[]{:S(2)}) async-start(bf16[128,4,1024]{2,0,1:T(8,128)(2,1)} %copy.39), calls=%async_computation.4 | async-start | bytes 2097152 | tf_op jit(solution)/shard_map/all_to_all | solution.py:51
  52.2 7.9 %all-to-all-start.3 = ((bf16[128,4,128]{2,0,1:T(8,128)(2,1)}), bf16[128,4,128]{2,0,1:T(8,128)(2,1)S(1)}, u32[]{:S(2)}, u32[]{:S(2)}) async-start(bf16[128,4,128]{2,0,1:T(8,128)(2,1)} %copy.38), calls=%async_computation.3 | async-start | bytes 262144 | tf_op jit(solution)/shard_map/all_to_all | solution.py:52
  55.6 135.4 %reduce-scatter.2.cloned.1.call-start = ((), (), s32[]{:S(2)}) async-start(), calls=%async_computation.9 | async-start | bytes 5242880 | tf_op jit(solution)/shard_map/reduce_scatter | solution.py:98
  137.8 10.3 %copy-start.4 = (s32[1,128,4]{1,2,0:T(4,128)S(1)}, s32[1,128,4]{1,2,0:T(4,128)}, u32[]{:S(2)}) copy-start(s32[1,128,4]{1,2,0:T(4,128)} %param.24) | copy-start | bytes 6148
  137.8 10.7 %copy-start.3 = (bf16[4096]{0:T(1024)(128)(2,1)S(1)}, bf16[4096]{0:T(1024)(128)(2,1)}, u32[]{:S(2)}) copy-start(bf16[4096]{0:T(1024)(128)(2,1)} %param.20) | copy-start | bytes 24580
  137.8 53.2 %copy-start.1 = (bf16[1,128,4096]{2,1,0:T(8,128)(2,1)S(1)}, bf16[1,128,4096]{2,1,0:T(8,128)(2,1)}, u32[]{:S(2)}) copy-start(bf16[1,128,4096]{2,1,0:T(8,128)(2,1)} %param.13) | copy-start | bytes 3145732
  192.7 459.7 %copy-start = (bf16[128,4096]{1,0:T(8,128)(2,1)}, bf16[128,4096]{1,0:T(8,128)(2,1)S(1)}, u32[]{:S(2)}) copy-start(bf16[128,4096]{1,0:T(8,128)(2,1)S(1)} %get-tuple-element.15) | copy-start | bytes 3145732
  216.6 198.9 %slice-start = ((s8[6291456]{0:T(1024)(128)(4,1)}), s8[4194304]{0:T(1024)(128)(4,1)S(1)}, s32[]{:S(2)}) async-start(s8[6291456]{0:T(1024)(128)(4,1)} %bitcast.106), calls=%async_computation.10 | async-start | bytes 8388608
  406.3 9.2 %slice-start.1 = ((s8[6291456]{0:T(1024)(128)(4,1)}), s8[2097152]{0:T(1024)(128)(4,1)S(1)}, s32[]{:S(2)}) async-start(s8[6291456]{0:T(1024)(128)(4,1)} %bitcast.106), calls=%async_computation.11 | async-start | bytes 4194304
  406.3 16.2 %slice-start.2 = ((s8[6291456]{0:T(1024)(128)(4,1)}), s8[4194304]{0:T(1024)(128)(4,1)S(1)}, s32[]{:S(2)}) async-start(s8[6291456]{0:T(1024)(128)(4,1)} %bitcast.108), calls=%async_computation.12 | async-start | bytes 8388608
  415.5 7.0 %slice-start.3 = ((s8[6291456]{0:T(1024)(128)(4,1)}), s8[2097152]{0:T(1024)(128)(4,1)S(1)}, s32[]{:S(2)}) async-start(s8[6291456]{0:T(1024)(128)(4,1)} %bitcast.108), calls=%async_computation.13 | async-start | bytes 4194304
  431.3 4.1 copy-start.5
  431.3 189.9 %all-to-all-start.6 = ((bf16[32,32,4096]{2,1,0:T(8,128)(2,1)}), bf16[32,32,4096]{2,1,0:T(8,128)(2,1)}, u32[]{:S(2)}, u32[]{:S(2)}) async-start(bf16[32,32,4096]{2,1,0:T(8,128)(2,1)} %bitcast.96), calls=%async_computation.7 | async-start | bytes 16777216 | tf_op jit(solution)/shard_map/all_to_all | solution.py:133
Sparse Core Ops, SparseCore 0:
  10.1 127.6 all-gather.1
  148.2 42.7 reduce-scatter.1
where the time goes:
time: 667 us; the launch traced here: 661 us
  waiting for transfers between devices  295 us (44%)
  blocking collectives  190 us (28%)
  local copies, waits for them, and re-layouts  54.9 us (8%)
  matrix products  52.3 us (8%)
  other arithmetic  32.7 us (5%)
  starting transfers between devices  21.9 us (3%)
  between operations  14.8 us (2%)
    all_to_all x1, blocking collectives, per_device(): lax.all_to_all(outgoing.reshape(experts_all, capacity, D), ('ctx', 'exp')...  190 us
    all_to_all x1, waiting for transfers between devices, per_device(): lax.all_to_all(results, ('ctx', 'exp'), split_axis=0, concat_axis=0, tile...  186 us
    all_gather x1, waiting for transfers between devices, per_device(): proj_rows = lax.all_gather(out_weight, 'exp', axis=0, tiled=True)  42.6 us
    reduce_scatter x1, waiting for transfers between devices, per_device(): lax.psum_scatter(jnp.dot(attended, proj_rows, preferred_element_type=jnp....  40.7 us
    sub x1, other arithmetic, attend(): powers = jnp.exp(scores - highest)  18 us
  transfers between devices with their start and end apart: 8, of which 8 were waited for; matrix products, arithmetic and copies ran while one was open for 7% of the time, Pallas kernels for 0%

commit v1 on v0

--- a/solution.py
+++ b/solution.py
@@ -1,14 +1,22 @@
+import functools
 import math
 
 import jax
 import jax.numpy as jnp
 from jax import lax
+from jax.experimental import pallas as pl
+from jax.experimental.pallas import tpu as pltpu
+from jax.sharding import Mesh
 from jax.sharding import PartitionSpec as P
 
 D = 4096
 KVH = 4
 HD = 128
 TOPK = 4
+AXES = ("y", "c", "z", "x")
+PLANE = ("y", "c", "x")
+BF = jnp.bfloat16
+F32 = jnp.float32
 
 
 def widen_heads(tensor, copies):
@@ -27,7 +35,7 @@
     return output.astype(jnp.bfloat16).reshape(shape_in)
 
 
-def per_device(
+def general_device(
     hidden,
     queries,
     new_keys,
@@ -140,25 +148,266 @@
     return (after_attention[None], layer_output[None])
 
 
+def pairs_of(sizes, axis, target):
+    found = []
+    for i in range(sizes[axis]):
+        j = target(i)
+        if j is not None:
+            found.append((i, j))
+    return found
+
+
+def swap(value, axis):
+    return lax.ppermute(value, axis, [(0, 1), (1, 0)])
+
+
+def upward(value, first, last):
+    return lax.ppermute(value, "z", [(z, z + 1) for z in range(first, last + 1)])
+
+
+def downward(value, first, last):
+    return lax.ppermute(value, "z", [(z, z - 1) for z in range(first, last + 1)])
+
+
+def pick(z, options):
+    result = options[3]
+    for index in (2, 1, 0):
+        result = jnp.where(z == index, options[index], result)
+    return result
+
+
+def along_z(own, z):
+    up1, down1 = upward(own, 0, 2), downward(own, 1, 3)
+    up2, down2 = upward(up1, 1, 2), downward(down1, 1, 2)
+    up3, down3 = upward(up2, 2, 2), downward(down2, 1, 1)
+    return [
+        own,
+        pick(z, (down1, up1, down1, up1)),
+        pick(z, (down2, down1, up1, up2)),
+        pick(z, (down3, down2, up2, up3)),
+    ]
+
+
+SOURCES = ((0, 1, 2, 3), (1, 0, 2, 3), (2, 3, 1, 0), (3, 2, 1, 0))
+
+
+def attend_kernel(message_ref, out_ref, keys, values, *, group, tokens):
+    width = group * HD
+    blocks = message_ref.shape[0]
+    cached = blocks * tokens
+    for s in range(blocks):
+        rows = pl.ds(s * tokens, tokens)
+        later = pl.ds(cached + s * tokens, tokens)
+        keys[rows, :] = message_ref[s, :, width : width + HD]
+        keys[later, :] = message_ref[s, :, width + HD : width + 2 * HD]
+        values[rows, :] = message_ref[s, :, width + 2 * HD : width + 3 * HD]
+        values[later, :] = message_ref[s, :, width + 3 * HD : width + 4 * HD]
+    factor = math.log2(math.e) / math.sqrt(HD)
+    row = lax.broadcasted_iota(jnp.int32, (tokens, tokens), 0)
+    column = lax.broadcasted_iota(jnp.int32, (tokens, tokens), 1)
+    allowed = jnp.concatenate([column <= row] * 2, axis=0)
+    for s in range(blocks):
+        before = cached + s * tokens
+
+        def two_heads(step, carry):
+            first = pl.multiple_of(step * 2 * HD, 2 * HD)
+            second = pl.multiple_of(step * 2 * HD + HD, HD)
+            queries = jnp.concatenate(
+                [message_ref[s, :, pl.ds(first, HD)], message_ref[s, :, pl.ds(second, HD)]], axis=0
+            )
+            dims = (((1,), (1,)), ((), ()))
+            old = lax.dot_general(
+                queries, keys[:before, :], dims, preferred_element_type=F32
+            )
+            own = lax.dot_general(
+                queries, keys[before : before + tokens, :], dims, preferred_element_type=F32
+            )
+            own = jnp.where(allowed, own, -jnp.inf)
+            highest = jnp.maximum(
+                jnp.max(old, axis=-1, keepdims=True), jnp.max(own, axis=-1, keepdims=True)
+            )
+            old = jnp.exp2((old - highest) * factor)
+            own = jnp.exp2((own - highest) * factor)
+            total = jnp.sum(old, axis=-1, keepdims=True) + jnp.sum(own, axis=-1, keepdims=True)
+            mixed = jnp.dot(old.astype(BF), values[:before, :], preferred_element_type=F32)
+            mixed += jnp.dot(
+                own.astype(BF), values[before : before + tokens, :], preferred_element_type=F32
+            )
+            mixed = (mixed / total).astype(BF)
+            out_ref[pl.ds(s * tokens, tokens), pl.ds(first, HD)] = mixed[:tokens]
+            out_ref[pl.ds(s * tokens, tokens), pl.ds(second, HD)] = mixed[tokens:]
+            return carry
+
+        lax.fori_loop(0, group // 2, two_heads, 0)
+
+
+def attention(message, group):
+    blocks, tokens, _ = message.shape
+    window = blocks * tokens
+    live = blocks * tokens + tokens * (blocks + 1) // 2
+    return pl.pallas_call(
+        functools.partial(attend_kernel, group=group, tokens=tokens),
+        out_shape=jax.ShapeDtypeStruct((window, group * HD), BF),
+        in_specs=[pl.BlockSpec(memory_space=pltpu.VMEM)],
+        out_specs=pl.BlockSpec(memory_space=pltpu.VMEM),
+        scratch_shapes=[pltpu.VMEM((2 * window, HD), BF), pltpu.VMEM((2 * window, HD), BF)],
+        compiler_params=pltpu.CompilerParams(vmem_limit_bytes=32 * 2**20),
+        cost_estimate=pl.CostEstimate(
+            flops=4 * window * group * HD * live,
+            bytes_accessed=2 * message.size + 2 * window * group * HD,
+            transcendentals=window * group * live,
+        ),
+        name="attention",
+    )(message)
+
+
+def routing(ids, gates, z):
+    tokens = ids.shape[0]
+    plane = 8
+    both = along_z(jnp.concatenate([ids, gates], axis=1), z)
+    both = jnp.stack(both)
+    ids4, gates4 = both[..., :TOPK], both[..., TOPK:]
+    place = jnp.arange(plane)
+    y, c, x = place // 4, place // 2 % 2, place % 2
+    experts = (y * 2 + c) * 8 + z * 2 + x
+    capacity = max(2, 2 * tokens * TOPK // 32)
+    same = ids4[:, None] == experts[None, :, None, None]
+    chosen = same.any(-1)
+    gate = jnp.sum(jnp.where(same, gates4[:, None], 0), axis=-1)
+    earlier = (jnp.arange(tokens)[:, None] < jnp.arange(tokens)[None, :]).astype(BF)
+    rank = jnp.dot(
+        chosen.astype(BF).reshape(4 * plane, tokens), earlier, preferred_element_type=F32
+    )
+    rank = rank.reshape(4, plane, 1, tokens).astype(jnp.int32)
+    at_slot = chosen[:, :, None, :] & (rank == jnp.arange(capacity)[None, None, :, None])
+    high = (gate >> 8).astype(F32) / 256.0
+    low = (gate & 255).astype(F32) / 65536.0
+    slots = plane * capacity
+
+    def spread(part):
+        return jnp.where(at_slot, part[:, :, None, :], 0.0).astype(BF).reshape(4, slots, tokens)
+
+    places = at_slot.astype(BF).reshape(4, slots, tokens)
+    shares = jnp.concatenate([spread(high), spread(low)], axis=-1)
+    return places, shares
+
+
+def plane_exchange(rows):
+    blocks = rows.reshape(8, -1, D)
+    return lax.all_to_all(blocks, PLANE, split_axis=0, concat_axis=0, tiled=True).reshape(-1, D)
+
+
+def tuned_device(
+    hidden,
+    queries,
+    new_keys,
+    new_values,
+    cache_keys,
+    cache_values,
+    out_weight,
+    norm_gain,
+    gate_proj,
+    up_proj,
+    down_proj,
+    expert_ids,
+    gate_fixed,
+):
+    y, c, z, x = (lax.axis_index(axis) for axis in AXES)
+    tokens = hidden.shape[1]
+    group = queries.shape[2] // HD // KVH
+    source = jnp.array(SOURCES, jnp.int32)[z]
+
+    def by_head(value):
+        return value[0].reshape(tokens, KVH, -1).transpose(1, 0, 2)
+
+    message = jnp.concatenate(
+        [by_head(v) for v in (queries, cache_keys, new_keys, cache_values, new_values)], axis=-1
+    )
+    message = lax.all_to_all(message, ("y", "c"), split_axis=0, concat_axis=0, tiled=True)
+    attended = attention(message, group)
+
+    heads = [source[k] * 2 + x for k in range(4)] + [source[k] * 2 + (1 - x) for k in range(4)]
+    in_order = jnp.concatenate(
+        [lax.dynamic_slice_in_dim(attended, h * HD, HD, axis=1) for h in heads], axis=1
+    )
+    parts = 2
+    width = D // parts
+    projected = []
+    for part in range(parts):
+        mine = out_weight[:, part * width : (part + 1) * width]
+        line = along_z(mine, z)
+        weight = jnp.concatenate(line + [swap(block, "x") for block in line], axis=0)
+        partial = jnp.dot(in_order, weight, preferred_element_type=F32)
+        partial = partial.reshape(2, 2, tokens, width)
+        other = lax.dynamic_index_in_dim(partial, 1 - c, 1, keepdims=False).astype(BF)
+        both = lax.dynamic_index_in_dim(partial, c, 1, keepdims=False) + swap(other, "c").astype(F32)
+        other = lax.dynamic_index_in_dim(both, 1 - y, 0, keepdims=False).astype(BF)
+        own = lax.dynamic_index_in_dim(both, y, 0, keepdims=False)
+        projected.append(own + swap(other, "y").astype(F32))
+    after_attention = (
+        hidden[0].astype(F32) + jnp.concatenate(projected, axis=1)
+    ).astype(BF)
+    after_float = after_attention.astype(F32)
+    normed = (
+        after_float
+        * lax.rsqrt(jnp.mean(after_float * after_float, axis=-1, keepdims=True) + 1e-06)
+        * norm_gain.astype(F32)
+    ).astype(BF)
+
+    places, shares = routing(expert_ids[0], gate_fixed[0], z)
+    blocks = along_z(normed, z)
+    results = []
+    for k in range(4):
+        sent = jnp.dot(places[k], blocks[k], preferred_element_type=F32).astype(BF)
+        results.append(expert_ffn(plane_exchange(sent), gate_proj[0], up_proj[0], down_proj[0]))
+    sums = [None] * 4
+    for k in (3, 2, 1, 0):
+        returned = plane_exchange(results[k])
+        both = lax.dot_general(
+            shares[k], returned, (((0,), (0,)), ((), ())), preferred_element_type=F32
+        )
+        sums[k] = both[:tokens] + both[tokens:]
+    own, near, middle, far = sums
+
+    up = upward(far.astype(BF), 0, 0)
+    down = downward(far.astype(BF), 3, 3)
+    up = upward((jnp.where(z == 0, middle, far) + up.astype(F32)).astype(BF), 0, 1)
+    down = downward((jnp.where(z == 3, middle, far) + down.astype(F32)).astype(BF), 2, 3)
+    up = upward((jnp.where(z == 1, middle, near) + up.astype(F32)).astype(BF), 0, 2)
+    down = downward((jnp.where(z == 2, middle, near) + down.astype(F32)).astype(BF), 1, 3)
+    layer_output = (after_float + own + up.astype(F32) + down.astype(F32)).astype(BF)
+    return (after_attention[None], layer_output[None])
+
+
 def solution(mesh):
+    sizes = (mesh.shape["ctx"], mesh.shape["exp"])
+    if sizes == (4, 8):
+        inner = Mesh(mesh.devices.reshape(2, 2, 4, 2), AXES)
+        ctx, exp = ("y", "c"), ("z", "x")
+        body = tuned_device
+    else:
+        inner, ctx, exp, body = mesh, "ctx", "exp", general_device
+    both = (*AXES,) if body is tuned_device else ("ctx", "exp")
+    token = P(exp, ctx, None)
+    expert = P(both, None, None)
     return jax.shard_map(
-        per_device,
-        mesh=mesh,
+        body,
+        mesh=inner,
         in_specs=(
-            P("exp", "ctx", None),
-            P("exp", "ctx", None),
-            P("exp", "ctx", None),
-            P("exp", "ctx", None),
-            P("exp", "ctx", None),
-            P("exp", "ctx", None),
-            P(("ctx", "exp"), None),
+            token,
+            token,
+            token,
+            token,
+            token,
+            token,
+            P(both, None),
             P(),
-            P(("ctx", "exp"), None, None),
-            P(("ctx", "exp"), None, None),
-            P(("ctx", "exp"), None, None),
-            P("exp", "ctx", None),
-            P("exp", "ctx", None),
-        ),
-        out_specs=(P("exp", "ctx", None), P("exp", "ctx", None)),
+            expert,
+            expert,
+            expert,
+            token,
+            token,
+        ),
+        out_specs=(token, token),
         check_vma=False,
     )

time: 667 us -> 518 us (0.78)
  blocking collectives: 190 us -> 0 us
  starting transfers between devices: 21.9 us -> 139 us
  waiting for transfers between devices: 295 us -> 221 us
  matrix products: 52.3 us -> 95 us
  local copies, waits for them, and re-layouts: 54.9 us -> 22.6 us
  Pallas kernels: 0 us -> 10.7 us
  between operations: 14.8 us -> 4.39 us
  other arithmetic: 32.7 us -> 23.4 us
    all_to_all x1 -> x0, blocking collectives: 190 us -> none  [per_device(): lax.all_to_all(outgoing.reshape(experts_all, capacity, D), ('ctx', 'exp')...]
    ppermute x0 -> x42, waiting for transfers between devices: none -> 181 us  [the longest x15 117 us: downward(): lax.ppermute(value, 'z', [(z, z - 1) for z in range(first, last + 1)])]
    all_to_all x6 -> x9, waiting for transfers between devices: 211 us -> 39.5 us  [the longest x8 39.5 us: plane_exchange(): lax.all_to_all(blocks, PLANE, split_axis=0, concat_axis=0, tiled=True)]
    ppermute x0 -> x42, starting transfers between devices: none -> 90.5 us  [the longest x15 60.8 us: upward(): lax.ppermute(value, 'z', [(z, z + 1) for z in range(first, last + 1)])]
    all_gather x1 -> x0, waiting for transfers between devices: 42.6 us -> none  [per_device(): proj_rows = lax.all_gather(out_weight, 'exp', axis=0, tiled=True)]
    reduce_scatter x1 -> x0, waiting for transfers between devices: 40.7 us -> none  [per_device(): lax.psum_scatter(jnp.dot(attended, proj_rows, preferred_element_type=jnp....]
    dot_general x1 -> x4, matrix products: 8.81 us -> 45.4 us  [expert_ffn(): output = jnp.dot(product, down_matrix, preferred_element_type=jnp.float32)]
    all_to_all x6 -> x9, starting transfers between devices: 21.8 us -> 49 us  [the longest x8 45.4 us: plane_exchange(): lax.all_to_all(blocks, PLANE, split_axis=0, concat_axis=0, tiled=True)]
  transfers between devices with their start and end apart: 8 -> 51, of which waited for: 8 -> 23; matrix products, arithmetic and copies ran while one was open for 7% -> 25% of each run, Pallas kernels for 0% -> 2%
where the time goes in v1:
time: 518 us; the launch traced here: 516 us
  waiting for transfers between devices  221 us (43%)
  starting transfers between devices  139 us (27%)
  matrix products  95 us (18%)
  other arithmetic  23.4 us (5%)
  local copies, waits for them, and re-layouts  22.6 us (4%)
  Pallas kernels  10.7 us (2%)
    ppermute x15, waiting for transfers between devices, downward(): lax.ppermute(value, 'z', [(z, z - 1) for z in range(first, last + 1)])  117 us
    ppermute x12, waiting for transfers between devices, swap(): return lax.ppermute(value, axis, [(0, 1), (1, 0)])  62.8 us
    ppermute x15, starting transfers between devices, upward(): lax.ppermute(value, 'z', [(z, z + 1) for z in range(first, last + 1)])  60.8 us
    all_to_all x8, starting transfers between devices, plane_exchange(): lax.all_to_all(blocks, PLANE, split_axis=0, concat_axis=0, tiled=True)  45.4 us
    dot_general x4, matrix products, expert_ffn(): output = jnp.dot(product, down_matrix, preferred_element_type=jnp.float32)  45.4 us
    all_to_all x8, waiting for transfers between devices, plane_exchange(): lax.all_to_all(blocks, PLANE, split_axis=0, concat_axis=0, tiled=True)  39.5 us
    dot_general x4, matrix products, expert_ffn(): jnp.dot(flat_rows, gate_matrix, preferred_element_type=jnp.float32)  24 us
    ppermute x15, starting transfers between devices, downward(): lax.ppermute(value, 'z', [(z, z - 1) for z in range(first, last + 1)])  19.4 us
  transfers between devices with their start and end apart: 51, of which 23 were waited for; matrix products, arithmetic and copies ran while one was open for 25% of the time, Pallas kernels for 2%

profile of v1, /device:TPU:0, one launch (start us, length us, event | category | flops | bytes accessed | tf_op | source)
XLA Modules:
  0.0 516.4 jit_solution(8764778364824747416)
XLA Ops:
  0.7 2.7 fusion.153
  4.7 6.4 %collective-permute-start.13 = (bf16[128,2048]{1,0:T(8,128)(2,1)}, bf16[128,2048]{1,0:T(8,128)(2,1)}, u32[]{:S(2)}, u32[]{:S(2)}) collective-permute-start(bf16[128,2048]{1,0:T(8,128)(2,1)} %get-tuple-element.23), channel_id=1, source_target_pairs={{0,2},{2,4},{4,6},{1,3},{3,5},{5,7},{8,10},{10,12},{12,14},{9,11},... | collective-permute-start | bytes 1572872 | tf_op jit(solution)/shard_map/ppermute | solution.py:165
  14.3 4.5 collective-permute-start.25
  25.0 3.6 all-to-all-start
  32.6 2.8 collective-permute-done.26
  42.2 4.6 collective-permute-start.1
  51.2 6.7 %collective-permute-done = bf16[128,2048]{1,0:T(8,128)(2,1)S(1)} collective-permute-done((bf16[128,2048]{1,0:T(8,128)(2,1)}, bf16[128,2048]{1,0:T(8,128)(2,1)S(1)}, u32[]{:S(2)}, u32[]{:S(2)}) %collective-permute-start) | collective-permute-done | bytes 524320 | tf_op jit(solution)/shard_map/ppermute | solution.py:169
  61.2 5.7 %collective-permute-done.14 = bf16[128,2048]{1,0:T(8,128)(2,1)S(1)} collective-permute-done((bf16[128,2048]{1,0:T(8,128)(2,1)S(1)}, bf16[128,2048]{1,0:T(8,128)(2,1)S(1)}, u32[]{:S(2)}, u32[]{:S(2)}) %collective-permute-start.14) | collective-permute-done | bytes 524320 | tf_op jit(solution)/shard_map/ppermute | solution.py:169
  70.2 11.3 %collective-permute-done.2 = bf16[128,2048]{1,0:T(8,128)(2,1)S(1)} collective-permute-done((bf16[128,2048]{1,0:T(8,128)(2,1)S(1)}, bf16[128,2048]{1,0:T(8,128)(2,1)S(1)}, u32[]{:S(2)}, u32[]{:S(2)}) %collective-permute-start.2) | collective-permute-done | bytes 524320 | tf_op jit(solution)/shard_map/ppermute | solution.py:169
  85.8 10.7 %attention.1 = bf16[512,1024]{1,0:T(8,128)(2,1)S(1)} custom-call(bf16[4,128,1536]{2,1,0:T(8,128)(2,1)S(1)} %all-to-all-done.message_ref), custom_call_target="tpu_custom_call" | custom-call | flops 1744830464 | bytes 2621440 | tf_op jit(solution)/shard_map/attention/pallas_call | solution.py:248
  101.9 9.8 %collective-permute-done.4 = bf16[128,2048]{1,0:T(8,128)(2,1)S(1)} collective-permute-done((bf16[128,2048]{1,0:T(8,128)(2,1)S(1)}, bf16[128,2048]{1,0:T(8,128)(2,1)S(1)}, u32[]{:S(2)}, u32[]{:S(2)}) %collective-permute-start.4) | collective-permute-done | bytes 524320 | tf_op jit(solution)/shard_map/ppermute | solution.py:169
  120.1 17.7 %collective-permute-done.20 = bf16[128,2048]{1,0:T(8,128)(2,1)S(1)} collective-permute-done((bf16[128,2048]{1,0:T(8,128)(2,1)S(1)}, bf16[128,2048]{1,0:T(8,128)(2,1)S(1)}, u32[]{:S(2)}, u32[]{:S(2)}) %collective-permute-start.20) | collective-permute-done | bytes 524320 | tf_op jit(solution)/shard_map/ppermute | solution.py:161
  140.5 8.6 %collective-permute-done.8 = bf16[128,2048]{1,0:T(8,128)(2,1)S(1)} collective-permute-done((bf16[128,2048]{1,0:T(8,128)(2,1)S(1)}, bf16[128,2048]{1,0:T(8,128)(2,1)S(1)}, u32[]{:S(2)}, u32[]{:S(2)}) %collective-permute-start.8) | collective-permute-done | bytes 524320 | tf_op jit(solution)/shard_map/ppermute | solution.py:161
  149.1 11.2 %collective-permute-done.21 = bf16[128,2048]{1,0:T(8,128)(2,1)S(1)} collective-permute-done((bf16[128,2048]{1,0:T(8,128)(2,1)S(1)}, bf16[128,2048]{1,0:T(8,128)(2,1)S(1)}, u32[]{:S(2)}, u32[]{:S(2)}) %collective-permute-start.21) | collective-permute-done | bytes 524320 | tf_op jit(solution)/shard_map/ppermute | solution.py:161
  161.1 4.5 fusion.158
  174.1 11.6 %collective-permute-done.23 = bf16[128,2048]{1,0:T(8,128)(2,1)S(1)} collective-permute-done((bf16[128,2048]{1,0:T(8,128)(2,1)S(1)}, bf16[128,2048]{1,0:T(8,128)(2,1)S(1)}, u32[]{:S(2)}, u32[]{:S(2)}) %collective-permute-start.23) | collective-permute-done | bytes 524320 | tf_op jit(solution)/shard_map/ppermute | solution.py:161
  185.9 10.7 %collective-permute-done.11 = bf16[128,2048]{1,0:T(8,128)(2,1)S(1)} collective-permute-done((bf16[128,2048]{1,0:T(8,128)(2,1)S(1)}, bf16[128,2048]{1,0:T(8,128)(2,1)S(1)}, u32[]{:S(2)}, u32[]{:S(2)}) %collective-permute-start.11) | collective-permute-done | bytes 524320 | tf_op jit(solution)/shard_map/ppermute | solution.py:161
  200.4 4.4 all-to-all-start.1
  206.4 5.6 %collective-permute-start.32 = (bf16[128,4096]{1,0:T(8,128)(2,1)S(1)}, bf16[128,4096]{1,0:T(8,128)(2,1)}, u32[]{:S(2)}, u32[]{:S(2)}) collective-permute-start(bf16[128,4096]{1,0:T(8,128)(2,1)S(1)} %fusion.44), channel_id=1, source_target_pairs={{0,2},{2,4},{4,6},{1,3},{3,5},{5,7},{8,10},{10,12},{12,14},{9,11},... | collective-permute-start | bytes 3145736 | tf_op jit(solution)/shard_map/ppermute | solution.py:165
  212.0 20.5 %collective-permute-done.30 = bf16[128,4096]{1,0:T(8,128)(2,1)} collective-permute-done((bf16[128,4096]{1,0:T(8,128)(2,1)S(1)}, bf16[128,4096]{1,0:T(8,128)(2,1)}, u32[]{:S(2)}, u32[]{:S(2)}) %collective-permute-start.30) | collective-permute-done | bytes 1048608 | tf_op jit(solution)/shard_map/ppermute | solution.py:169
  234.6 3.6 convolution_convert_fusion.1
  238.2 4.4 all-to-all-start.5
  242.5 16.7 %collective-permute-done.31 = bf16[128,4096]{1,0:T(8,128)(2,1)S(1)} collective-permute-done((bf16[128,4096]{1,0:T(8,128)(2,1)}, bf16[128,4096]{1,0:T(8,128)(2,1)S(1)}, u32[]{:S(2)}, u32[]{:S(2)}) %collective-permute-start.31) | collective-permute-done | bytes 1048608 | tf_op jit(solution)/shard_map/ppermute | solution.py:169
  261.3 23.7 %collective-permute-done.34 = bf16[128,4096]{1,0:T(8,128)(2,1)S(1)} collective-permute-done((bf16[128,4096]{1,0:T(8,128)(2,1)S(1)}, bf16[128,4096]{1,0:T(8,128)(2,1)S(1)}, u32[]{:S(2)}, u32[]{:S(2)}) %collective-permute-start.34) | collective-permute-done | bytes 1048608 | tf_op jit(solution)/shard_map/ppermute | solution.py:169
  287.1 4.4 all-to-all-start.7
  294.6 23.0 %all-to-all-done.7 = bf16[8,32,4096]{2,1,0:T(8,128)(2,1)} async-done(((bf16[8,32,4096]{2,1,0:T(8,128)(2,1)}), bf16[8,32,4096]{2,1,0:T(8,128)(2,1)}, u32[]{:S(2)}, u32[]{:S(2)}) %all-to-all-start.7) | async-done | bytes 2097184 | tf_op jit(solution)/shard_map/all_to_all | solution.py:297
  317.6 16.4 %all-to-all-start.3 = ((bf16[8,32,4096]{2,1,0:T(8,128)(2,1)}), bf16[8,32,4096]{2,1,0:T(8,128)(2,1)S(1)}, u32[]{:S(2)}, u32[]{:S(2)}) async-start(bf16[8,32,4096]{2,1,0:T(8,128)(2,1)} %bitcast.50), calls=%async_computation.3 | async-start | bytes 4194304 | tf_op jit(solution)/shard_map/all_to_all | solution.py:297
  334.1 6.1 %fusion.22 = f32[256,768]{1,0:T(8,128)} fusion(bf16[256,4096]{1,0:T(8,128)(2,1)} %bitcast.42, bf16[1,4096,768]{2,1,0:T(8,128)(2,1)} %param.22), kind=kOutput, calls=%fused_computation.22 | convolution fusion | flops 1610612736 | bytes 9175040 | tf_op jit(solution)/shard_map/dot_general | solution.py:31
  340.2 6.1 %fusion.16 = f32[256,768]{1,0:T(8,128)} fusion(bf16[256,4096]{1,0:T(8,128)(2,1)} %bitcast.63, bf16[1,4096,768]{2,1,0:T(8,128)(2,1)} %param.22), kind=kOutput, calls=%fused_computation.16 | convolution fusion | flops 1610612736 | bytes 9175040 | tf_op jit(solution)/shard_map/dot_general | solution.py:31
  346.3 11.4 %fusion.33 = bf16[256,4096]{1,0:T(8,128)(2,1)} fusion(bf16[1,768,4096]{2,1,0:T(8,128)(2,1)} %param.24, bf16[256,4096]{1,0:T(8,128)(2,1)} %bitcast.63, bf16[1,4096,768]{2,1,0:T(8,128)(2,1)} %param.23, f32[256,768]{1,0:T(8,128)} %fusion.16), kind=kOutput, calls=%fused_computation.31 | convolution fusion | flops 3223453696 | bytes 17563648 | tf_op jit(solution)/shard_map/dot_general | solution.py:34
  357.6 2.5 all-to-all-done.3
  361.5 3.6 all-to-all-start.8
  365.1 6.3 %fusion.18 = f32[256,768]{1,0:T(8,128)} fusion(bf16[256,4096]{1,0:T(8,128)(2,1)} %bitcast.57, bf16[1,4096,768]{2,1,0:T(8,128)(2,1)} %param.22), kind=kOutput, calls=%fused_computation.18 | convolution fusion | flops 1610612736 | bytes 9175040 | tf_op jit(solution)/shard_map/dot_general | solution.py:31
  371.4 5.5 %fusion.20 = f32[256,768]{1,0:T(8,128)} fusion(bf16[256,4096]{1,0:T(8,128)(2,1)S(1)} %bitcast.220, bf16[1,4096,768]{2,1,0:T(8,128)(2,1)} %param.22), kind=kOutput, calls=%fused_computation.20 | convolution fusion | flops 1610612736 | bytes 9175040 | tf_op jit(solution)/shard_map/dot_general | solution.py:31
  376.9 11.4 %fusion.27 = bf16[256,4096]{1,0:T(8,128)(2,1)} fusion(bf16[1,768,4096]{2,1,0:T(8,128)(2,1)} %param.24, bf16[256,4096]{1,0:T(8,128)(2,1)} %bitcast.219, bf16[1,4096,768]{2,1,0:T(8,128)(2,1)} %param.23, f32[256,768]{1,0:T(8,128)} %fusion.20), kind=kOutput, calls=%fused_computation.29 | convolution fusion | flops 3223453696 | bytes 17563648 | tf_op jit(solution)/shard_map/dot_general | solution.py:34
  388.3 2.9 all-to-all-done.8
  392.5 3.6 all-to-all-start.4
  403.2 11.4 %fusion.30 = bf16[256,4096]{1,0:T(8,128)(2,1)} fusion(bf16[1,768,4096]{2,1,0:T(8,128)(2,1)} %param.24, bf16[256,4096]{1,0:T(8,128)(2,1)} %bitcast.57, bf16[1,4096,768]{2,1,0:T(8,128)(2,1)} %param.23, f32[256,768]{1,0:T(8,128)} %fusion.18), kind=kOutput, calls=%fused_computation.30 | convolution fusion | flops 3223453696 | bytes 17563648 | tf_op jit(solution)/shard_map/dot_general | solution.py:34
  414.6 7.6 %all-to-all-done.4 = bf16[8,32,4096]{2,1,0:T(8,128)(2,1)S(1)} async-done(((bf16[8,32,4096]{2,1,0:T(8,128)(2,1)}), bf16[8,32,4096]{2,1,0:T(8,128)(2,1)S(1)}, u32[]{:S(2)}, u32[]{:S(2)}) %all-to-all-start.4) | async-done | bytes 2097184 | tf_op jit(solution)/shard_map/all_to_all | solution.py:297
  422.2 4.4 all-to-all-start.6
  429.2 3.1 add_convert_fusion.3
  432.3 2.5 collective-permute-start.37
  438.0 11.3 %fusion.24 = bf16[256,4096]{1,0:T(8,128)(2,1)} fusion(bf16[1,768,4096]{2,1,0:T(8,128)(2,1)} %param.24, bf16[256,4096]{1,0:T(8,128)(2,1)} %bitcast.42, bf16[1,4096,768]{2,1,0:T(8,128)(2,1)} %param.23, f32[256,768]{1,0:T(8,128)} %fusion.22), kind=kOutput, calls=%fused_computation.28 | convolution fusion | flops 3223453696 | bytes 17563648 | tf_op jit(solution)/shard_map/dot_general | solution.py:34
  449.3 3.4 all-to-all-done.6
  452.7 4.4 all-to-all-start.2
  459.4 3.7 add_convert_fusion.2
  464.4 28.0 %collective-permute-start.38 = (bf16[128,4096]{1,0:T(8,128)(2,1)}, bf16[128,4096]{1,0:T(8,128)(2,1)S(1)}, u32[]{:S(2)}, u32[]{:S(2)}) collective-permute-start(bf16[128,4096]{1,0:T(8,128)(2,1)} %get-tuple-element.18), channel_id=1, source_target_pairs={{0,2},{2,4},{4,6},{1,3},{3,5},{5,7},{8,10},{10,12},{12,14},{9,11},... | collective-permute-start | bytes 3145736 | tf_op jit(solution)/shard_map/ppermute | solution.py:165
  494.9 18.4 %collective-permute-done.41 = bf16[128,4096]{1,0:T(8,128)(2,1)S(1)} collective-permute-done((bf16[128,4096]{1,0:T(8,128)(2,1)}, bf16[128,4096]{1,0:T(8,128)(2,1)S(1)}, u32[]{:S(2)}, u32[]{:S(2)}) %collective-permute-start.41) | collective-permute-done | bytes 1048608 | tf_op jit(solution)/shard_map/ppermute | solution.py:169
  (189 shorter events, 98.8 us)
Async XLA Ops:
  3.4 43.6 %collective-permute-start.12 = (bf16[128,2048]{1,0:T(8,128)(2,1)}, bf16[128,2048]{1,0:T(8,128)(2,1)S(1)}, u32[]{:S(2)}, u32[]{:S(2)}) collective-permute-start(bf16[128,2048]{1,0:T(8,128)(2,1)} %get-tuple-element.23), channel_id=1, source_target_pairs={{2,0},{4,2},{6,4},{3,1},{5,3},{7,5},{10,8},{12,10},{14,12},{11,9},... | collective-permute-start | bytes 1572872 | tf_op jit(solution)/shard_map/ppermute | solution.py:169
  4.7 43.6 %collective-permute-start.13 = (bf16[128,2048]{1,0:T(8,128)(2,1)}, bf16[128,2048]{1,0:T(8,128)(2,1)}, u32[]{:S(2)}, u32[]{:S(2)}) collective-permute-start(bf16[128,2048]{1,0:T(8,128)(2,1)} %get-tuple-element.23), channel_id=1, source_target_pairs={{0,2},{2,4},{4,6},{1,3},{3,5},{5,7},{8,10},{10,12},{12,14},{9,11},... | collective-permute-start | bytes 1572872 | tf_op jit(solution)/shard_map/ppermute | solution.py:165
  11.0 103.1 %collective-permute-start.18 = (bf16[128,2048]{1,0:T(8,128)(2,1)}, bf16[128,2048]{1,0:T(8,128)(2,1)}, u32[]{:S(2)}, u32[]{:S(2)}) collective-permute-start(bf16[128,2048]{1,0:T(8,128)(2,1)} %get-tuple-element.23), channel_id=1, source_target_pairs={{0,1},{1,0},{2,3},{3,2},{4,5},{5,4},{6,7},{7,6},{8,9},{9,8},{10,11... | collective-permute-start | bytes 1572872 | tf_op jit(solution)/shard_map/ppermute | solution.py:161
  13.0 17.0 %collective-permute-start.24 = (s32[128,8]{0,1:T(8,128)S(1)}, s32[128,8]{0,1:T(8,128)S(1)}, u32[]{:S(2)}, u32[]{:S(2)}) collective-permute-start(s32[128,8]{0,1:T(8,128)S(1)} %get-tuple-element.38), channel_id=1, source_target_pairs={{2,0},{4,2},{6,4},{3,1},{5,3},{7,5},{10,8},{12,10},{14,12},{11,9},... | collective-permute-start | bytes 12296 | tf_op jit(solution)/shard_map/ppermute | solution.py:169
  14.3 17.0 %collective-permute-start.25 = (s32[128,8]{0,1:T(8,128)S(1)}, s32[128,8]{0,1:T(8,128)S(1)}, u32[]{:S(2)}, u32[]{:S(2)}) collective-permute-start(s32[128,8]{0,1:T(8,128)S(1)} %get-tuple-element.38), channel_id=1, source_target_pairs={{0,2},{2,4},{4,6},{1,3},{3,5},{5,7},{8,10},{10,12},{12,14},{9,11},... | collective-permute-start | bytes 12296 | tf_op jit(solution)/shard_map/ppermute | solution.py:165
  25.0 60.7 %all-to-all-start = ((bf16[4,128,1536]{2,1,0:T(8,128)(2,1)}), bf16[4,128,1536]{2,1,0:T(8,128)(2,1)S(1)}, u32[]{:S(2)}, u32[]{:S(2)}) async-start(bf16[4,128,1536]{2,1,0:T(8,128)(2,1)} %bitcast_dynamic-update-slice_fusion.1), calls=%async_computation | async-start | bytes 3145728 | tf_op jit(solution)/shard_map/all_to_all | solution.py:326
  30.0 5.5 %collective-permute-start.26 = (s32[128,8]{0,1:T(8,128)S(1)}, s32[128,8]{0,1:T(8,128)S(1)}, u32[]{:S(2)}, u32[]{:S(2)}) collective-permute-start(s32[128,8]{0,1:T(8,128)S(1)} %collective-permute-done.24), channel_id=1, source_target_pairs={{2,0},{4,2},{3,1},{5,3},{10,8},{12,10},{11,9},{13,11},{18,16},{20,... | collective-permute-start | bytes 12296 | tf_op jit(solution)/shard_map/ppermute | solution.py:169
  31.3 5.5 %collective-permute-start.27 = (s32[128,8]{0,1:T(8,128)S(1)}, s32[128,8]{0,1:T(8,128)S(1)}, u32[]{:S(2)}, u32[]{:S(2)}) collective-permute-start(s32[128,8]{0,1:T(8,128)S(1)} %collective-permute-done.25), channel_id=1, source_target_pairs={{2,4},{4,6},{3,5},{5,7},{10,12},{12,14},{11,13},{13,15},{18,20},{2... | collective-permute-start | bytes 12296 | tf_op jit(solution)/shard_map/ppermute | solution.py:165
  35.5 5.5 %collective-permute-start.28 = (s32[128,8]{0,1:T(8,128)S(1)}, s32[128,8]{0,1:T(8,128)S(1)}, u32[]{:S(2)}, u32[]{:S(2)}) collective-permute-start(s32[128,8]{0,1:T(8,128)S(1)} %collective-permute-done.26), channel_id=1, source_target_pairs={{2,0},{3,1},{10,8},{11,9},{18,16},{19,17},{26,24},{27,25}} | collective-permute-start | bytes 12296 | tf_op jit(solution)/shard_map/ppermute | solution.py:169
  40.9 17.0 %collective-permute-start = (bf16[128,2048]{1,0:T(8,128)(2,1)}, bf16[128,2048]{1,0:T(8,128)(2,1)S(1)}, u32[]{:S(2)}, u32[]{:S(2)}) collective-permute-start(bf16[128,2048]{1,0:T(8,128)(2,1)} %get-tuple-element.20), channel_id=1, source_target_pairs={{2,0},{4,2},{6,4},{3,1},{5,3},{7,5},{10,8},{12,10},{14,12},{11,9},... | collective-permute-start | bytes 1572872 | tf_op jit(solution)/shard_map/ppermute | solution.py:169
  42.2 15.8 %collective-permute-start.1 = (bf16[128,2048]{1,0:T(8,128)(2,1)}, bf16[128,2048]{1,0:T(8,128)(2,1)S(1)}, u32[]{:S(2)}, u32[]{:S(2)}) collective-permute-start(bf16[128,2048]{1,0:T(8,128)(2,1)} %get-tuple-element.20), channel_id=1, source_target_pairs={{0,2},{2,4},{4,6},{1,3},{3,5},{5,7},{8,10},{10,12},{12,14},{9,11},... | collective-permute-start | bytes 1572872 | tf_op jit(solution)/shard_map/ppermute | solution.py:165
  47.0 19.9 %collective-permute-start.14 = (bf16[128,2048]{1,0:T(8,128)(2,1)S(1)}, bf16[128,2048]{1,0:T(8,128)(2,1)S(1)}, u32[]{:S(2)}, u32[]{:S(2)}) collective-permute-start(bf16[128,2048]{1,0:T(8,128)(2,1)S(1)} %collective-permute-done.12), channel_id=1, source_target_pairs={{2,0},{4,2},{3,1},{5,3},{10,8},{12,10},{11,9},{13,11},{18,16},{20,... | collective-permute-start | bytes 1572872 | tf_op jit(solution)/shard_map/ppermute | solution.py:169
  48.3 19.9 %collective-permute-start.15 = (bf16[128,2048]{1,0:T(8,128)(2,1)}, bf16[128,2048]{1,0:T(8,128)(2,1)S(1)}, u32[]{:S(2)}, u32[]{:S(2)}) collective-permute-start(bf16[128,2048]{1,0:T(8,128)(2,1)} %collective-permute-done.13), channel_id=1, source_target_pairs={{2,4},{4,6},{3,5},{5,7},{10,12},{12,14},{11,13},{13,15},{18,20},{2... | collective-permute-start | bytes 1572872 | tf_op jit(solution)/shard_map/ppermute | solution.py:165
  57.9 81.4 %collective-permute-start.6 = (bf16[128,2048]{1,0:T(8,128)(2,1)}, bf16[128,2048]{1,0:T(8,128)(2,1)}, u32[]{:S(2)}, u32[]{:S(2)}) collective-permute-start(bf16[128,2048]{1,0:T(8,128)(2,1)} %get-tuple-element.20), channel_id=1, source_target_pairs={{0,1},{1,0},{2,3},{3,2},{4,5},{5,4},{6,7},{7,6},{8,9},{9,8},{10,11... | collective-permute-start | bytes 1572872 | tf_op jit(solution)/shard_map/ppermute | solution.py:161
  58.0 58.7 %collective-permute-start.19 = (bf16[128,2048]{1,0:T(8,128)(2,1)}, bf16[128,2048]{1,0:T(8,128)(2,1)}, u32[]{:S(2)}, u32[]{:S(2)}) collective-permute-start(bf16[128,2048]{1,0:T(8,128)(2,1)} %get-tuple-element.17), channel_id=1, source_target_pairs={{0,1},{1,0},{2,3},{3,2},{4,5},{5,4},{6,7},{7,6},{8,9},{9,8},{10,11... | collective-permute-start | bytes 1572872 | tf_op jit(solution)/shard_map/ppermute | solution.py:161
  66.8 14.7 %collective-permute-start.2 = (bf16[128,2048]{1,0:T(8,128)(2,1)S(1)}, bf16[128,2048]{1,0:T(8,128)(2,1)S(1)}, u32[]{:S(2)}, u32[]{:S(2)}) collective-permute-start(bf16[128,2048]{1,0:T(8,128)(2,1)S(1)} %collective-permute-done), channel_id=1, source_target_pairs={{2,0},{4,2},{3,1},{5,3},{10,8},{12,10},{11,9},{13,11},{18,16},{20,... | collective-permute-start | bytes 1572872 | tf_op jit(solution)/shard_map/ppermute | solution.py:169
  68.1 14.7 %collective-permute-start.3 = (bf16[128,2048]{1,0:T(8,128)(2,1)S(1)}, bf16[128,2048]{1,0:T(8,128)(2,1)S(1)}, u32[]{:S(2)}, u32[]{:S(2)}) collective-permute-start(bf16[128,2048]{1,0:T(8,128)(2,1)S(1)} %collective-permute-done.1), channel_id=1, source_target_pairs={{2,4},{4,6},{3,5},{5,7},{10,12},{12,14},{11,13},{13,15},{18,20},{2... | collective-permute-start | bytes 1572872 | tf_op jit(solution)/shard_map/ppermute | solution.py:165
  81.6 15.4 %collective-permute-start.16 = (bf16[128,2048]{1,0:T(8,128)(2,1)S(1)}, bf16[128,2048]{1,0:T(8,128)(2,1)}, u32[]{:S(2)}, u32[]{:S(2)}) collective-permute-start(bf16[128,2048]{1,0:T(8,128)(2,1)S(1)} %collective-permute-done.14), channel_id=1, source_target_pairs={{2,0},{3,1},{10,8},{11,9},{18,16},{19,17},{26,24},{27,25}} | collective-permute-start | bytes 1572872 | tf_op jit(solution)/shard_map/ppermute | solution.py:169
  82.9 15.5 %collective-permute-start.17 = (bf16[128,2048]{1,0:T(8,128)(2,1)S(1)}, bf16[128,2048]{1,0:T(8,128)(2,1)}, u32[]{:S(2)}, u32[]{:S(2)}) collective-permute-start(bf16[128,2048]{1,0:T(8,128)(2,1)S(1)} %collective-permute-done.15), channel_id=1, source_target_pairs={{4,6},{5,7},{12,14},{13,15},{20,22},{21,23},{28,30},{29,31}} | collective-permute-start | bytes 1572872 | tf_op jit(solution)/shard_map/ppermute | solution.py:165
  97.0 14.7 %collective-permute-start.4 = (bf16[128,2048]{1,0:T(8,128)(2,1)S(1)}, bf16[128,2048]{1,0:T(8,128)(2,1)S(1)}, u32[]{:S(2)}, u32[]{:S(2)}) collective-permute-start(bf16[128,2048]{1,0:T(8,128)(2,1)S(1)} %collective-permute-done.2), channel_id=1, source_target_pairs={{2,0},{3,1},{10,8},{11,9},{18,16},{19,17},{26,24},{27,25}} | collective-permute-start | bytes 1572872 | tf_op jit(solution)/shard_map/ppermute | solution.py:169
  98.4 13.9 %collective-permute-start.5 = (bf16[128,2048]{1,0:T(8,128)(2,1)S(1)}, bf16[128,2048]{1,0:T(8,128)(2,1)S(1)}, u32[]{:S(2)}, u32[]{:S(2)}) collective-permute-start(bf16[128,2048]{1,0:T(8,128)(2,1)S(1)} %copy-done.6), channel_id=1, source_target_pairs={{4,6},{5,7},{12,14},{13,15},{20,22},{21,23},{28,30},{29,31}} | collective-permute-start | bytes 1572872 | tf_op jit(solution)/shard_map/ppermute | solution.py:165
  111.7 28.7 %collective-permute-start.7 = (bf16[128,2048]{1,0:T(8,128)(2,1)S(1)}, bf16[128,2048]{1,0:T(8,128)(2,1)S(1)}, u32[]{:S(2)}, u32[]{:S(2)}) collective-permute-start(bf16[128,2048]{1,0:T(8,128)(2,1)S(1)} %copy-done.13), channel_id=1, source_target_pairs={{0,1},{1,0},{2,3},{3,2},{4,5},{5,4},{6,7},{7,6},{8,9},{9,8},{10,11... | collective-permute-start | bytes 1572872 | tf_op jit(solution)/shard_map/ppermute | solution.py:161
  112.3 25.5 %collective-permute-start.20 = (bf16[128,2048]{1,0:T(8,128)(2,1)S(1)}, bf16[128,2048]{1,0:T(8,128)(2,1)S(1)}, u32[]{:S(2)}, u32[]{:S(2)}) collective-permute-start(bf16[128,2048]{1,0:T(8,128)(2,1)S(1)} %copy-done.12), channel_id=1, source_target_pairs={{0,1},{1,0},{2,3},{3,2},{4,5},{5,4},{6,7},{7,6},{8,9},{9,8},{10,11... | collective-permute-start | bytes 1572872 | tf_op jit(solution)/shard_map/ppermute | solution.py:161
  114.1 34.9 %collective-permute-start.8 = (bf16[128,2048]{1,0:T(8,128)(2,1)S(1)}, bf16[128,2048]{1,0:T(8,128)(2,1)S(1)}, u32[]{:S(2)}, u32[]{:S(2)}) collective-permute-start(bf16[128,2048]{1,0:T(8,128)(2,1)S(1)} %copy-done.11), channel_id=1, source_target_pairs={{0,1},{1,0},{2,3},{3,2},{4,5},{5,4},{6,7},{7,6},{8,9},{9,8},{10,11... | collective-permute-start | bytes 1572872 | tf_op jit(solution)/shard_map/ppermute | solution.py:161
  116.7 43.6 %collective-permute-start.21 = (bf16[128,2048]{1,0:T(8,128)(2,1)S(1)}, bf16[128,2048]{1,0:T(8,128)(2,1)S(1)}, u32[]{:S(2)}, u32[]{:S(2)}) collective-permute-start(bf16[128,2048]{1,0:T(8,128)(2,1)S(1)} %get-tuple-element.13), channel_id=1, source_target_pairs={{0,1},{1,0},{2,3},{3,2},{4,5},{5,4},{6,7},{7,6},{8,9},{9,8},{10,11... | collective-permute-start | bytes 1572872 | tf_op jit(solution)/shard_map/ppermute | solution.py:161
  137.8 29.8 %collective-permute-start.9 = (bf16[128,2048]{1,0:T(8,128)(2,1)S(1)}, bf16[128,2048]{1,0:T(8,128)(2,1)S(1)}, u32[]{:S(2)}, u32[]{:S(2)}) collective-permute-start(bf16[128,2048]{1,0:T(8,128)(2,1)S(1)} %get-tuple-element.7), channel_id=1, source_target_pairs={{0,1},{1,0},{2,3},{3,2},{4,5},{5,4},{6,7},{7,6},{8,9},{9,8},{10,11... | collective-permute-start | bytes 1572872 | tf_op jit(solution)/shard_map/ppermute | solution.py:161
  171.0 14.8 %collective-permute-start.23 = (bf16[128,2048]{1,0:T(8,128)(2,1)S(1)}, bf16[128,2048]{1,0:T(8,128)(2,1)S(1)}, u32[]{:S(2)}, u32[]{:S(2)}) collective-permute-start(bf16[128,2048]{1,0:T(8,128)(2,1)S(1)} %fusion.104), channel_id=1, source_target_pairs={{0,16},{16,0},{1,17},{17,1},{2,18},{18,2},{3,19},{19,3},{4,20},{20... | collective-permute-start | bytes 1572872 | tf_op jit(solution)/shard_map/ppermute | solution.py:161
  173.3 23.3 %collective-permute-start.11 = (bf16[128,2048]{1,0:T(8,128)(2,1)S(1)}, bf16[128,2048]{1,0:T(8,128)(2,1)S(1)}, u32[]{:S(2)}, u32[]{:S(2)}) collective-permute-start(bf16[128,2048]{1,0:T(8,128)(2,1)S(1)} %fusion.103), channel_id=1, source_target_pairs={{0,16},{16,0},{1,17},{17,1},{2,18},{18,2},{3,19},{19,3},{4,20},{20... | collective-permute-start | bytes 1572872 | tf_op jit(solution)/shard_map/ppermute | solution.py:161
  200.4 37.8 %all-to-all-start.1 = ((bf16[8,32,4096]{2,1,0:T(8,128)(2,1)}), bf16[8,32,4096]{2,1,0:T(8,128)(2,1)}, u32[]{:S(2)}, u32[]{:S(2)}) async-start(bf16[8,32,4096]{2,1,0:T(8,128)(2,1)} %bitcast.41), calls=%async_computation.1 | async-start | bytes 4194304 | tf_op jit(solution)/shard_map/all_to_all | solution.py:297
  205.1 27.4 %collective-permute-start.30 = (bf16[128,4096]{1,0:T(8,128)(2,1)S(1)}, bf16[128,4096]{1,0:T(8,128)(2,1)}, u32[]{:S(2)}, u32[]{:S(2)}) collective-permute-start(bf16[128,4096]{1,0:T(8,128)(2,1)S(1)} %fusion.44), channel_id=1, source_target_pairs={{2,0},{4,2},{6,4},{3,1},{5,3},{7,5},{10,8},{12,10},{14,12},{11,9},... | collective-permute-start | bytes 3145736 | tf_op jit(solution)/shard_map/ppermute | solution.py:169
  206.4 27.4 %collective-permute-start.32 = (bf16[128,4096]{1,0:T(8,128)(2,1)S(1)}, bf16[128,4096]{1,0:T(8,128)(2,1)}, u32[]{:S(2)}, u32[]{:S(2)}) collective-permute-start(bf16[128,4096]{1,0:T(8,128)(2,1)S(1)} %fusion.44), channel_id=1, source_target_pairs={{0,2},{2,4},{4,6},{1,3},{3,5},{5,7},{8,10},{10,12},{12,14},{9,11},... | collective-permute-start | bytes 3145736 | tf_op jit(solution)/shard_map/ppermute | solution.py:165
  232.6 26.7 %collective-permute-start.31 = (bf16[128,4096]{1,0:T(8,128)(2,1)}, bf16[128,4096]{1,0:T(8,128)(2,1)S(1)}, u32[]{:S(2)}, u32[]{:S(2)}) collective-permute-start(bf16[128,4096]{1,0:T(8,128)(2,1)} %collective-permute-done.30), channel_id=1, source_target_pairs={{2,0},{4,2},{3,1},{5,3},{10,8},{12,10},{11,9},{13,11},{18,16},{20,... | collective-permute-start | bytes 3145736 | tf_op jit(solution)/shard_map/ppermute | solution.py:169
  233.9 26.7 %collective-permute-start.33 = (bf16[128,4096]{1,0:T(8,128)(2,1)}, bf16[128,4096]{1,0:T(8,128)(2,1)S(1)}, u32[]{:S(2)}, u32[]{:S(2)}) collective-permute-start(bf16[128,4096]{1,0:T(8,128)(2,1)} %collective-permute-done.32), channel_id=1, source_target_pairs={{2,4},{4,6},{3,5},{5,7},{10,12},{12,14},{11,13},{13,15},{18,20},{2... | collective-permute-start | bytes 3145736 | tf_op jit(solution)/shard_map/ppermute | solution.py:165
  238.2 48.9 %all-to-all-start.5 = ((bf16[8,32,4096]{2,1,0:T(8,128)(2,1)}), bf16[8,32,4096]{2,1,0:T(8,128)(2,1)}, u32[]{:S(2)}, u32[]{:S(2)}) async-start(bf16[8,32,4096]{2,1,0:T(8,128)(2,1)} %bitcast.217), calls=%async_computation.5 | async-start | bytes 4194304 | tf_op jit(solution)/shard_map/all_to_all | solution.py:297
  259.3 25.7 %collective-permute-start.34 = (bf16[128,4096]{1,0:T(8,128)(2,1)S(1)}, bf16[128,4096]{1,0:T(8,128)(2,1)S(1)}, u32[]{:S(2)}, u32[]{:S(2)}) collective-permute-start(bf16[128,4096]{1,0:T(8,128)(2,1)S(1)} %collective-permute-done.31), channel_id=1, source_target_pairs={{2,0},{3,1},{10,8},{11,9},{18,16},{19,17},{26,24},{27,25}} | collective-permute-start | bytes 3145736 | tf_op jit(solution)/shard_map/ppermute | solution.py:169
  260.6 24.4 %collective-permute-start.35 = (bf16[128,4096]{1,0:T(8,128)(2,1)S(1)}, bf16[128,4096]{1,0:T(8,128)(2,1)S(1)}, u32[]{:S(2)}, u32[]{:S(2)}) collective-permute-start(bf16[128,4096]{1,0:T(8,128)(2,1)S(1)} %collective-permute-done.33), channel_id=1, source_target_pairs={{4,6},{5,7},{12,14},{13,15},{20,22},{21,23},{28,30},{29,31}} | collective-permute-start | bytes 3145736 | tf_op jit(solution)/shard_map/ppermute | solution.py:165
  287.1 30.5 %all-to-all-start.7 = ((bf16[8,32,4096]{2,1,0:T(8,128)(2,1)}), bf16[8,32,4096]{2,1,0:T(8,128)(2,1)}, u32[]{:S(2)}, u32[]{:S(2)}) async-start(bf16[8,32,4096]{2,1,0:T(8,128)(2,1)} %bitcast.62), calls=%async_computation.7 | async-start | bytes 4194304 | tf_op jit(solution)/shard_map/all_to_all | solution.py:297
  317.6 42.5 %all-to-all-start.3 = ((bf16[8,32,4096]{2,1,0:T(8,128)(2,1)}), bf16[8,32,4096]{2,1,0:T(8,128)(2,1)S(1)}, u32[]{:S(2)}, u32[]{:S(2)}) async-start(bf16[8,32,4096]{2,1,0:T(8,128)(2,1)} %bitcast.50), calls=%async_computation.3 | async-start | bytes 4194304 | tf_op jit(solution)/shard_map/all_to_all | solution.py:297
  361.5 29.7 %all-to-all-start.8 = ((bf16[8,32,4096]{2,1,0:T(8,128)(2,1)}), bf16[8,32,4096]{2,1,0:T(8,128)(2,1)S(1)}, u32[]{:S(2)}, u32[]{:S(2)}) async-start(bf16[8,32,4096]{2,1,0:T(8,128)(2,1)} %bitcast.221), calls=%async_computation.8 | async-start | bytes 4194304 | tf_op jit(solution)/shard_map/all_to_all | solution.py:297
  392.5 29.7 %all-to-all-start.4 = ((bf16[8,32,4096]{2,1,0:T(8,128)(2,1)}), bf16[8,32,4096]{2,1,0:T(8,128)(2,1)S(1)}, u32[]{:S(2)}, u32[]{:S(2)}) async-start(bf16[8,32,4096]{2,1,0:T(8,128)(2,1)} %bitcast.218), calls=%async_computation.4 | async-start | bytes 4194304 | tf_op jit(solution)/shard_map/all_to_all | solution.py:297
  400.8 28.4 %collective-permute-start.36 = (bf16[128,4096]{1,0:T(8,128)(2,1)}, bf16[128,4096]{1,0:T(8,128)(2,1)}, u32[]{:S(2)}, u32[]{:S(2)}) collective-permute-start(bf16[128,4096]{1,0:T(8,128)(2,1)} %fusion.149), channel_id=1, source_target_pairs={{0,2},{1,3},{8,10},{9,11},{16,18},{17,19},{24,26},{25,27}} | collective-permute-start | bytes 3145736 | tf_op jit(solution)/shard_map/ppermute | solution.py:165
  422.2 30.5 %all-to-all-start.6 = ((bf16[8,32,4096]{2,1,0:T(8,128)(2,1)}), bf16[8,32,4096]{2,1,0:T(8,128)(2,1)}, u32[]{:S(2)}, u32[]{:S(2)}) async-start(bf16[8,32,4096]{2,1,0:T(8,128)(2,1)} %bitcast.215), calls=%async_computation.6 | async-start | bytes 4194304 | tf_op jit(solution)/shard_map/all_to_all | solution.py:297
  428.3 6.5 %collective-permute-start.39 = (bf16[128,4096]{1,0:T(8,128)(2,1)}, bf16[128,4096]{1,0:T(8,128)(2,1)S(1)}, u32[]{:S(2)}, u32[]{:S(2)}) collective-permute-start(bf16[128,4096]{1,0:T(8,128)(2,1)} %fusion.149), channel_id=1, source_target_pairs={{6,4},{7,5},{14,12},{15,13},{22,20},{23,21},{30,28},{31,29}} | collective-permute-start | bytes 3145736 | tf_op jit(solution)/shard_map/ppermute | solution.py:169
  432.3 27.1 %collective-permute-start.37 = (bf16[128,4096]{1,0:T(8,128)(2,1)}, bf16[128,4096]{1,0:T(8,128)(2,1)}, u32[]{:S(2)}, u32[]{:S(2)}) collective-permute-start(bf16[128,4096]{1,0:T(8,128)(2,1)} %get-tuple-element.2), channel_id=1, source_target_pairs={{0,2},{2,4},{1,3},{3,5},{8,10},{10,12},{9,11},{11,13},{16,18},{18,... | collective-permute-start | bytes 3145736 | tf_op jit(solution)/shard_map/ppermute | solution.py:165
  436.4 23.1 %collective-permute-start.40 = (bf16[128,4096]{1,0:T(8,128)(2,1)}, bf16[128,4096]{1,0:T(8,128)(2,1)}, u32[]{:S(2)}, u32[]{:S(2)}) collective-permute-start(bf16[128,4096]{1,0:T(8,128)(2,1)} %add_convert_fusion.1), channel_id=1, source_target_pairs={{4,2},{6,4},{5,3},{7,5},{12,10},{14,12},{13,11},{15,13},{20,18},{2... | collective-permute-start | bytes 3145736 | tf_op jit(solution)/shard_map/ppermute | solution.py:169
  452.7 39.8 %all-to-all-start.2 = ((bf16[8,32,4096]{2,1,0:T(8,128)(2,1)}), bf16[8,32,4096]{2,1,0:T(8,128)(2,1)}, u32[]{:S(2)}, u32[]{:S(2)}) async-start(bf16[8,32,4096]{2,1,0:T(8,128)(2,1)} %bitcast.216), calls=%async_computation.2 | async-start | bytes 4194304 | tf_op jit(solution)/shard_map/all_to_all | solution.py:297
  463.1 50.1 %collective-permute-start.41 = (bf16[128,4096]{1,0:T(8,128)(2,1)}, bf16[128,4096]{1,0:T(8,128)(2,1)S(1)}, u32[]{:S(2)}, u32[]{:S(2)}) collective-permute-start(bf16[128,4096]{1,0:T(8,128)(2,1)} %get-tuple-element.19), channel_id=1, source_target_pairs={{2,0},{4,2},{6,4},{3,1},{5,3},{7,5},{10,8},{12,10},{14,12},{11,9},... | collective-permute-start | bytes 3145736 | tf_op jit(solution)/shard_map/ppermute | solution.py:169
  464.4 50.1 %collective-permute-start.38 = (bf16[128,4096]{1,0:T(8,128)(2,1)}, bf16[128,4096]{1,0:T(8,128)(2,1)S(1)}, u32[]{:S(2)}, u32[]{:S(2)}) collective-permute-start(bf16[128,4096]{1,0:T(8,128)(2,1)} %get-tuple-element.18), channel_id=1, source_target_pairs={{0,2},{2,4},{4,6},{1,3},{3,5},{5,7},{8,10},{10,12},{12,14},{9,11},... | collective-permute-start | bytes 3145736 | tf_op jit(solution)/shard_map/ppermute | solution.py:165
  (25 other events, 205.3 us)

commit v2 on v1

--- a/solution.py
+++ b/solution.py
@@ -16,6 +16,7 @@
 AXES = ("y", "c", "z", "x")
 PLANE = ("y", "c", "x")
 BF = jnp.bfloat16
+VMEM = 20 * 2**20
 F32 = jnp.float32
 
 
@@ -148,47 +149,27 @@
     return (after_attention[None], layer_output[None])
 
 
-def pairs_of(sizes, axis, target):
-    found = []
-    for i in range(sizes[axis]):
-        j = target(i)
-        if j is not None:
-            found.append((i, j))
-    return found
-
-
 def swap(value, axis):
     return lax.ppermute(value, axis, [(0, 1), (1, 0)])
 
 
-def upward(value, first, last):
-    return lax.ppermute(value, "z", [(z, z + 1) for z in range(first, last + 1)])
-
-
-def downward(value, first, last):
-    return lax.ppermute(value, "z", [(z, z - 1) for z in range(first, last + 1)])
-
-
-def pick(z, options):
-    result = options[3]
-    for index in (2, 1, 0):
-        result = jnp.where(z == index, options[index], result)
-    return result
-
-
-def along_z(own, z):
-    up1, down1 = upward(own, 0, 2), downward(own, 1, 3)
-    up2, down2 = upward(up1, 1, 2), downward(down1, 1, 2)
-    up3, down3 = upward(up2, 2, 2), downward(down2, 1, 1)
-    return [
-        own,
-        pick(z, (down1, up1, down1, up1)),
-        pick(z, (down2, down1, up1, up2)),
-        pick(z, (down3, down2, up2, up3)),
-    ]
-
+def along(value, pairs):
+    return lax.ppermute(value, "z", pairs)
+
+
+OUTER = [(0, 1), (1, 0), (2, 3), (3, 2)]
+INNER = [(1, 2), (2, 1)]
+OUTWARD = [(1, 0), (2, 3)]
+INWARD = [(0, 1), (3, 2)]
 
 SOURCES = ((0, 1, 2, 3), (1, 0, 2, 3), (2, 3, 1, 0), (3, 2, 1, 0))
+
+
+def along_z(own, inner):
+    near, middle_in = along(own, OUTER), along(own, INNER)
+    middle_out, far_in = along(middle_in, OUTWARD), along(near, INNER)
+    far_out = along(far_in, OUTWARD)
+    return [own, near, jnp.where(inner, middle_in, middle_out), jnp.where(inner, far_in, far_out)]
 
 
 def attend_kernel(message_ref, out_ref, keys, values, *, group, tokens):
@@ -261,10 +242,10 @@
     )(message)
 
 
-def routing(ids, gates, z):
+def routing(ids, gates, z, inner):
     tokens = ids.shape[0]
     plane = 8
-    both = along_z(jnp.concatenate([ids, gates], axis=1), z)
+    both = along_z(jnp.concatenate([ids, gates], axis=1), inner)
     both = jnp.stack(both)
     ids4, gates4 = both[..., :TOPK], both[..., TOPK:]
     place = jnp.arange(plane)
@@ -288,13 +269,185 @@
         return jnp.where(at_slot, part[:, :, None, :], 0.0).astype(BF).reshape(4, slots, tokens)
 
     places = at_slot.astype(BF).reshape(4, slots, tokens)
-    shares = jnp.concatenate([spread(high), spread(low)], axis=-1)
+    shares = jnp.concatenate([spread(high), spread(low)], axis=-1).transpose(0, 2, 1)
     return places, shares
 
 
 def plane_exchange(rows):
     blocks = rows.reshape(8, -1, D)
     return lax.all_to_all(blocks, PLANE, split_axis=0, concat_axis=0, tiled=True).reshape(-1, D)
+
+
+def experts_kernel(*refs, blocks, steps):
+    rows, (gate_ref, up_ref, down_ref) = refs[:blocks], refs[blocks : blocks + 3]
+    outs, (gate, up, product) = refs[blocks + 3 : 2 * blocks + 3], refs[2 * blocks + 3 :]
+    step = pl.program_id(0)
+    count = rows[0].shape[0]
+    spans = [pl.ds(block * count, count) for block in range(blocks)]
+
+    @pl.when(step < steps)
+    def _():
+        for ref, span in zip(rows, spans):
+            more_gate = jnp.dot(ref[...], gate_ref[0], preferred_element_type=F32)
+            more_up = jnp.dot(ref[...], up_ref[0], preferred_element_type=F32)
+
+            @pl.when(step == 0)
+            def _():
+                gate[span, :] = more_gate
+                up[span, :] = more_up
+
+            @pl.when((step > 0) & (step < steps - 1))
+            def _():
+                gate[span, :] += more_gate
+                up[span, :] += more_up
+
+            @pl.when(step == steps - 1)
+            def _():
+                total = gate[span, :] + more_gate
+                silu = total / (1.0 + jnp.exp(-total))
+                product[span, :] = (silu * (up[span, :] + more_up)).astype(BF)
+
+    @pl.when(step >= steps)
+    def _():
+        for ref, span in zip(outs, spans):
+            ref[...] = jnp.dot(
+                product[span, :], down_ref[0], preferred_element_type=F32
+            ).astype(BF)
+
+
+def experts(blocks, gate_proj, up_proj, down_proj):
+    count, hidden = blocks[0].shape[0], gate_proj.shape[2]
+    total = count * len(blocks)
+    steps = 4
+    tile = D // steps
+    read = pl.BlockSpec((count, tile), lambda j: (0, jnp.minimum(j, steps - 1)))
+    write = pl.BlockSpec((count, tile), lambda j: (0, jnp.maximum(j - steps, 0)))
+    inner = pl.BlockSpec((1, tile, hidden), lambda j: (0, jnp.minimum(j, steps - 1), 0))
+    outer = pl.BlockSpec((1, hidden, tile), lambda j: (0, 0, jnp.maximum(j - steps, 0)))
+    return pl.pallas_call(
+        functools.partial(experts_kernel, blocks=len(blocks), steps=steps),
+        grid=(2 * steps,),
+        out_shape=[jax.ShapeDtypeStruct((count, D), BF)] * len(blocks),
+        in_specs=[read] * len(blocks) + [inner, inner, outer],
+        out_specs=[write] * len(blocks),
+        scratch_shapes=[
+            pltpu.VMEM((total, hidden), F32),
+            pltpu.VMEM((total, hidden), F32),
+            pltpu.VMEM((total, hidden), BF),
+        ],
+        compiler_params=pltpu.CompilerParams(vmem_limit_bytes=30 * 2**20),
+        cost_estimate=pl.CostEstimate(
+            flops=total, bytes_accessed=total, transcendentals=0
+        ),
+        name="experts",
+    )(*blocks, gate_proj, up_proj, down_proj)
+
+
+def expert_kernel(rows_ref, gate_ref, up_ref, down_ref, out_ref, total):
+    step = pl.program_id(0)
+    rows = rows_ref[...]
+    gate = jnp.dot(rows, gate_ref[0], preferred_element_type=F32)
+    up = jnp.dot(rows, up_ref[0], preferred_element_type=F32)
+    product = (gate / (1.0 + jnp.exp(-gate)) * up).astype(BF)
+    output = jnp.dot(product, down_ref[0], preferred_element_type=F32)
+
+    @pl.when(step == 0)
+    def _():
+        total[...] = output
+
+    @pl.when((step > 0) & (step < pl.num_programs(0) - 1))
+    def _():
+        total[...] += output
+
+    @pl.when(step == pl.num_programs(0) - 1)
+    def _():
+        out_ref[...] = (total[...] + output).astype(BF)
+
+
+def expert(rows, gate_proj, up_proj, down_proj):
+    count, hidden = rows.shape[0], gate_proj.shape[2]
+    tile = 256
+    return pl.pallas_call(
+        expert_kernel,
+        grid=(hidden // tile,),
+        out_shape=jax.ShapeDtypeStruct(rows.shape, BF),
+        in_specs=[
+            pl.BlockSpec((count, D), lambda j: (0, 0)),
+            pl.BlockSpec((1, D, tile), lambda j: (0, 0, j)),
+            pl.BlockSpec((1, D, tile), lambda j: (0, 0, j)),
+            pl.BlockSpec((1, tile, D), lambda j: (0, j, 0)),
+        ],
+        out_specs=pl.BlockSpec((count, D), lambda j: (0, 0)),
+        scratch_shapes=[pltpu.VMEM((count, D), F32)],
+        compiler_params=pltpu.CompilerParams(vmem_limit_bytes=40 * 2**20),
+        cost_estimate=pl.CostEstimate(
+            flops=6 * count * D * hidden,
+            bytes_accessed=6 * D * hidden + 4 * count * D,
+            transcendentals=count * hidden,
+        ),
+        name="expert",
+    )(rows, gate_proj, up_proj, down_proj)
+
+
+def combine_kernel(share_ref, rows_ref, *refs):
+    *added, out_ref = refs
+    both = jnp.dot(share_ref[...], rows_ref[...], preferred_element_type=F32)
+    tokens = out_ref.shape[0]
+    total = both[:tokens] + both[tokens:]
+    for ref in added:
+        total += ref[...].astype(F32)
+    out_ref[...] = total.astype(out_ref.dtype)
+
+
+def combine(share, rows, *added):
+    slots = rows.shape[0]
+    tokens = share.shape[0] // 2
+    tile = D // 2
+    block = pl.BlockSpec((tokens, tile), lambda j: (0, j))
+    return pl.pallas_call(
+        combine_kernel,
+        grid=(D // tile,),
+        out_shape=jax.ShapeDtypeStruct((tokens, D), BF),
+        in_specs=[
+            pl.BlockSpec((2 * tokens, slots), lambda j: (0, 0)),
+            pl.BlockSpec((slots, tile), lambda j: (0, j)),
+        ]
+        + [block] * len(added),
+        out_specs=block,
+        compiler_params=pltpu.CompilerParams(vmem_limit_bytes=VMEM),
+        cost_estimate=pl.CostEstimate(
+            flops=tokens, bytes_accessed=tokens, transcendentals=0
+        ),
+        name="combine",
+    )(share, rows, *added)
+
+
+def slots_kernel(place_ref, *refs):
+    *blocks, out_ref = refs
+    block = blocks[0][...]
+    for ref in blocks[1:]:
+        block = block + ref[...]
+    out_ref[...] = jnp.dot(place_ref[...], block, preferred_element_type=F32).astype(BF)
+
+
+def slots_of(place, *blocks):
+    slots, tokens = place.shape
+    tile = D // 2
+    return pl.pallas_call(
+        slots_kernel,
+        grid=(D // tile,),
+        out_shape=jax.ShapeDtypeStruct((slots, D), BF),
+        in_specs=[pl.BlockSpec((slots, tokens), lambda j: (0, 0))]
+        + [pl.BlockSpec((tokens, tile), lambda j: (0, j))] * len(blocks),
+        out_specs=pl.BlockSpec((slots, tile), lambda j: (0, j)),
+        compiler_params=pltpu.CompilerParams(vmem_limit_bytes=VMEM),
+        cost_estimate=pl.CostEstimate(flops=slots, bytes_accessed=slots, transcendentals=0),
+        name="slots",
+    )(place, *blocks)
+
+
+def together(*values):
+    return lax.optimization_barrier(values)
 
 
 def tuned_device(
@@ -316,6 +469,7 @@
     tokens = hidden.shape[1]
     group = queries.shape[2] // HD // KVH
     source = jnp.array(SOURCES, jnp.int32)[z]
+    inner = (z == 1) | (z == 2)
 
     def by_head(value):
         return value[0].reshape(tokens, KVH, -1).transpose(1, 0, 2)
@@ -330,13 +484,30 @@
     in_order = jnp.concatenate(
         [lax.dynamic_slice_in_dim(attended, h * HD, HD, axis=1) for h in heads], axis=1
     )
+    own = out_weight
+    near, middle_in, across = together(along(own, OUTER), along(own, INNER), swap(own, "x"))
+    middle_out, far_in, near_x, ids, gates = together(
+        along(middle_in, OUTWARD),
+        along(near, INNER),
+        swap(near, "x"),
+        expert_ids[0],
+        gate_fixed[0],
+    )
+    middle = jnp.where(inner, middle_in, middle_out)
     parts = 2
     width = D // parts
+    columns = [slice(part * width, (part + 1) * width) for part in range(parts)]
+    far_out, middle_x, last_in = together(
+        along(far_in, OUTWARD), swap(middle, "x"), along(near_x[:, columns[1]], INNER)
+    )
+    places, shares = routing(ids, gates, z, inner)
+    far = jnp.where(inner, far_in, far_out)
+    line = [own, near, middle, far, across, near_x, middle_x]
+    last, last_out = together(swap(far[:, columns[0]], "x"), along(last_in, OUTWARD))
+    last = [last, jnp.where(inner, last_in, last_out)]
     projected = []
     for part in range(parts):
-        mine = out_weight[:, part * width : (part + 1) * width]
-        line = along_z(mine, z)
-        weight = jnp.concatenate(line + [swap(block, "x") for block in line], axis=0)
+        weight = jnp.concatenate([block[:, columns[part]] for block in line] + [last[part]], axis=0)
         partial = jnp.dot(in_order, weight, preferred_element_type=F32)
         partial = partial.reshape(2, 2, tokens, width)
         other = lax.dynamic_index_in_dim(partial, 1 - c, 1, keepdims=False).astype(BF)
@@ -354,28 +525,43 @@
         * norm_gain.astype(F32)
     ).astype(BF)
 
-    places, shares = routing(expert_ids[0], gate_fixed[0], z)
-    blocks = along_z(normed, z)
-    results = []
-    for k in range(4):
-        sent = jnp.dot(places[k], blocks[k], preferred_element_type=F32).astype(BF)
-        results.append(expert_ffn(plane_exchange(sent), gate_proj[0], up_proj[0], down_proj[0]))
-    sums = [None] * 4
-    for k in (3, 2, 1, 0):
-        returned = plane_exchange(results[k])
-        both = lax.dot_general(
-            shares[k], returned, (((0,), (0,)), ((), ())), preferred_element_type=F32
-        )
-        sums[k] = both[:tokens] + both[tokens:]
-    own, near, middle, far = sums
-
-    up = upward(far.astype(BF), 0, 0)
-    down = downward(far.astype(BF), 3, 3)
-    up = upward((jnp.where(z == 0, middle, far) + up.astype(F32)).astype(BF), 0, 1)
-    down = downward((jnp.where(z == 3, middle, far) + down.astype(F32)).astype(BF), 2, 3)
-    up = upward((jnp.where(z == 1, middle, near) + up.astype(F32)).astype(BF), 0, 2)
-    down = downward((jnp.where(z == 2, middle, near) + down.astype(F32)).astype(BF), 1, 3)
-    layer_output = (after_float + own + up.astype(F32) + down.astype(F32)).astype(BF)
+    weights = (gate_proj, up_proj, down_proj)
+
+    near, middle_in = along(normed, OUTER), along(normed, INNER)
+    own_rows = plane_exchange(slots_of(places[0], normed))
+    near_slots, own_rows = together(slots_of(places[1], near), own_rows)
+    near_rows = plane_exchange(near_slots)
+    middle_out, far_in = along(middle_in, OUTWARD), along(near, INNER)
+    middle_slots, near_rows, far_in, shares = together(
+        slots_of(places[2], middle_in, middle_out), near_rows, far_in, shares
+    )
+    middle_rows = plane_exchange(middle_slots)
+    far_out = along(far_in, OUTWARD)
+    own_out, near_out = experts((own_rows, near_rows), *weights)
+    far_slots, middle_rows, own_out, near_out = together(
+        slots_of(places[3], far_in, far_out), middle_rows, own_out, near_out
+    )
+    far_rows = plane_exchange(far_slots)
+    middle_out = expert(middle_rows, *weights)
+    far_rows, middle_out = together(far_rows, middle_out)
+    far_out = expert(far_rows, *weights)
+
+    far = plane_exchange(far_out)
+    far_sum = combine(shares[3], far)
+    middle_out, far, far_sum = together(middle_out, far, far_sum)
+    middle = plane_exchange(middle_out)
+    outer_far = along(far_sum, INWARD)
+    near_out, middle, outer_far = together(near_out, middle, outer_far)
+    near = plane_exchange(near_out)
+    outer_middle = along(combine(shares[2], middle), INWARD)
+    inner_far = along(combine(shares[3], far, outer_far), INNER)
+    own_out, near, outer_middle, inner_far = together(own_out, near, outer_middle, inner_far)
+    own = plane_exchange(own_out)
+    inner_middle = along(combine(shares[2], middle, outer_middle), INNER)
+    all_near = along(combine(shares[1], near, inner_far), OUTER)
+    layer_output = combine(
+        shares[0], own, after_attention, inner_middle, all_near
+    )
     return (after_attention[None], layer_output[None])
 
 

time: 518 us -> 433 us (0.84)
  matrix products: 95 us -> 9.18 us
  starting transfers between devices: 139 us -> 82.1 us
  Pallas kernels: 10.7 us -> 65.6 us
  local copies, waits for them, and re-layouts: 22.6 us -> 55 us
  waiting for transfers between devices: 221 us -> 206 us
  other arithmetic: 23.4 us -> 8.68 us
    dot_general x16 -> x0, matrix products: 88 us -> none  [the longest x4 45.4 us: expert_ffn(): output = jnp.dot(product, down_matrix, preferred_element_type=jnp.float32)]
    pallas_call x0 -> x13, Pallas kernels: none -> 55 us  [the longest x2 19.2 us: expert(): pl.pallas_call(expert_kernel, grid=(hidden // tile,), out_shape=jax.Shape...]
    ppermute x30 -> x22, starting transfers between devices: 80.1 us -> 38.2 us  [along(): return lax.ppermute(value, 'z', pairs)]
    ppermute x12 -> x8, waiting for transfers between devices: 62.8 us -> 27.7 us  [swap(): return lax.ppermute(value, axis, [(0, 1), (1, 0)])]
    unnamed x66 -> x93, local copies, waits for them, and re-layouts: 15.2 us -> 41.1 us
    ppermute x30 -> x22, waiting for transfers between devices: 119 us -> 141 us  [along(): return lax.ppermute(value, 'z', pairs)]
    all_to_all x8, starting transfers between devices: 45.4 us -> 32.4 us  [plane_exchange(): lax.all_to_all(blocks, PLANE, split_axis=0, concat_axis=0, tiled=True)]
    convert_element_type x4 -> x1, other arithmetic: 9.69 us -> 0.12 us  [routing(): places = at_slot.astype(BF).reshape(4, slots, tokens)]
  transfers between devices with their start and end apart: 51 -> 39, of which waited for: 23 -> 18; matrix products, arithmetic and copies ran while one was open for 25% -> 9% of each run, Pallas kernels for 2% -> 12%
where the time goes in v2:
time: 433 us; the launch traced here: 431 us
  waiting for transfers between devices  206 us (48%)
  starting transfers between devices  82.1 us (19%)
  Pallas kernels  65.6 us (15%)
  local copies, waits for them, and re-layouts  55 us (13%)
  matrix products  9.18 us (2%)
  other arithmetic  8.68 us (2%)
    ppermute x22, waiting for transfers between devices, along(): return lax.ppermute(value, 'z', pairs)  141 us
    unnamed x93, local copies, waits for them, and re-layouts  41.1 us
    ppermute x22, starting transfers between devices, along(): return lax.ppermute(value, 'z', pairs)  38.2 us
    all_to_all x8, waiting for transfers between devices, plane_exchange(): lax.all_to_all(blocks, PLANE, split_axis=0, concat_axis=0, tiled=True)  36.4 us
    all_to_all x8, starting transfers between devices, plane_exchange(): lax.all_to_all(blocks, PLANE, split_axis=0, concat_axis=0, tiled=True)  32.4 us
    ppermute x8, waiting for transfers between devices, swap(): return lax.ppermute(value, axis, [(0, 1), (1, 0)])  27.7 us
    pallas_call x2, Pallas kernels, expert(): pl.pallas_call(expert_kernel, grid=(hidden // tile,), out_shape=jax.Shape...  19.2 us
    pallas_call x1, Pallas kernels, experts(): pl.pallas_call(functools.partial(experts_kernel, blocks=len(blocks), step...  16 us
  transfers between devices with their start and end apart: 39, of which 18 were waited for; matrix products, arithmetic and copies ran while one was open for 9% of the time, Pallas kernels for 12%

profile of v2, /device:TPU:0, one launch (start us, length us, event | category | flops | bytes accessed | tf_op | source)
XLA Modules:
  0.0 430.7 jit_solution(5307646311064128941)
XLA Ops:
  0.7 3.1 collective-permute-start
  14.0 3.6 all-to-all-start
  22.6 4.6 %collective-permute-done = bf16[128,4096]{1,0:T(8,128)(2,1)} collective-permute-done((bf16[128,4096]{1,0:T(8,128)(2,1)}, bf16[128,4096]{1,0:T(8,128)(2,1)}, u32[]{:S(2)}, u32[]{:S(2)}) %collective-permute-start) | collective-permute-done | bytes 1048608 | tf_op jit(solution)/shard_map/ppermute | solution.py:157
  27.2 3.1 collective-permute-done.2
  34.7 2.3 slice_dynamic-update-slice_fusion.10
  37.6 10.7 %attention.1 = bf16[512,1024]{1,0:T(8,128)(2,1)S(1)} custom-call(bf16[4,128,1536]{2,1,0:T(8,128)(2,1)S(1)} %all-to-all-done.message_ref), custom_call_target="tpu_custom_call" | custom-call | flops 1744830464 | bytes 2621440 | tf_op jit(solution)/shard_map/attention/pallas_call | solution.py:229
  48.8 11.5 %collective-permute-done.3 = bf16[128,4096]{1,0:T(8,128)(2,1)} collective-permute-done((bf16[128,4096]{1,0:T(8,128)(2,1)}, bf16[128,4096]{1,0:T(8,128)(2,1)}, u32[]{:S(2)}, u32[]{:S(2)}) %collective-permute-start.3) | collective-permute-done | bytes 1048608 | tf_op jit(solution)/shard_map/ppermute | solution.py:157
  69.5 17.8 %collective-permute-done.17 = s32[128,8]{0,1:T(8,128)S(1)} collective-permute-done((s32[128,8]{0,1:T(8,128)S(1)}, s32[128,8]{0,1:T(8,128)S(1)}, u32[]{:S(2)}, u32[]{:S(2)}) %collective-permute-start.17) | collective-permute-done | bytes 4128 | tf_op jit(solution)/shard_map/ppermute | solution.py:157
  90.7 2.3 slice_dynamic-update-slice_fusion.9
  95.3 3.2 collective-permute-done.9
  98.5 3.4 collective-permute-done.10
  103.1 4.5 %fusion.27 = f32[512,2048]{1,0:T(8,128)S(1)} fusion(bf16[512,1024]{1,0:T(8,128)(2,1)S(1)} %dynamic-slice_dynamic-update-slice_fusion, bf16[1024,2048]{1,0:T(8,128)(2,1)} %get-tuple-element.113), kind=kOutput, calls=%fused_computation.100 | convolution fusion | flops 2147483648 | bytes 9437184 | tf_op jit(solution)/shard_map/dot_general | solution.py:511
  107.9 4.5 %fusion.26 = f32[512,2048]{1,0:T(8,128)S(1)} fusion(bf16[512,1024]{1,0:T(8,128)(2,1)S(1)} %dynamic-slice_dynamic-update-slice_fusion, bf16[1024,2048]{1,0:T(8,128)(2,1)} %get-tuple-element.114), kind=kOutput, calls=%fused_computation.99 | convolution fusion | flops 2147483648 | bytes 9437184 | tf_op jit(solution)/shard_map/dot_general | solution.py:511
  117.5 11.1 %collective-permute-done.14 = bf16[128,2048]{1,0:T(8,128)(2,1)S(1)} collective-permute-done((bf16[128,2048]{1,0:T(8,128)(2,1)S(1)}, bf16[128,2048]{1,0:T(8,128)(2,1)S(1)}, u32[]{:S(2)}, u32[]{:S(2)}) %collective-permute-start.14) | collective-permute-done | bytes 524320 | tf_op jit(solution)/shard_map/ppermute | solution.py:153
  128.7 10.1 %collective-permute-done.12 = bf16[128,2048]{1,0:T(8,128)(2,1)S(1)} collective-permute-done((bf16[128,2048]{1,0:T(8,128)(2,1)S(1)}, bf16[128,2048]{1,0:T(8,128)(2,1)S(1)}, u32[]{:S(2)}, u32[]{:S(2)}) %collective-permute-start.12) | collective-permute-done | bytes 524320 | tf_op jit(solution)/shard_map/ppermute | solution.py:153
  140.0 1.9 slots.6
  142.9 3.7 all-to-all-start.1
  148.6 23.9 %collective-permute-done.22.refs_0_ = bf16[128,4096]{1,0:T(8,128)(2,1)S(1)} collective-permute-done((bf16[128,4096]{1,0:T(8,128)(2,1)}, bf16[128,4096]{1,0:T(8,128)(2,1)S(1)}, u32[]{:S(2)}, u32[]{:S(2)}) %collective-permute-start.22) | collective-permute-done | bytes 1048608 | tf_op jit(solution)/shard_map/ppermute | solution.py:157
  172.4 1.9 slots.5
  175.4 4.4 %all-to-all-start.2 = ((bf16[8,32,4096]{2,1,0:T(8,128)(2,1)}), bf16[8,32,4096]{2,1,0:T(8,128)(2,1)}, u32[]{:S(2)}, u32[]{:S(2)}) async-start(bf16[8,32,4096]{2,1,0:T(8,128)(2,1)} %bitcast.39), calls=%async_computation.2 | async-start | bytes 4194304 | tf_op jit(solution)/shard_map/all_to_all | solution.py:278
  187.4 2.0 copy.54
  194.3 13.2 %collective-permute-done.21.refs_1_ = bf16[128,4096]{1,0:T(8,128)(2,1)} collective-permute-done((bf16[128,4096]{1,0:T(8,128)(2,1)}, bf16[128,4096]{1,0:T(8,128)(2,1)}, u32[]{:S(2)}, u32[]{:S(2)}) %collective-permute-start.21) | collective-permute-done | bytes 1048608 | tf_op jit(solution)/shard_map/ppermute | solution.py:157
  207.5 3.1 slots.4
  210.5 4.4 %all-to-all-start.3 = ((bf16[8,32,4096]{2,1,0:T(8,128)(2,1)}), bf16[8,32,4096]{2,1,0:T(8,128)(2,1)}, u32[]{:S(2)}, u32[]{:S(2)}) async-start(bf16[8,32,4096]{2,1,0:T(8,128)(2,1)} %bitcast.48), calls=%async_computation.3 | async-start | bytes 4194304 | tf_op jit(solution)/shard_map/all_to_all | solution.py:278
  216.4 2.8 copy-done
  219.2 2.8 copy-done.3
  222.0 16.0 %experts.1 = (bf16[256,4096]{1,0:T(8,128)(2,1)S(1)}, bf16[256,4096]{1,0:T(8,128)(2,1)S(1)}) custom-call(bf16[256,4096]{1,0:T(8,128)(2,1)S(1)} %bitcast.110, bf16[256,4096]{1,0:T(8,128)(2,1)} %bitcast.40.refs_1_, bf16[1,4096,768]{2,1,0:T(8,128)(2,1)S(1)} %copy-done, bf16[1,4096,768]{2,1,0:T(8,128)(2,1)S(1)} %copy-done.3, bf16[1,768,4096]{2,1,0:T(8,128)(2,1)} %down_ref.3), custom_call_target="tpu_custom_call" | custom-call | flops 512 | bytes 512 | tf_op jit(solution)/shard_map/experts/pallas_call | solution.py:327
  242.4 2.9 slots.7
  245.3 3.9 all-to-all-start.4
  249.2 2.8 copy-done.1
  252.0 9.9 %expert.2 = bf16[256,4096]{1,0:T(8,128)(2,1)S(1)} custom-call(bf16[256,4096]{1,0:T(8,128)(2,1)} %bitcast.49.rows_ref, bf16[1,4096,768]{2,1,0:T(8,128)(2,1)S(1)} %copy-done.1, bf16[1,4096,768]{2,1,0:T(8,128)(2,1)} %up_ref.3, bf16[1,768,4096]{2,1,0:T(8,128)(2,1)} %down_ref.3), custom_call_target="tpu_custom_call" | custom-call | flops 4831838208 | bytes 23068672 | tf_op jit(solution)/shard_map/expert/pallas_call | solution.py:370
  263.3 12.1 %all-to-all-done.4 = bf16[8,32,4096]{2,1,0:T(8,128)(2,1)S(1)} async-done(((bf16[8,32,4096]{2,1,0:T(8,128)(2,1)}), bf16[8,32,4096]{2,1,0:T(8,128)(2,1)S(1)}, u32[]{:S(2)}, u32[]{:S(2)}) %all-to-all-start.4) | async-done | bytes 2097184 | tf_op jit(solution)/shard_map/all_to_all | solution.py:278
  275.4 2.8 copy-done.2
  278.1 9.3 %expert.3 = bf16[256,4096]{1,0:T(8,128)(2,1)S(1)} custom-call(bf16[256,4096]{1,0:T(8,128)(2,1)S(1)} %bitcast.112, bf16[1,4096,768]{2,1,0:T(8,128)(2,1)S(1)} %copy-done.2, bf16[1,4096,768]{2,1,0:T(8,128)(2,1)} %up_ref.3, bf16[1,768,4096]{2,1,0:T(8,128)(2,1)} %down_ref.3), custom_call_target="tpu_custom_call" | custom-call | flops 4831838208 | bytes 23068672 | tf_op jit(solution)/shard_map/expert/pallas_call | solution.py:370
  288.8 3.6 all-to-all-start.5
  292.5 1.8 slice_bitcast_fusion
  294.2 24.3 %all-to-all-done.5 = bf16[8,32,4096]{2,1,0:T(8,128)(2,1)S(1)} async-done(((bf16[8,32,4096]{2,1,0:T(8,128)(2,1)}), bf16[8,32,4096]{2,1,0:T(8,128)(2,1)S(1)}, u32[]{:S(2)}, u32[]{:S(2)}) %all-to-all-start.5) | async-done | bytes 2097184 | tf_op jit(solution)/shard_map/all_to_all | solution.py:278
  320.7 3.6 all-to-all-start.6
  324.3 3.2 collective-permute-start.25
  327.5 23.2 %collective-permute-done.25.refs_0_ = bf16[128,4096]{1,0:T(8,128)(2,1)S(1)} collective-permute-done((bf16[128,4096]{1,0:T(8,128)(2,1)}, bf16[128,4096]{1,0:T(8,128)(2,1)S(1)}, u32[]{:S(2)}, u32[]{:S(2)}) %collective-permute-start.25) | collective-permute-done | bytes 1048608 | tf_op jit(solution)/shard_map/ppermute | solution.py:157
  351.7 4.4 %all-to-all-start.7 = ((bf16[8,32,4096]{2,1,0:T(8,128)(2,1)}), bf16[8,32,4096]{2,1,0:T(8,128)(2,1)}, u32[]{:S(2)}, u32[]{:S(2)}) async-start(bf16[8,32,4096]{2,1,0:T(8,128)(2,1)} %bitcast.115), calls=%async_computation.7 | async-start | bytes 4194304 | tf_op jit(solution)/shard_map/all_to_all | solution.py:278
  357.2 4.4 %collective-permute-start.26 = (bf16[128,4096]{1,0:T(8,128)(2,1)S(1)}, bf16[128,4096]{1,0:T(8,128)(2,1)S(1)}, u32[]{:S(2)}, u32[]{:S(2)}) collective-permute-start(bf16[128,4096]{1,0:T(8,128)(2,1)S(1)} %combine.7), channel_id=1, source_target_pairs={{0,2},{6,4},{1,3},{7,5},{8,10},{14,12},{9,11},{15,13},{16,18},{22,... | collective-permute-start | bytes 3145736 | tf_op jit(solution)/shard_map/ppermute | solution.py:157
  364.8 19.7 %collective-permute-done.26.refs_0_ = bf16[128,4096]{1,0:T(8,128)(2,1)S(1)} collective-permute-done((bf16[128,4096]{1,0:T(8,128)(2,1)S(1)}, bf16[128,4096]{1,0:T(8,128)(2,1)S(1)}, u32[]{:S(2)}, u32[]{:S(2)}) %collective-permute-start.26) | collective-permute-done | bytes 1048608 | tf_op jit(solution)/shard_map/ppermute | solution.py:157
  386.6 4.5 %all-to-all-start.8 = ((bf16[8,32,4096]{2,1,0:T(8,128)(2,1)}), bf16[8,32,4096]{2,1,0:T(8,128)(2,1)}, u32[]{:S(2)}, u32[]{:S(2)}) async-start(bf16[8,32,4096]{2,1,0:T(8,128)(2,1)} %bitcast.114), calls=%async_computation.8 | async-start | bytes 4194304 | tf_op jit(solution)/shard_map/all_to_all | solution.py:278
  394.4 2.2 combine.10
  396.6 7.6 %collective-permute-start.29 = (bf16[128,4096]{1,0:T(8,128)(2,1)S(1)}, bf16[128,4096]{1,0:T(8,128)(2,1)S(1)}, u32[]{:S(2)}, u32[]{:S(2)}) collective-permute-start(bf16[128,4096]{1,0:T(8,128)(2,1)S(1)} %combine.10), channel_id=1, source_target_pairs={{0,2},{2,0},{4,6},{6,4},{1,3},{3,1},{5,7},{7,5},{8,10},{10,8},{12,... | collective-permute-start | bytes 3145736 | tf_op jit(solution)/shard_map/ppermute | solution.py:157
  405.4 22.2 %collective-permute-done.29.refs_2_ = bf16[128,4096]{1,0:T(8,128)(2,1)S(1)} collective-permute-done((bf16[128,4096]{1,0:T(8,128)(2,1)S(1)}, bf16[128,4096]{1,0:T(8,128)(2,1)S(1)}, u32[]{:S(2)}, u32[]{:S(2)}) %collective-permute-start.29) | collective-permute-done | bytes 1048608 | tf_op jit(solution)/shard_map/ppermute | solution.py:157
  427.6 3.1 combine.11
  (191 shorter events, 79.3 us)
Async XLA Ops:
  0.7 26.6 %collective-permute-start = (bf16[128,4096]{1,0:T(8,128)(2,1)}, bf16[128,4096]{1,0:T(8,128)(2,1)}, u32[]{:S(2)}, u32[]{:S(2)}) collective-permute-start(bf16[128,4096]{1,0:T(8,128)(2,1)} %param.20), channel_id=1, source_target_pairs={{0,2},{2,0},{4,6},{6,4},{1,3},{3,1},{5,7},{7,5},{8,10},{10,8},{12,... | collective-permute-start | bytes 3145736 | tf_op jit(solution)/shard_map/ppermute | solution.py:157
  3.8 23.5 %collective-permute-start.1 = (bf16[128,4096]{1,0:T(8,128)(2,1)}, bf16[128,4096]{1,0:T(8,128)(2,1)}, u32[]{:S(2)}, u32[]{:S(2)}) collective-permute-start(bf16[128,4096]{1,0:T(8,128)(2,1)} %param.20), channel_id=1, source_target_pairs={{2,4},{4,2},{3,5},{5,3},{10,12},{12,10},{11,13},{13,11},{18,20},{2... | collective-permute-start | bytes 3145736 | tf_op jit(solution)/shard_map/ppermute | solution.py:157
  5.4 24.9 %collective-permute-start.2 = (bf16[128,4096]{1,0:T(8,128)(2,1)}, bf16[128,4096]{1,0:T(8,128)(2,1)}, u32[]{:S(2)}, u32[]{:S(2)}) collective-permute-start(bf16[128,4096]{1,0:T(8,128)(2,1)} %param.20), channel_id=1, source_target_pairs={{0,1},{1,0},{2,3},{3,2},{4,5},{5,4},{6,7},{7,6},{8,9},{9,8},{10,11... | collective-permute-start | bytes 3145736 | tf_op jit(solution)/shard_map/ppermute | solution.py:153
  9.0 12.4 %copy-start.32 = (bf16[4096]{0:T(1024)(128)(2,1)S(1)}, bf16[4096]{0:T(1024)(128)(2,1)}, u32[]{:S(2)}) copy-start(bf16[4096]{0:T(1024)(128)(2,1)} %param.21) | copy-start | bytes 24580
  9.1 12.5 %copy-start.26 = (bf16[128,4096]{1,0:T(8,128)(2,1)S(1)}, bf16[128,4096]{1,0:T(8,128)(2,1)}, u32[]{:S(2)}) copy-start(bf16[128,4096]{1,0:T(8,128)(2,1)} %param.20) | copy-start | bytes 3145732
  14.0 23.6 %all-to-all-start = ((bf16[4,128,1536]{2,1,0:T(8,128)(2,1)}), bf16[4,128,1536]{2,1,0:T(8,128)(2,1)S(1)}, u32[]{:S(2)}, u32[]{:S(2)}) async-start(bf16[4,128,1536]{2,1,0:T(8,128)(2,1)} %bitcast_dynamic-update-slice_fusion.1), calls=%async_computation | async-start | bytes 3145728 | tf_op jit(solution)/shard_map/all_to_all | solution.py:480
  30.3 30.0 %collective-permute-start.4 = (bf16[128,4096]{1,0:T(8,128)(2,1)}, bf16[128,4096]{1,0:T(8,128)(2,1)}, u32[]{:S(2)}, u32[]{:S(2)}) collective-permute-start(bf16[128,4096]{1,0:T(8,128)(2,1)} %collective-permute-done), channel_id=1, source_target_pairs={{2,4},{4,2},{3,5},{5,3},{10,12},{12,10},{11,13},{13,11},{18,20},{2... | collective-permute-start | bytes 3145736 | tf_op jit(solution)/shard_map/ppermute | solution.py:157
  32.0 28.3 %collective-permute-start.5 = (bf16[128,4096]{1,0:T(8,128)(2,1)}, bf16[128,4096]{1,0:T(8,128)(2,1)S(1)}, u32[]{:S(2)}, u32[]{:S(2)}) collective-permute-start(bf16[128,4096]{1,0:T(8,128)(2,1)} %collective-permute-done), channel_id=1, source_target_pairs={{0,1},{1,0},{2,3},{3,2},{4,5},{5,4},{6,7},{7,6},{8,9},{9,8},{10,11... | collective-permute-start | bytes 3145736 | tf_op jit(solution)/shard_map/ppermute | solution.py:153
  33.5 26.8 %collective-permute-start.3 = (bf16[128,4096]{1,0:T(8,128)(2,1)}, bf16[128,4096]{1,0:T(8,128)(2,1)}, u32[]{:S(2)}, u32[]{:S(2)}) collective-permute-start(bf16[128,4096]{1,0:T(8,128)(2,1)} %collective-permute-done.1), channel_id=1, source_target_pairs={{2,0},{4,6},{3,1},{5,7},{10,8},{12,14},{11,9},{13,15},{18,16},{20,... | collective-permute-start | bytes 3145736 | tf_op jit(solution)/shard_map/ppermute | solution.py:157
  37.0 23.3 %copy-start.33 = (s32[1,128,4]{1,2,0:T(4,128)S(1)}, s32[1,128,4]{1,2,0:T(4,128)}, u32[]{:S(2)}) copy-start(s32[1,128,4]{1,2,0:T(4,128)} %param.26) | copy-start | bytes 6148
  37.0 23.3 %copy-start.34 = (s32[1,128,4]{1,2,0:T(4,128)S(1)}, s32[1,128,4]{1,2,0:T(4,128)}, u32[]{:S(2)}) copy-start(s32[1,128,4]{1,2,0:T(4,128)} %param.25) | copy-start | bytes 6148
  60.3 4.8 %collective-permute-start.15 = (s32[128,8]{0,1:T(8,128)S(1)}, s32[128,8]{0,1:T(8,128)S(1)}, u32[]{:S(2)}, u32[]{:S(2)}) collective-permute-start(s32[128,8]{0,1:T(8,128)S(1)} %get-tuple-element.108), channel_id=1, source_target_pairs={{0,2},{2,0},{4,6},{6,4},{1,3},{3,1},{5,7},{7,5},{8,10},{10,8},{12,... | collective-permute-start | bytes 12296 | tf_op jit(solution)/shard_map/ppermute | solution.py:157
  60.4 5.4 %collective-permute-start.16 = (s32[128,8]{0,1:T(8,128)S(1)}, s32[128,8]{0,1:T(8,128)S(1)}, u32[]{:S(2)}, u32[]{:S(2)}) collective-permute-start(s32[128,8]{0,1:T(8,128)S(1)} %get-tuple-element.108), channel_id=1, source_target_pairs={{2,4},{4,2},{3,5},{5,3},{10,12},{12,10},{11,13},{13,11},{18,20},{2... | collective-permute-start | bytes 12296 | tf_op jit(solution)/shard_map/ppermute | solution.py:157
  61.1 26.4 %collective-permute-start.6 = (bf16[128,4096]{1,0:T(8,128)(2,1)}, bf16[128,4096]{1,0:T(8,128)(2,1)S(1)}, u32[]{:S(2)}, u32[]{:S(2)}) collective-permute-start(bf16[128,4096]{1,0:T(8,128)(2,1)} %collective-permute-done.4), channel_id=1, source_target_pairs={{2,0},{4,6},{3,1},{5,7},{10,8},{12,14},{11,9},{13,15},{18,16},{20,... | collective-permute-start | bytes 3145736 | tf_op jit(solution)/shard_map/ppermute | solution.py:157
  63.7 23.7 %collective-permute-start.7 = (bf16[128,4096]{1,0:T(8,128)(2,1)S(1)}, bf16[128,4096]{1,0:T(8,128)(2,1)S(1)}, u32[]{:S(2)}, u32[]{:S(2)}) collective-permute-start(bf16[128,4096]{1,0:T(8,128)(2,1)S(1)} %broadcast_select_fusion.1), channel_id=1, source_target_pairs={{0,1},{1,0},{2,3},{3,2},{4,5},{5,4},{6,7},{7,6},{8,9},{9,8},{10,11... | collective-permute-start | bytes 3145736 | tf_op jit(solution)/shard_map/ppermute | solution.py:153
  64.4 23.0 %collective-permute-start.8 = (bf16[128,2048]{1,0:T(8,128)(2,1)S(1)}, bf16[128,2048]{1,0:T(8,128)(2,1)S(1)}, u32[]{:S(2)}, u32[]{:S(2)}) collective-permute-start(bf16[128,2048]{1,0:T(8,128)(2,1)S(1)} %slice.107), channel_id=1, source_target_pairs={{2,4},{4,2},{3,5},{5,3},{10,12},{12,10},{11,13},{13,11},{18,20},{2... | collective-permute-start | bytes 1572872 | tf_op jit(solution)/shard_map/ppermute | solution.py:157
  65.2 3.0 collective-permute-start.18
  65.8 21.4 %collective-permute-start.17 = (s32[128,8]{0,1:T(8,128)S(1)}, s32[128,8]{0,1:T(8,128)S(1)}, u32[]{:S(2)}, u32[]{:S(2)}) collective-permute-start(s32[128,8]{0,1:T(8,128)S(1)} %collective-permute-done.16), channel_id=1, source_target_pairs={{2,0},{4,6},{3,1},{5,7},{10,8},{12,14},{11,9},{13,15},{18,16},{20,... | collective-permute-start | bytes 12296 | tf_op jit(solution)/shard_map/ppermute | solution.py:157
  68.2 19.2 %collective-permute-start.19 = (s32[128,8]{0,1:T(8,128)S(1)}, s32[128,8]{0,1:T(8,128)S(1)}, u32[]{:S(2)}, u32[]{:S(2)}) collective-permute-start(s32[128,8]{0,1:T(8,128)S(1)} %collective-permute-done.18), channel_id=1, source_target_pairs={{2,0},{4,6},{3,1},{5,7},{10,8},{12,14},{11,9},{13,15},{18,16},{20,... | collective-permute-start | bytes 12296 | tf_op jit(solution)/shard_map/ppermute | solution.py:157
  87.4 25.8 %copy-start.31 = (pred[4,8,128]{2,1,0:T(8,128)(4,1)}, pred[4,8,128]{2,1,0:T(8,128)(4,1)S(1)}, u32[]{:S(2)}) copy-start(pred[4,8,128]{2,1,0:T(8,128)(4,1)S(1)} %compare_reduce_fusion) | copy-start | bytes 12292
  88.7 9.8 %collective-permute-start.9 = (bf16[128,2048]{1,0:T(8,128)(2,1)S(1)}, bf16[128,2048]{1,0:T(8,128)(2,1)S(1)}, u32[]{:S(2)}, u32[]{:S(2)}) collective-permute-start(bf16[128,2048]{1,0:T(8,128)(2,1)S(1)} %get-tuple-element.88), channel_id=1, source_target_pairs={{0,1},{1,0},{2,3},{3,2},{4,5},{5,4},{6,7},{7,6},{8,9},{9,8},{10,11... | collective-permute-start | bytes 1572872 | tf_op jit(solution)/shard_map/ppermute | solution.py:153
  89.3 12.7 %collective-permute-start.10 = (bf16[128,2048]{1,0:T(8,128)(2,1)S(1)}, bf16[128,2048]{1,0:T(8,128)(2,1)S(1)}, u32[]{:S(2)}, u32[]{:S(2)}) collective-permute-start(bf16[128,2048]{1,0:T(8,128)(2,1)S(1)} %collective-permute-done.8), channel_id=1, source_target_pairs={{2,0},{4,6},{3,1},{5,7},{10,8},{12,14},{11,9},{13,15},{18,16},{20,... | collective-permute-start | bytes 1572872 | tf_op jit(solution)/shard_map/ppermute | solution.py:157
  107.8 5.6 %collective-permute-start.13 = (bf16[2,128,2048]{2,1,0:T(8,128)(2,1)S(1)}, bf16[2,128,2048]{2,1,0:T(8,128)(2,1)S(1)}, u32[]{:S(2)}, u32[]{:S(2)}) collective-permute-start(bf16[2,128,2048]{2,1,0:T(8,128)(2,1)S(1)} %fusion.7), channel_id=1, source_target_pairs={{0,8},{8,0},{1,9},{9,1},{2,10},{10,2},{3,11},{11,3},{4,12},{12,4},... | collective-permute-start | bytes 3145736 | tf_op jit(solution)/shard_map/ppermute | solution.py:153
  112.6 2.8 collective-permute-start.11
  113.7 14.9 %collective-permute-start.14 = (bf16[128,2048]{1,0:T(8,128)(2,1)S(1)}, bf16[128,2048]{1,0:T(8,128)(2,1)S(1)}, u32[]{:S(2)}, u32[]{:S(2)}) collective-permute-start(bf16[128,2048]{1,0:T(8,128)(2,1)S(1)} %fusion.9), channel_id=1, source_target_pairs={{0,16},{16,0},{1,17},{17,1},{2,18},{18,2},{3,19},{19,3},{4,20},{20... | collective-permute-start | bytes 1572872 | tf_op jit(solution)/shard_map/ppermute | solution.py:153
  115.8 23.3 %copy-start.24 = (bf16[1,128,4096]{2,1,0:T(8,128)(2,1)S(1)}, bf16[1,128,4096]{2,1,0:T(8,128)(2,1)}, u32[]{:S(2)}) copy-start(bf16[1,128,4096]{2,1,0:T(8,128)(2,1)} %param.14) | copy-start | bytes 3145732
  115.9 23.0 %collective-permute-start.12 = (bf16[128,2048]{1,0:T(8,128)(2,1)S(1)}, bf16[128,2048]{1,0:T(8,128)(2,1)S(1)}, u32[]{:S(2)}, u32[]{:S(2)}) collective-permute-start(bf16[128,2048]{1,0:T(8,128)(2,1)S(1)} %fusion.8), channel_id=1, source_target_pairs={{0,16},{16,0},{1,17},{17,1},{2,18},{18,2},{3,19},{19,3},{4,20},{20... | collective-permute-start | bytes 1572872 | tf_op jit(solution)/shard_map/ppermute | solution.py:153
  142.9 32.5 %all-to-all-start.1 = ((bf16[8,32,4096]{2,1,0:T(8,128)(2,1)}), bf16[8,32,4096]{2,1,0:T(8,128)(2,1)S(1)}, u32[]{:S(2)}, u32[]{:S(2)}) async-start(bf16[8,32,4096]{2,1,0:T(8,128)(2,1)} %bitcast.37), calls=%async_computation.1 | async-start | bytes 4194304 | tf_op jit(solution)/shard_map/all_to_all | solution.py:278
  146.6 25.8 %collective-permute-start.22 = (bf16[128,4096]{1,0:T(8,128)(2,1)}, bf16[128,4096]{1,0:T(8,128)(2,1)S(1)}, u32[]{:S(2)}, u32[]{:S(2)}) collective-permute-start(bf16[128,4096]{1,0:T(8,128)(2,1)} %copy-done.8), channel_id=1, source_target_pairs={{0,2},{2,0},{4,6},{6,4},{1,3},{3,1},{5,7},{7,5},{8,10},{10,8},{12,... | collective-permute-start | bytes 3145736 | tf_op jit(solution)/shard_map/ppermute | solution.py:157
  146.8 33.0 %collective-permute-start.20 = (bf16[128,4096]{1,0:T(8,128)(2,1)}, bf16[128,4096]{1,0:T(8,128)(2,1)}, u32[]{:S(2)}, u32[]{:S(2)}) collective-permute-start(bf16[128,4096]{1,0:T(8,128)(2,1)} %copy-done.8), channel_id=1, source_target_pairs={{2,4},{4,2},{3,5},{5,3},{10,12},{12,10},{11,13},{13,11},{18,20},{2... | collective-permute-start | bytes 3145736 | tf_op jit(solution)/shard_map/ppermute | solution.py:157
  175.4 35.1 %all-to-all-start.2 = ((bf16[8,32,4096]{2,1,0:T(8,128)(2,1)}), bf16[8,32,4096]{2,1,0:T(8,128)(2,1)}, u32[]{:S(2)}, u32[]{:S(2)}) async-start(bf16[8,32,4096]{2,1,0:T(8,128)(2,1)} %bitcast.39), calls=%async_computation.2 | async-start | bytes 4194304 | tf_op jit(solution)/shard_map/all_to_all | solution.py:278
  179.8 27.6 %collective-permute-start.21 = (bf16[128,4096]{1,0:T(8,128)(2,1)}, bf16[128,4096]{1,0:T(8,128)(2,1)}, u32[]{:S(2)}, u32[]{:S(2)}) collective-permute-start(bf16[128,4096]{1,0:T(8,128)(2,1)} %collective-permute-done.20.refs_0_), channel_id=1, source_target_pairs={{2,0},{4,6},{3,1},{5,7},{10,8},{12,14},{11,9},{13,15},{18,16},{20,... | collective-permute-start | bytes 3145736 | tf_op jit(solution)/shard_map/ppermute | solution.py:157
  181.1 29.4 %collective-permute-start.23 = (bf16[128,4096]{1,0:T(8,128)(2,1)}, bf16[128,4096]{1,0:T(8,128)(2,1)}, u32[]{:S(2)}, u32[]{:S(2)}) collective-permute-start(bf16[128,4096]{1,0:T(8,128)(2,1)} %copy-done.11), channel_id=1, source_target_pairs={{2,4},{4,2},{3,5},{5,3},{10,12},{12,10},{11,13},{13,11},{18,20},{2... | collective-permute-start | bytes 3145736 | tf_op jit(solution)/shard_map/ppermute | solution.py:157
  210.5 34.8 %all-to-all-start.3 = ((bf16[8,32,4096]{2,1,0:T(8,128)(2,1)}), bf16[8,32,4096]{2,1,0:T(8,128)(2,1)}, u32[]{:S(2)}, u32[]{:S(2)}) async-start(bf16[8,32,4096]{2,1,0:T(8,128)(2,1)} %bitcast.48), calls=%async_computation.3 | async-start | bytes 4194304 | tf_op jit(solution)/shard_map/all_to_all | solution.py:278
  214.9 27.5 %collective-permute-start.24 = (bf16[128,4096]{1,0:T(8,128)(2,1)}, bf16[128,4096]{1,0:T(8,128)(2,1)S(1)}, u32[]{:S(2)}, u32[]{:S(2)}) collective-permute-start(bf16[128,4096]{1,0:T(8,128)(2,1)} %collective-permute-done.23.refs_0_), channel_id=1, source_target_pairs={{2,0},{4,6},{3,1},{5,7},{10,8},{12,14},{11,9},{13,15},{18,16},{20,... | collective-permute-start | bytes 3145736 | tf_op jit(solution)/shard_map/ppermute | solution.py:157
  245.3 30.0 %all-to-all-start.4 = ((bf16[8,32,4096]{2,1,0:T(8,128)(2,1)}), bf16[8,32,4096]{2,1,0:T(8,128)(2,1)S(1)}, u32[]{:S(2)}, u32[]{:S(2)}) async-start(bf16[8,32,4096]{2,1,0:T(8,128)(2,1)} %bitcast.50), calls=%async_computation.4 | async-start | bytes 4194304 | tf_op jit(solution)/shard_map/all_to_all | solution.py:278
  288.8 29.7 %all-to-all-start.5 = ((bf16[8,32,4096]{2,1,0:T(8,128)(2,1)}), bf16[8,32,4096]{2,1,0:T(8,128)(2,1)S(1)}, u32[]{:S(2)}, u32[]{:S(2)}) async-start(bf16[8,32,4096]{2,1,0:T(8,128)(2,1)} %bitcast.113), calls=%async_computation.5 | async-start | bytes 4194304 | tf_op jit(solution)/shard_map/all_to_all | solution.py:278
  320.7 31.1 %all-to-all-start.6 = ((bf16[8,32,4096]{2,1,0:T(8,128)(2,1)}), bf16[8,32,4096]{2,1,0:T(8,128)(2,1)S(1)}, u32[]{:S(2)}, u32[]{:S(2)}) async-start(bf16[8,32,4096]{2,1,0:T(8,128)(2,1)} %bitcast.111), calls=%async_computation.6 | async-start | bytes 4194304 | tf_op jit(solution)/shard_map/all_to_all | solution.py:278
  324.3 26.5 %collective-permute-start.25 = (bf16[128,4096]{1,0:T(8,128)(2,1)}, bf16[128,4096]{1,0:T(8,128)(2,1)S(1)}, u32[]{:S(2)}, u32[]{:S(2)}) collective-permute-start(bf16[128,4096]{1,0:T(8,128)(2,1)} %copy-done.12), channel_id=1, source_target_pairs={{0,2},{6,4},{1,3},{7,5},{8,10},{14,12},{9,11},{15,13},{16,18},{22,... | collective-permute-start | bytes 3145736 | tf_op jit(solution)/shard_map/ppermute | solution.py:157
  351.7 34.9 %all-to-all-start.7 = ((bf16[8,32,4096]{2,1,0:T(8,128)(2,1)}), bf16[8,32,4096]{2,1,0:T(8,128)(2,1)}, u32[]{:S(2)}, u32[]{:S(2)}) async-start(bf16[8,32,4096]{2,1,0:T(8,128)(2,1)} %bitcast.115), calls=%async_computation.7 | async-start | bytes 4194304 | tf_op jit(solution)/shard_map/all_to_all | solution.py:278
  357.2 27.2 %collective-permute-start.26 = (bf16[128,4096]{1,0:T(8,128)(2,1)S(1)}, bf16[128,4096]{1,0:T(8,128)(2,1)S(1)}, u32[]{:S(2)}, u32[]{:S(2)}) collective-permute-start(bf16[128,4096]{1,0:T(8,128)(2,1)S(1)} %combine.7), channel_id=1, source_target_pairs={{0,2},{6,4},{1,3},{7,5},{8,10},{14,12},{9,11},{15,13},{16,18},{22,... | collective-permute-start | bytes 3145736 | tf_op jit(solution)/shard_map/ppermute | solution.py:157
  364.0 21.5 %collective-permute-start.27 = (bf16[128,4096]{1,0:T(8,128)(2,1)S(1)}, bf16[128,4096]{1,0:T(8,128)(2,1)S(1)}, u32[]{:S(2)}, u32[]{:S(2)}) collective-permute-start(bf16[128,4096]{1,0:T(8,128)(2,1)S(1)} %combine.8), channel_id=1, source_target_pairs={{2,4},{4,2},{3,5},{5,3},{10,12},{12,10},{11,13},{13,11},{18,20},{2... | collective-permute-start | bytes 3145736 | tf_op jit(solution)/shard_map/ppermute | solution.py:157
  386.6 41.0 %all-to-all-start.8 = ((bf16[8,32,4096]{2,1,0:T(8,128)(2,1)}), bf16[8,32,4096]{2,1,0:T(8,128)(2,1)}, u32[]{:S(2)}, u32[]{:S(2)}) async-start(bf16[8,32,4096]{2,1,0:T(8,128)(2,1)} %bitcast.114), calls=%async_computation.8 | async-start | bytes 4194304 | tf_op jit(solution)/shard_map/all_to_all | solution.py:278
  392.3 11.9 %copy-start.21 = (f32[128,2048]{1,0:T(8,128)S(1)}, f32[128,2048]{1,0:T(8,128)}, u32[]{:S(2)}) copy-start(f32[128,2048]{1,0:T(8,128)} %copy-done.20) | copy-start | bytes 3145732
  392.3 11.9 %copy-start.23 = (f32[128,2048]{1,0:T(8,128)S(1)}, f32[128,2048]{1,0:T(8,128)}, u32[]{:S(2)}) copy-start(f32[128,2048]{1,0:T(8,128)} %copy-done.22) | copy-start | bytes 3145732
  392.3 11.9 %copy-start.25 = (bf16[1,128,4096]{2,1,0:T(8,128)(2,1)S(1)}, bf16[1,128,4096]{2,1,0:T(8,128)(2,1)}, u32[]{:S(2)}) copy-start(bf16[1,128,4096]{2,1,0:T(8,128)(2,1)} %param.14) | copy-start | bytes 3145732
  393.5 11.9 %collective-permute-start.28 = (bf16[128,4096]{1,0:T(8,128)(2,1)S(1)}, bf16[128,4096]{1,0:T(8,128)(2,1)S(1)}, u32[]{:S(2)}, u32[]{:S(2)}) collective-permute-start(bf16[128,4096]{1,0:T(8,128)(2,1)S(1)} %combine.9), channel_id=1, source_target_pairs={{2,4},{4,2},{3,5},{5,3},{10,12},{12,10},{11,13},{13,11},{18,20},{2... | collective-permute-start | bytes 3145736 | tf_op jit(solution)/shard_map/ppermute | solution.py:157
  396.6 31.0 %collective-permute-start.29 = (bf16[128,4096]{1,0:T(8,128)(2,1)S(1)}, bf16[128,4096]{1,0:T(8,128)(2,1)S(1)}, u32[]{:S(2)}, u32[]{:S(2)}) collective-permute-start(bf16[128,4096]{1,0:T(8,128)(2,1)S(1)} %combine.10), channel_id=1, source_target_pairs={{0,2},{2,0},{4,6},{6,4},{1,3},{3,1},{5,7},{7,5},{8,10},{10,8},{12,... | collective-permute-start | bytes 3145736 | tf_op jit(solution)/shard_map/ppermute | solution.py:157
  (26 other events, 94.4 us)

commit v3 on v2

--- a/solution.py
+++ b/solution.py
@@ -16,6 +16,7 @@
 AXES = ("y", "c", "z", "x")
 PLANE = ("y", "c", "x")
 BF = jnp.bfloat16
+COST = 30 * 10**9
 VMEM = 20 * 2**20
 F32 = jnp.float32
 
@@ -335,7 +336,7 @@
             pltpu.VMEM((total, hidden), F32),
             pltpu.VMEM((total, hidden), BF),
         ],
-        compiler_params=pltpu.CompilerParams(vmem_limit_bytes=30 * 2**20),
+        compiler_params=pltpu.CompilerParams(vmem_limit_bytes=58 * 2**20),
         cost_estimate=pl.CostEstimate(
             flops=total, bytes_accessed=total, transcendentals=0
         ),
@@ -379,7 +380,7 @@
         ],
         out_specs=pl.BlockSpec((count, D), lambda j: (0, 0)),
         scratch_shapes=[pltpu.VMEM((count, D), F32)],
-        compiler_params=pltpu.CompilerParams(vmem_limit_bytes=40 * 2**20),
+        compiler_params=pltpu.CompilerParams(vmem_limit_bytes=58 * 2**20),
         cost_estimate=pl.CostEstimate(
             flops=6 * count * D * hidden,
             bytes_accessed=6 * D * hidden + 4 * count * D,
@@ -430,7 +431,7 @@
     out_ref[...] = jnp.dot(place_ref[...], block, preferred_element_type=F32).astype(BF)
 
 
-def slots_of(place, *blocks):
+def slots_of(place, *blocks, cost=None):
     slots, tokens = place.shape
     tile = D // 2
     return pl.pallas_call(
@@ -441,7 +442,9 @@
         + [pl.BlockSpec((tokens, tile), lambda j: (0, j))] * len(blocks),
         out_specs=pl.BlockSpec((slots, tile), lambda j: (0, j)),
         compiler_params=pltpu.CompilerParams(vmem_limit_bytes=VMEM),
-        cost_estimate=pl.CostEstimate(flops=slots, bytes_accessed=slots, transcendentals=0),
+        cost_estimate=pl.CostEstimate(
+            flops=cost or slots, bytes_accessed=slots, transcendentals=0
+        ),
         name="slots",
     )(place, *blocks)
 
@@ -497,18 +500,24 @@
     parts = 2
     width = D // parts
     columns = [slice(part * width, (part + 1) * width) for part in range(parts)]
-    far_out, middle_x, last_in = together(
-        along(far_in, OUTWARD), swap(middle, "x"), along(near_x[:, columns[1]], INNER)
+    first = jnp.concatenate([own, near, middle, across, near_x], axis=0)
+    early_heads = jnp.concatenate([in_order[:, : 3 * HD], in_order[:, 4 * HD : 6 * HD]], axis=1)
+    late_heads = jnp.concatenate([in_order[:, 3 * HD : 4 * HD], in_order[:, 6 * HD :]], axis=1)
+    early = [
+        jnp.dot(early_heads, first[:, at], preferred_element_type=F32) for at in columns
+    ]
+    far_out, middle_x, last_in, *early = together(
+        along(far_in, OUTWARD), swap(middle, "x"), along(near_x[:, columns[1]], INNER), *early
     )
     places, shares = routing(ids, gates, z, inner)
     far = jnp.where(inner, far_in, far_out)
-    line = [own, near, middle, far, across, near_x, middle_x]
+    late = [far, middle_x]
     last, last_out = together(swap(far[:, columns[0]], "x"), along(last_in, OUTWARD))
     last = [last, jnp.where(inner, last_in, last_out)]
     projected = []
     for part in range(parts):
-        weight = jnp.concatenate([block[:, columns[part]] for block in line] + [last[part]], axis=0)
-        partial = jnp.dot(in_order, weight, preferred_element_type=F32)
+        weight = jnp.concatenate([block[:, columns[part]] for block in late] + [last[part]], axis=0)
+        partial = early[part] + jnp.dot(late_heads, weight, preferred_element_type=F32)
         partial = partial.reshape(2, 2, tokens, width)
         other = lax.dynamic_index_in_dim(partial, 1 - c, 1, keepdims=False).astype(BF)
         both = lax.dynamic_index_in_dim(partial, c, 1, keepdims=False) + swap(other, "c").astype(F32)
@@ -529,17 +538,17 @@
 
     near, middle_in = along(normed, OUTER), along(normed, INNER)
     own_rows = plane_exchange(slots_of(places[0], normed))
-    near_slots, own_rows = together(slots_of(places[1], near), own_rows)
+    near_slots, own_rows = together(slots_of(places[1], near, cost=COST), own_rows)
     near_rows = plane_exchange(near_slots)
     middle_out, far_in = along(middle_in, OUTWARD), along(near, INNER)
     middle_slots, near_rows, far_in, shares = together(
-        slots_of(places[2], middle_in, middle_out), near_rows, far_in, shares
+        slots_of(places[2], middle_in, middle_out, cost=COST), near_rows, far_in, shares
     )
     middle_rows = plane_exchange(middle_slots)
     far_out = along(far_in, OUTWARD)
     own_out, near_out = experts((own_rows, near_rows), *weights)
     far_slots, middle_rows, own_out, near_out = together(
-        slots_of(places[3], far_in, far_out), middle_rows, own_out, near_out
+        slots_of(places[3], far_in, far_out, cost=COST), middle_rows, own_out, near_out
     )
     far_rows = plane_exchange(far_slots)
     middle_out = expert(middle_rows, *weights)
@@ -551,14 +560,16 @@
     middle_out, far, far_sum = together(middle_out, far, far_sum)
     middle = plane_exchange(middle_out)
     outer_far = along(far_sum, INWARD)
-    near_out, middle, outer_far = together(near_out, middle, outer_far)
+    inner_sum = combine(shares[3], far, outer_far)
+    near_out, middle, inner_sum = together(near_out, middle, inner_sum)
     near = plane_exchange(near_out)
+    inner_far = along(inner_sum, INNER)
     outer_middle = along(combine(shares[2], middle), INWARD)
-    inner_far = along(combine(shares[3], far, outer_far), INNER)
-    own_out, near, outer_middle, inner_far = together(own_out, near, outer_middle, inner_far)
+    near_sum = combine(shares[1], near, inner_far)
+    own_out, near_sum = together(own_out, near_sum)
     own = plane_exchange(own_out)
     inner_middle = along(combine(shares[2], middle, outer_middle), INNER)
-    all_near = along(combine(shares[1], near, inner_far), OUTER)
+    all_near = along(near_sum, OUTER)
     layer_output = combine(
         shares[0], own, after_attention, inner_middle, all_near
     )

time: 433 us -> 424 us (0.979)
  local copies, waits for them, and re-layouts: 55 us -> 33.1 us
  Pallas kernels: 65.6 us -> 76.3 us
    ppermute x22, waiting for transfers between devices: 141 us -> 97.5 us  [along(): return lax.ppermute(value, 'z', pairs)]
    all_to_all x8, waiting for transfers between devices: 36.4 us -> 79.4 us  [plane_exchange(): lax.all_to_all(blocks, PLANE, split_axis=0, concat_axis=0, tiled=True)]
    unnamed x93 -> x76, local copies, waits for them, and re-layouts: 41.1 us -> 22.5 us
    pallas_call x2, Pallas kernels: 19.2 us -> 25.6 us  [expert(): pl.pallas_call(expert_kernel, grid=(hidden // tile,), out_shape=jax.Shape...]
    dot_general x2 -> x4, matrix products: 9.04 us -> 9.58 us  [the longest x2 7.07 us: tuned_device(): jnp.dot(early_heads, first[:, at], preferred_element_type=F32)]
  transfers between devices with their start and end apart: 39 -> 39, of which waited for: 18 -> 22; matrix products, arithmetic and copies ran while one was open for 9% -> 9% of each run, Pallas kernels for 12% -> 14%
where the time goes in v3:
time: 424 us; the launch traced here: 422 us
  waiting for transfers between devices  202 us (48%)
  starting transfers between devices  85.8 us (20%)
  Pallas kernels  76.3 us (18%)
  local copies, waits for them, and re-layouts  33.1 us (8%)
  other arithmetic  11.1 us (3%)
  matrix products  9.72 us (2%)
    ppermute x22, waiting for transfers between devices, along(): return lax.ppermute(value, 'z', pairs)  97.5 us
    all_to_all x8, waiting for transfers between devices, plane_exchange(): lax.all_to_all(blocks, PLANE, split_axis=0, concat_axis=0, tiled=True)  79.4 us
    ppermute x22, starting transfers between devices, along(): return lax.ppermute(value, 'z', pairs)  40.4 us
    all_to_all x8, starting transfers between devices, plane_exchange(): lax.all_to_all(blocks, PLANE, split_axis=0, concat_axis=0, tiled=True)  32.9 us
    pallas_call x2, Pallas kernels, expert(): pl.pallas_call(expert_kernel, grid=(hidden // tile,), out_shape=jax.Shape...  25.6 us
    ppermute x8, waiting for transfers between devices, swap(): return lax.ppermute(value, axis, [(0, 1), (1, 0)])  24.2 us
    unnamed x76, local copies, waits for them, and re-layouts  22.5 us
    pallas_call x1, Pallas kernels, experts(): pl.pallas_call(functools.partial(experts_kernel, blocks=len(blocks), step...  18.4 us
  transfers between devices with their start and end apart: 39, of which 22 were waited for; matrix products, arithmetic and copies ran while one was open for 9% of the time, Pallas kernels for 14%

profile of v3, /device:TPU:0, one launch (start us, length us, event | category | flops | bytes accessed | tf_op | source)
XLA Modules:
  0.0 422.0 jit_solution(12745388418688071621)
XLA Ops:
  0.6 3.1 collective-permute-start
  13.2 3.6 all-to-all-start
  20.8 2.3 constant_dynamic-update-slice_fusion.4
  23.1 4.1 collective-permute-done
  27.2 2.2 collective-permute-done.2
  33.9 2.3 constant_dynamic-update-slice_fusion.3
  36.8 10.7 %attention.1 = bf16[512,1024]{1,0:T(8,128)(2,1)S(1)} custom-call(bf16[4,128,1536]{2,1,0:T(8,128)(2,1)S(1)} %all-to-all-done.message_ref), custom_call_target="tpu_custom_call" | custom-call | flops 1744830464 | bytes 2621440 | tf_op jit(solution)/shard_map/attention/pallas_call | solution.py:230
  47.9 13.2 %collective-permute-done.3 = bf16[128,4096]{1,0:T(8,128)(2,1)} collective-permute-done((bf16[128,4096]{1,0:T(8,128)(2,1)}, bf16[128,4096]{1,0:T(8,128)(2,1)}, u32[]{:S(2)}, u32[]{:S(2)}) %collective-permute-start.3) | collective-permute-done | bytes 1048608 | tf_op jit(solution)/shard_map/ppermute | solution.py:158
  63.2 2.5 constant_dynamic-update-slice_fusion.2
  67.0 2.3 constant_dynamic-update-slice_fusion.1
  70.4 3.5 fusion.2
  75.9 3.5 fusion
  80.8 6.6 %collective-permute-done.17 = s32[128,8]{0,1:T(8,128)S(1)} collective-permute-done((s32[128,8]{0,1:T(8,128)S(1)}, s32[128,8]{0,1:T(8,128)S(1)}, u32[]{:S(2)}, u32[]{:S(2)}) %collective-permute-start.17) | collective-permute-done | bytes 4128 | tf_op jit(solution)/shard_map/ppermute | solution.py:158
  92.9 6.7 %collective-permute-done.9 = bf16[128,2048]{1,0:T(8,128)(2,1)S(1)} collective-permute-done((bf16[128,2048]{1,0:T(8,128)(2,1)S(1)}, bf16[128,2048]{1,0:T(8,128)(2,1)S(1)}, u32[]{:S(2)}, u32[]{:S(2)}) %collective-permute-start.9) | collective-permute-done | bytes 524320 | tf_op jit(solution)/shard_map/ppermute | solution.py:154
  99.5 2.8 collective-permute-done.10
  117.7 5.9 %collective-permute-done.14 = bf16[128,2048]{1,0:T(8,128)(2,1)} collective-permute-done((bf16[128,2048]{1,0:T(8,128)(2,1)S(1)}, bf16[128,2048]{1,0:T(8,128)(2,1)}, u32[]{:S(2)}, u32[]{:S(2)}) %collective-permute-start.14) | collective-permute-done | bytes 524320 | tf_op jit(solution)/shard_map/ppermute | solution.py:154
  124.7 9.1 %collective-permute-done.12 = bf16[128,2048]{1,0:T(8,128)(2,1)} collective-permute-done((bf16[128,2048]{1,0:T(8,128)(2,1)}, bf16[128,2048]{1,0:T(8,128)(2,1)}, u32[]{:S(2)}, u32[]{:S(2)}) %collective-permute-start.12) | collective-permute-done | bytes 524320 | tf_op jit(solution)/shard_map/ppermute | solution.py:154
  137.1 2.3 collective-permute-start.22
  142.6 4.4 %all-to-all-start.1 = ((bf16[8,32,4096]{2,1,0:T(8,128)(2,1)}), bf16[8,32,4096]{2,1,0:T(8,128)(2,1)}, u32[]{:S(2)}, u32[]{:S(2)}) async-start(bf16[8,32,4096]{2,1,0:T(8,128)(2,1)} %bitcast.37), calls=%async_computation.1 | async-start | bytes 4194304 | tf_op jit(solution)/shard_map/all_to_all | solution.py:279
  148.3 13.4 %collective-permute-done.22.refs_0_ = bf16[128,4096]{1,0:T(8,128)(2,1)} collective-permute-done((bf16[128,4096]{1,0:T(8,128)(2,1)S(1)}, bf16[128,4096]{1,0:T(8,128)(2,1)}, u32[]{:S(2)}, u32[]{:S(2)}) %collective-permute-start.22) | collective-permute-done | bytes 1048608 | tf_op jit(solution)/shard_map/ppermute | solution.py:158
  162.4 2.9 slots.5
  165.3 7.8 %all-to-all-done.1 = bf16[8,32,4096]{2,1,0:T(8,128)(2,1)} async-done(((bf16[8,32,4096]{2,1,0:T(8,128)(2,1)}), bf16[8,32,4096]{2,1,0:T(8,128)(2,1)}, u32[]{:S(2)}, u32[]{:S(2)}) %all-to-all-start.1) | async-done | bytes 2097184 | tf_op jit(solution)/shard_map/all_to_all | solution.py:279
  173.1 4.3 %all-to-all-start.2 = ((bf16[8,32,4096]{2,1,0:T(8,128)(2,1)}), bf16[8,32,4096]{2,1,0:T(8,128)(2,1)}, u32[]{:S(2)}, u32[]{:S(2)}) async-start(bf16[8,32,4096]{2,1,0:T(8,128)(2,1)} %bitcast.39), calls=%async_computation.2 | async-start | bytes 4194304 | tf_op jit(solution)/shard_map/all_to_all | solution.py:279
  177.5 7.6 %collective-permute-done.21.refs_1_ = bf16[128,4096]{1,0:T(8,128)(2,1)} collective-permute-done((bf16[128,4096]{1,0:T(8,128)(2,1)S(1)}, bf16[128,4096]{1,0:T(8,128)(2,1)}, u32[]{:S(2)}, u32[]{:S(2)}) %collective-permute-start.21) | collective-permute-done | bytes 1048608 | tf_op jit(solution)/shard_map/ppermute | solution.py:158
  185.1 3.0 slots.4
  188.1 15.6 %all-to-all-done.2 = bf16[8,32,4096]{2,1,0:T(8,128)(2,1)} async-done(((bf16[8,32,4096]{2,1,0:T(8,128)(2,1)}), bf16[8,32,4096]{2,1,0:T(8,128)(2,1)}, u32[]{:S(2)}, u32[]{:S(2)}) %all-to-all-start.2) | async-done | bytes 2097184 | tf_op jit(solution)/shard_map/all_to_all | solution.py:279
  204.9 4.6 %all-to-all-start.3 = ((bf16[8,32,4096]{2,1,0:T(8,128)(2,1)}), bf16[8,32,4096]{2,1,0:T(8,128)(2,1)}, u32[]{:S(2)}, u32[]{:S(2)}) async-start(bf16[8,32,4096]{2,1,0:T(8,128)(2,1)} %bitcast.48), calls=%async_computation.3 | async-start | bytes 4194304 | tf_op jit(solution)/shard_map/all_to_all | solution.py:279
  209.5 18.4 %experts.1 = (bf16[256,4096]{1,0:T(8,128)(2,1)}, bf16[256,4096]{1,0:T(8,128)(2,1)}) custom-call(bf16[256,4096]{1,0:T(8,128)(2,1)} %bitcast.38.refs_0_, bf16[256,4096]{1,0:T(8,128)(2,1)} %bitcast.40.refs_1_, bf16[1,4096,768]{2,1,0:T(8,128)(2,1)} %gate_ref.3, bf16[1,4096,768]{2,1,0:T(8,128)(2,1)} %up_ref.3, bf16[1,768,4096]{2,1,0:T(8,128)(2,1)} %down_ref.3), custom_call_target="tpu_custom_call" | custom-call | flops 512 | bytes 512 | tf_op jit(solution)/shard_map/experts/pallas_call | solution.py:328
  227.9 2.3 collective-permute-done.24.refs_1_
  232.4 3.1 all-to-all-done.3
  235.5 3.6 all-to-all-start.4
  239.1 12.8 %expert.2 = bf16[256,4096]{1,0:T(8,128)(2,1)} custom-call(bf16[256,4096]{1,0:T(8,128)(2,1)} %bitcast.49.rows_ref, bf16[1,4096,768]{2,1,0:T(8,128)(2,1)} %gate_ref.3, bf16[1,4096,768]{2,1,0:T(8,128)(2,1)} %up_ref.3, bf16[1,768,4096]{2,1,0:T(8,128)(2,1)} %down_ref.3), custom_call_target="tpu_custom_call" | custom-call | flops 4831838208 | bytes 23068672 | tf_op jit(solution)/shard_map/expert/pallas_call | solution.py:371
  251.9 13.3 %all-to-all-done.4 = bf16[8,32,4096]{2,1,0:T(8,128)(2,1)S(1)} async-done(((bf16[8,32,4096]{2,1,0:T(8,128)(2,1)}), bf16[8,32,4096]{2,1,0:T(8,128)(2,1)S(1)}, u32[]{:S(2)}, u32[]{:S(2)}) %all-to-all-start.4) | async-done | bytes 2097184 | tf_op jit(solution)/shard_map/all_to_all | solution.py:279
  266.5 12.8 %expert.3 = bf16[256,4096]{1,0:T(8,128)(2,1)} custom-call(bf16[256,4096]{1,0:T(8,128)(2,1)} %bitcast.119, bf16[1,4096,768]{2,1,0:T(8,128)(2,1)} %gate_ref.3, bf16[1,4096,768]{2,1,0:T(8,128)(2,1)} %up_ref.3, bf16[1,768,4096]{2,1,0:T(8,128)(2,1)} %down_ref.3), custom_call_target="tpu_custom_call" | custom-call | flops 4831838208 | bytes 23068672 | tf_op jit(solution)/shard_map/expert/pallas_call | solution.py:371
  279.3 3.6 all-to-all-start.5
  284.7 24.3 %all-to-all-done.5 = bf16[8,32,4096]{2,1,0:T(8,128)(2,1)S(1)} async-done(((bf16[8,32,4096]{2,1,0:T(8,128)(2,1)}), bf16[8,32,4096]{2,1,0:T(8,128)(2,1)S(1)}, u32[]{:S(2)}, u32[]{:S(2)}) %all-to-all-start.5) | async-done | bytes 2097184 | tf_op jit(solution)/shard_map/all_to_all | solution.py:279
  311.1 3.6 all-to-all-start.6
  314.7 4.7 %collective-permute-start.25 = (bf16[128,4096]{1,0:T(8,128)(2,1)}, bf16[128,4096]{1,0:T(8,128)(2,1)S(1)}, u32[]{:S(2)}, u32[]{:S(2)}) collective-permute-start(bf16[128,4096]{1,0:T(8,128)(2,1)} %copy-done.2), channel_id=1, source_target_pairs={{0,2},{6,4},{1,3},{7,5},{8,10},{14,12},{9,11},{15,13},{16,18},{22,... | collective-permute-start | bytes 3145736 | tf_op jit(solution)/shard_map/ppermute | solution.py:158
  319.4 23.2 %collective-permute-done.25.refs_0_ = bf16[128,4096]{1,0:T(8,128)(2,1)S(1)} collective-permute-done((bf16[128,4096]{1,0:T(8,128)(2,1)}, bf16[128,4096]{1,0:T(8,128)(2,1)S(1)}, u32[]{:S(2)}, u32[]{:S(2)}) %collective-permute-start.25) | collective-permute-done | bytes 1048608 | tf_op jit(solution)/shard_map/ppermute | solution.py:158
  346.5 4.4 %all-to-all-start.7 = ((bf16[8,32,4096]{2,1,0:T(8,128)(2,1)}), bf16[8,32,4096]{2,1,0:T(8,128)(2,1)}, u32[]{:S(2)}, u32[]{:S(2)}) async-start(bf16[8,32,4096]{2,1,0:T(8,128)(2,1)} %bitcast.123), calls=%async_computation.7 | async-start | bytes 4194304 | tf_op jit(solution)/shard_map/all_to_all | solution.py:279
  353.6 7.1 %collective-permute-start.27 = (bf16[128,4096]{1,0:T(8,128)(2,1)}, bf16[128,4096]{1,0:T(8,128)(2,1)}, u32[]{:S(2)}, u32[]{:S(2)}) collective-permute-start(bf16[128,4096]{1,0:T(8,128)(2,1)} %combine.9), channel_id=1, source_target_pairs={{0,2},{6,4},{1,3},{7,5},{8,10},{14,12},{9,11},{15,13},{16,18},{22,... | collective-permute-start | bytes 3145736 | tf_op jit(solution)/shard_map/ppermute | solution.py:158
  361.7 15.3 %all-to-all-done.7 = bf16[8,32,4096]{2,1,0:T(8,128)(2,1)} async-done(((bf16[8,32,4096]{2,1,0:T(8,128)(2,1)}), bf16[8,32,4096]{2,1,0:T(8,128)(2,1)}, u32[]{:S(2)}, u32[]{:S(2)}) %all-to-all-start.7) | async-done | bytes 2097184 | tf_op jit(solution)/shard_map/all_to_all | solution.py:279
  378.2 2.2 combine.8
  381.5 4.4 %all-to-all-start.8 = ((bf16[8,32,4096]{2,1,0:T(8,128)(2,1)}), bf16[8,32,4096]{2,1,0:T(8,128)(2,1)}, u32[]{:S(2)}, u32[]{:S(2)}) async-start(bf16[8,32,4096]{2,1,0:T(8,128)(2,1)} %bitcast.122), calls=%async_computation.8 | async-start | bytes 4194304 | tf_op jit(solution)/shard_map/all_to_all | solution.py:279
  385.9 2.2 combine.10
  388.9 6.7 %collective-permute-start.29 = (bf16[128,4096]{1,0:T(8,128)(2,1)S(1)}, bf16[128,4096]{1,0:T(8,128)(2,1)S(1)}, u32[]{:S(2)}, u32[]{:S(2)}) collective-permute-start(bf16[128,4096]{1,0:T(8,128)(2,1)S(1)} %copy-done.4), channel_id=1, source_target_pairs={{0,2},{2,0},{4,6},{6,4},{1,3},{3,1},{5,7},{7,5},{8,10},{10,8},{12,... | collective-permute-start | bytes 3145736 | tf_op jit(solution)/shard_map/ppermute | solution.py:158
  396.8 22.2 %collective-permute-done.29.refs_2_ = bf16[128,4096]{1,0:T(8,128)(2,1)S(1)} collective-permute-done((bf16[128,4096]{1,0:T(8,128)(2,1)S(1)}, bf16[128,4096]{1,0:T(8,128)(2,1)S(1)}, u32[]{:S(2)}, u32[]{:S(2)}) %collective-permute-start.29) | collective-permute-done | bytes 1048608 | tf_op jit(solution)/shard_map/ppermute | solution.py:158
  419.0 3.1 combine.11
  (181 shorter events, 74.4 us)
Async XLA Ops:
  0.6 26.6 %collective-permute-start = (bf16[128,4096]{1,0:T(8,128)(2,1)}, bf16[128,4096]{1,0:T(8,128)(2,1)}, u32[]{:S(2)}, u32[]{:S(2)}) collective-permute-start(bf16[128,4096]{1,0:T(8,128)(2,1)} %param.20), channel_id=1, source_target_pairs={{0,2},{2,0},{4,6},{6,4},{1,3},{3,1},{5,7},{7,5},{8,10},{10,8},{12,... | collective-permute-start | bytes 3145736 | tf_op jit(solution)/shard_map/ppermute | solution.py:158
  3.7 23.5 %collective-permute-start.1 = (bf16[128,4096]{1,0:T(8,128)(2,1)}, bf16[128,4096]{1,0:T(8,128)(2,1)S(1)}, u32[]{:S(2)}, u32[]{:S(2)}) collective-permute-start(bf16[128,4096]{1,0:T(8,128)(2,1)} %param.20), channel_id=1, source_target_pairs={{2,4},{4,2},{3,5},{5,3},{10,12},{12,10},{11,13},{13,11},{18,20},{2... | collective-permute-start | bytes 3145736 | tf_op jit(solution)/shard_map/ppermute | solution.py:158
  4.4 25.0 %collective-permute-start.2 = (bf16[128,4096]{1,0:T(8,128)(2,1)}, bf16[128,4096]{1,0:T(8,128)(2,1)}, u32[]{:S(2)}, u32[]{:S(2)}) collective-permute-start(bf16[128,4096]{1,0:T(8,128)(2,1)} %param.20), channel_id=1, source_target_pairs={{0,1},{1,0},{2,3},{3,2},{4,5},{5,4},{6,7},{7,6},{8,9},{9,8},{10,11... | collective-permute-start | bytes 3145736 | tf_op jit(solution)/shard_map/ppermute | solution.py:154
  13.2 23.6 %all-to-all-start = ((bf16[4,128,1536]{2,1,0:T(8,128)(2,1)}), bf16[4,128,1536]{2,1,0:T(8,128)(2,1)S(1)}, u32[]{:S(2)}, u32[]{:S(2)}) async-start(bf16[4,128,1536]{2,1,0:T(8,128)(2,1)} %bitcast_dynamic-update-slice_fusion.1), calls=%async_computation | async-start | bytes 3145728 | tf_op jit(solution)/shard_map/all_to_all | solution.py:483
  29.4 31.7 %collective-permute-start.4 = (bf16[128,4096]{1,0:T(8,128)(2,1)}, bf16[128,4096]{1,0:T(8,128)(2,1)}, u32[]{:S(2)}, u32[]{:S(2)}) collective-permute-start(bf16[128,4096]{1,0:T(8,128)(2,1)} %collective-permute-done), channel_id=1, source_target_pairs={{2,4},{4,2},{3,5},{5,3},{10,12},{12,10},{11,13},{13,11},{18,20},{2... | collective-permute-start | bytes 3145736 | tf_op jit(solution)/shard_map/ppermute | solution.py:158
  31.1 30.0 %collective-permute-start.5 = (bf16[128,4096]{1,0:T(8,128)(2,1)}, bf16[128,4096]{1,0:T(8,128)(2,1)S(1)}, u32[]{:S(2)}, u32[]{:S(2)}) collective-permute-start(bf16[128,4096]{1,0:T(8,128)(2,1)} %collective-permute-done), channel_id=1, source_target_pairs={{0,1},{1,0},{2,3},{3,2},{4,5},{5,4},{6,7},{7,6},{8,9},{9,8},{10,11... | collective-permute-start | bytes 3145736 | tf_op jit(solution)/shard_map/ppermute | solution.py:154
  32.6 28.5 %collective-permute-start.3 = (bf16[128,4096]{1,0:T(8,128)(2,1)}, bf16[128,4096]{1,0:T(8,128)(2,1)}, u32[]{:S(2)}, u32[]{:S(2)}) collective-permute-start(bf16[128,4096]{1,0:T(8,128)(2,1)} %copy-done.19), channel_id=1, source_target_pairs={{2,0},{4,6},{3,1},{5,7},{10,8},{12,14},{11,9},{13,15},{18,16},{20,... | collective-permute-start | bytes 3145736 | tf_op jit(solution)/shard_map/ppermute | solution.py:158
  47.5 13.6 %copy-start.28 = (s32[1,128,4]{1,2,0:T(4,128)S(1)}, s32[1,128,4]{1,2,0:T(4,128)}, u32[]{:S(2)}) copy-start(s32[1,128,4]{1,2,0:T(4,128)} %param.26) | copy-start | bytes 6148
  47.5 13.6 %copy-start.29 = (s32[1,128,4]{1,2,0:T(4,128)S(1)}, s32[1,128,4]{1,2,0:T(4,128)}, u32[]{:S(2)}) copy-start(s32[1,128,4]{1,2,0:T(4,128)} %param.25) | copy-start | bytes 6148
  47.5 15.7 %copy-start.20 = (bf16[128,4096]{1,0:T(8,128)(2,1)S(1)}, bf16[128,4096]{1,0:T(8,128)(2,1)}, u32[]{:S(2)}) copy-start(bf16[128,4096]{1,0:T(8,128)(2,1)} %copy-done.19) | copy-start | bytes 3145732
  61.1 12.8 %collective-permute-start.15 = (s32[128,8]{0,1:T(8,128)S(1)}, s32[128,8]{0,1:T(8,128)S(1)}, u32[]{:S(2)}, u32[]{:S(2)}) collective-permute-start(s32[128,8]{0,1:T(8,128)S(1)} %get-tuple-element.103), channel_id=1, source_target_pairs={{0,2},{2,0},{4,6},{6,4},{1,3},{3,1},{5,7},{7,5},{8,10},{10,8},{12,... | collective-permute-start | bytes 12296 | tf_op jit(solution)/shard_map/ppermute | solution.py:158
  61.2 13.4 %collective-permute-start.16 = (s32[128,8]{0,1:T(8,128)S(1)}, s32[128,8]{0,1:T(8,128)S(1)}, u32[]{:S(2)}, u32[]{:S(2)}) collective-permute-start(s32[128,8]{0,1:T(8,128)S(1)} %get-tuple-element.103), channel_id=1, source_target_pairs={{2,4},{4,2},{3,5},{5,3},{10,12},{12,10},{11,13},{13,11},{18,20},{2... | collective-permute-start | bytes 12296 | tf_op jit(solution)/shard_map/ppermute | solution.py:158
  61.9 27.6 %collective-permute-start.6 = (bf16[128,4096]{1,0:T(8,128)(2,1)}, bf16[128,4096]{1,0:T(8,128)(2,1)S(1)}, u32[]{:S(2)}, u32[]{:S(2)}) collective-permute-start(bf16[128,4096]{1,0:T(8,128)(2,1)} %collective-permute-done.4), channel_id=1, source_target_pairs={{2,0},{4,6},{3,1},{5,7},{10,8},{12,14},{11,9},{13,15},{18,16},{20,... | collective-permute-start | bytes 3145736 | tf_op jit(solution)/shard_map/ppermute | solution.py:158
  65.7 23.8 %collective-permute-start.7 = (bf16[128,4096]{1,0:T(8,128)(2,1)S(1)}, bf16[128,4096]{1,0:T(8,128)(2,1)S(1)}, u32[]{:S(2)}, u32[]{:S(2)}) collective-permute-start(bf16[128,4096]{1,0:T(8,128)(2,1)S(1)} %get-tuple-element.81), channel_id=1, source_target_pairs={{0,1},{1,0},{2,3},{3,2},{4,5},{5,4},{6,7},{7,6},{8,9},{9,8},{10,11... | collective-permute-start | bytes 3145736 | tf_op jit(solution)/shard_map/ppermute | solution.py:154
  66.3 23.1 %collective-permute-start.8 = (bf16[128,2048]{1,0:T(8,128)(2,1)S(1)}, bf16[128,2048]{1,0:T(8,128)(2,1)S(1)}, u32[]{:S(2)}, u32[]{:S(2)}) collective-permute-start(bf16[128,2048]{1,0:T(8,128)(2,1)S(1)} %slice.84), channel_id=1, source_target_pairs={{2,4},{4,2},{3,5},{5,3},{10,12},{12,10},{11,13},{13,11},{18,20},{2... | collective-permute-start | bytes 1572872 | tf_op jit(solution)/shard_map/ppermute | solution.py:158
  74.0 5.5 %collective-permute-start.18 = (s32[128,8]{0,1:T(8,128)S(1)}, s32[128,8]{0,1:T(8,128)S(1)}, u32[]{:S(2)}, u32[]{:S(2)}) collective-permute-start(s32[128,8]{0,1:T(8,128)S(1)} %collective-permute-done.15), channel_id=1, source_target_pairs={{2,4},{4,2},{3,5},{5,3},{10,12},{12,10},{11,13},{13,11},{18,20},{2... | collective-permute-start | bytes 12296 | tf_op jit(solution)/shard_map/ppermute | solution.py:158
  74.6 12.8 %collective-permute-start.17 = (s32[128,8]{0,1:T(8,128)S(1)}, s32[128,8]{0,1:T(8,128)S(1)}, u32[]{:S(2)}, u32[]{:S(2)}) collective-permute-start(s32[128,8]{0,1:T(8,128)S(1)} %collective-permute-done.16), channel_id=1, source_target_pairs={{2,0},{4,6},{3,1},{5,7},{10,8},{12,14},{11,9},{13,15},{18,16},{20,... | collective-permute-start | bytes 12296 | tf_op jit(solution)/shard_map/ppermute | solution.py:158
  79.5 10.0 %collective-permute-start.19 = (s32[128,8]{0,1:T(8,128)S(1)}, s32[128,8]{0,1:T(8,128)S(1)}, u32[]{:S(2)}, u32[]{:S(2)}) collective-permute-start(s32[128,8]{0,1:T(8,128)S(1)} %collective-permute-done.18), channel_id=1, source_target_pairs={{2,0},{4,6},{3,1},{5,7},{10,8},{12,14},{11,9},{13,15},{18,16},{20,... | collective-permute-start | bytes 12296 | tf_op jit(solution)/shard_map/ppermute | solution.py:158
  89.7 9.8 %collective-permute-start.9 = (bf16[128,2048]{1,0:T(8,128)(2,1)S(1)}, bf16[128,2048]{1,0:T(8,128)(2,1)S(1)}, u32[]{:S(2)}, u32[]{:S(2)}) collective-permute-start(bf16[128,2048]{1,0:T(8,128)(2,1)S(1)} %get-tuple-element.89), channel_id=1, source_target_pairs={{0,1},{1,0},{2,3},{3,2},{4,5},{5,4},{6,7},{7,6},{8,9},{9,8},{10,11... | collective-permute-start | bytes 1572872 | tf_op jit(solution)/shard_map/ppermute | solution.py:154
  91.3 11.1 %collective-permute-start.10 = (bf16[128,2048]{1,0:T(8,128)(2,1)S(1)}, bf16[128,2048]{1,0:T(8,128)(2,1)S(1)}, u32[]{:S(2)}, u32[]{:S(2)}) collective-permute-start(bf16[128,2048]{1,0:T(8,128)(2,1)S(1)} %collective-permute-done.8), channel_id=1, source_target_pairs={{2,0},{4,6},{3,1},{5,7},{10,8},{12,14},{11,9},{13,15},{18,16},{20,... | collective-permute-start | bytes 1572872 | tf_op jit(solution)/shard_map/ppermute | solution.py:158
  104.9 3.3 collective-permute-start.13
  107.6 2.8 collective-permute-start.11
  108.6 15.0 %collective-permute-start.14 = (bf16[128,2048]{1,0:T(8,128)(2,1)S(1)}, bf16[128,2048]{1,0:T(8,128)(2,1)}, u32[]{:S(2)}, u32[]{:S(2)}) collective-permute-start(bf16[128,2048]{1,0:T(8,128)(2,1)S(1)} %fusion.25), channel_id=1, source_target_pairs={{0,16},{16,0},{1,17},{17,1},{2,18},{18,2},{3,19},{19,3},{4,20},{20... | collective-permute-start | bytes 1572872 | tf_op jit(solution)/shard_map/ppermute | solution.py:154
  112.9 20.9 %collective-permute-start.12 = (bf16[128,2048]{1,0:T(8,128)(2,1)}, bf16[128,2048]{1,0:T(8,128)(2,1)}, u32[]{:S(2)}, u32[]{:S(2)}) collective-permute-start(bf16[128,2048]{1,0:T(8,128)(2,1)} %fusion.24), channel_id=1, source_target_pairs={{0,16},{16,0},{1,17},{17,1},{2,18},{18,2},{3,19},{19,3},{4,20},{20... | collective-permute-start | bytes 1572872 | tf_op jit(solution)/shard_map/ppermute | solution.py:154
  117.6 16.2 %copy-start.15 = (f32[2,128,2048]{2,1,0:T(8,128)S(1)}, f32[2,128,2048]{2,1,0:T(8,128)}, u32[]{:S(2)}) copy-start(f32[2,128,2048]{2,1,0:T(8,128)} %copy-done.14) | copy-start | bytes 6291460
  117.7 17.4 %copy-start.16 = (bf16[1,128,4096]{2,1,0:T(8,128)(2,1)S(1)}, bf16[1,128,4096]{2,1,0:T(8,128)(2,1)}, u32[]{:S(2)}) copy-start(bf16[1,128,4096]{2,1,0:T(8,128)(2,1)} %param.14) | copy-start | bytes 3145732
  124.7 10.7 %copy-start.9 = (f32[128,2048]{1,0:T(8,128)}, f32[128,2048]{1,0:T(8,128)S(1)}, u32[]{:S(2)}) copy-start(f32[128,2048]{1,0:T(8,128)S(1)} %bitcast_add_fusion.2) | copy-start | bytes 3145732
  136.3 10.6 %collective-permute-start.20 = (bf16[128,4096]{1,0:T(8,128)(2,1)S(1)}, bf16[128,4096]{1,0:T(8,128)(2,1)S(1)}, u32[]{:S(2)}, u32[]{:S(2)}) collective-permute-start(bf16[128,4096]{1,0:T(8,128)(2,1)S(1)} %fusion.9.refs_0_), channel_id=1, source_target_pairs={{2,4},{4,2},{3,5},{5,3},{10,12},{12,10},{11,13},{13,11},{18,20},{2... | collective-permute-start | bytes 3145736 | tf_op jit(solution)/shard_map/ppermute | solution.py:158
  137.1 24.6 %collective-permute-start.22 = (bf16[128,4096]{1,0:T(8,128)(2,1)S(1)}, bf16[128,4096]{1,0:T(8,128)(2,1)}, u32[]{:S(2)}, u32[]{:S(2)}) collective-permute-start(bf16[128,4096]{1,0:T(8,128)(2,1)S(1)} %fusion.9.refs_0_), channel_id=1, source_target_pairs={{0,2},{2,0},{4,6},{6,4},{1,3},{3,1},{5,7},{7,5},{8,10},{10,8},{12,... | collective-permute-start | bytes 3145736 | tf_op jit(solution)/shard_map/ppermute | solution.py:158
  142.6 30.6 %all-to-all-start.1 = ((bf16[8,32,4096]{2,1,0:T(8,128)(2,1)}), bf16[8,32,4096]{2,1,0:T(8,128)(2,1)}, u32[]{:S(2)}, u32[]{:S(2)}) async-start(bf16[8,32,4096]{2,1,0:T(8,128)(2,1)} %bitcast.37), calls=%async_computation.1 | async-start | bytes 4194304 | tf_op jit(solution)/shard_map/all_to_all | solution.py:279
  147.0 38.1 %collective-permute-start.21 = (bf16[128,4096]{1,0:T(8,128)(2,1)S(1)}, bf16[128,4096]{1,0:T(8,128)(2,1)}, u32[]{:S(2)}, u32[]{:S(2)}) collective-permute-start(bf16[128,4096]{1,0:T(8,128)(2,1)S(1)} %collective-permute-done.20.refs_0_), channel_id=1, source_target_pairs={{2,0},{4,6},{3,1},{5,7},{10,8},{12,14},{11,9},{13,15},{18,16},{20,... | collective-permute-start | bytes 3145736 | tf_op jit(solution)/shard_map/ppermute | solution.py:158
  161.7 26.4 %collective-permute-start.23 = (bf16[128,4096]{1,0:T(8,128)(2,1)}, bf16[128,4096]{1,0:T(8,128)(2,1)S(1)}, u32[]{:S(2)}, u32[]{:S(2)}) collective-permute-start(bf16[128,4096]{1,0:T(8,128)(2,1)} %collective-permute-done.22.refs_0_), channel_id=1, source_target_pairs={{2,4},{4,2},{3,5},{5,3},{10,12},{12,10},{11,13},{13,11},{18,20},{2... | collective-permute-start | bytes 3145736 | tf_op jit(solution)/shard_map/ppermute | solution.py:158
  173.1 30.5 %all-to-all-start.2 = ((bf16[8,32,4096]{2,1,0:T(8,128)(2,1)}), bf16[8,32,4096]{2,1,0:T(8,128)(2,1)}, u32[]{:S(2)}, u32[]{:S(2)}) async-start(bf16[8,32,4096]{2,1,0:T(8,128)(2,1)} %bitcast.39), calls=%async_computation.2 | async-start | bytes 4194304 | tf_op jit(solution)/shard_map/all_to_all | solution.py:279
  203.7 26.6 %collective-permute-start.24 = (bf16[128,4096]{1,0:T(8,128)(2,1)S(1)}, bf16[128,4096]{1,0:T(8,128)(2,1)S(1)}, u32[]{:S(2)}, u32[]{:S(2)}) collective-permute-start(bf16[128,4096]{1,0:T(8,128)(2,1)S(1)} %collective-permute-done.23.refs_0_), channel_id=1, source_target_pairs={{2,0},{4,6},{3,1},{5,7},{10,8},{12,14},{11,9},{13,15},{18,16},{20,... | collective-permute-start | bytes 3145736 | tf_op jit(solution)/shard_map/ppermute | solution.py:158
  204.9 30.5 %all-to-all-start.3 = ((bf16[8,32,4096]{2,1,0:T(8,128)(2,1)}), bf16[8,32,4096]{2,1,0:T(8,128)(2,1)}, u32[]{:S(2)}, u32[]{:S(2)}) async-start(bf16[8,32,4096]{2,1,0:T(8,128)(2,1)} %bitcast.48), calls=%async_computation.3 | async-start | bytes 4194304 | tf_op jit(solution)/shard_map/all_to_all | solution.py:279
  235.5 29.7 %all-to-all-start.4 = ((bf16[8,32,4096]{2,1,0:T(8,128)(2,1)}), bf16[8,32,4096]{2,1,0:T(8,128)(2,1)S(1)}, u32[]{:S(2)}, u32[]{:S(2)}) async-start(bf16[8,32,4096]{2,1,0:T(8,128)(2,1)} %bitcast.51), calls=%async_computation.4 | async-start | bytes 4194304 | tf_op jit(solution)/shard_map/all_to_all | solution.py:279
  279.3 29.7 %all-to-all-start.5 = ((bf16[8,32,4096]{2,1,0:T(8,128)(2,1)}), bf16[8,32,4096]{2,1,0:T(8,128)(2,1)S(1)}, u32[]{:S(2)}, u32[]{:S(2)}) async-start(bf16[8,32,4096]{2,1,0:T(8,128)(2,1)} %bitcast.120), calls=%async_computation.5 | async-start | bytes 4194304 | tf_op jit(solution)/shard_map/all_to_all | solution.py:279
  311.1 35.3 %all-to-all-start.6 = ((bf16[8,32,4096]{2,1,0:T(8,128)(2,1)}), bf16[8,32,4096]{2,1,0:T(8,128)(2,1)S(1)}, u32[]{:S(2)}, u32[]{:S(2)}) async-start(bf16[8,32,4096]{2,1,0:T(8,128)(2,1)} %bitcast.118), calls=%async_computation.6 | async-start | bytes 4194304 | tf_op jit(solution)/shard_map/all_to_all | solution.py:279
  314.7 27.9 %collective-permute-start.25 = (bf16[128,4096]{1,0:T(8,128)(2,1)}, bf16[128,4096]{1,0:T(8,128)(2,1)S(1)}, u32[]{:S(2)}, u32[]{:S(2)}) collective-permute-start(bf16[128,4096]{1,0:T(8,128)(2,1)} %copy-done.2), channel_id=1, source_target_pairs={{0,2},{6,4},{1,3},{7,5},{8,10},{14,12},{9,11},{15,13},{16,18},{22,... | collective-permute-start | bytes 3145736 | tf_op jit(solution)/shard_map/ppermute | solution.py:158
  346.5 30.6 %all-to-all-start.7 = ((bf16[8,32,4096]{2,1,0:T(8,128)(2,1)}), bf16[8,32,4096]{2,1,0:T(8,128)(2,1)}, u32[]{:S(2)}, u32[]{:S(2)}) async-start(bf16[8,32,4096]{2,1,0:T(8,128)(2,1)} %bitcast.123), calls=%async_computation.7 | async-start | bytes 4194304 | tf_op jit(solution)/shard_map/all_to_all | solution.py:279
  350.8 26.2 %copy-start.8 = (bf16[256,256]{1,0:T(8,128)(2,1)S(1)}, bf16[256,256]{1,0:T(8,128)(2,1)}, u32[]{:S(2)}) copy-start(bf16[256,256]{1,0:T(8,128)(2,1)} %get-tuple-element.92.share_ref) | copy-start | bytes 393220
  350.9 9.9 %collective-permute-start.26 = (bf16[128,4096]{1,0:T(8,128)(2,1)}, bf16[128,4096]{1,0:T(8,128)(2,1)S(1)}, u32[]{:S(2)}, u32[]{:S(2)}) collective-permute-start(bf16[128,4096]{1,0:T(8,128)(2,1)} %copy-done.5), channel_id=1, source_target_pairs={{2,4},{4,2},{3,5},{5,3},{10,12},{12,10},{11,13},{13,11},{18,20},{2... | collective-permute-start | bytes 3145736 | tf_op jit(solution)/shard_map/ppermute | solution.py:158
  353.6 32.2 %collective-permute-start.27 = (bf16[128,4096]{1,0:T(8,128)(2,1)}, bf16[128,4096]{1,0:T(8,128)(2,1)}, u32[]{:S(2)}, u32[]{:S(2)}) collective-permute-start(bf16[128,4096]{1,0:T(8,128)(2,1)} %combine.9), channel_id=1, source_target_pairs={{0,2},{6,4},{1,3},{7,5},{8,10},{14,12},{9,11},{15,13},{16,18},{22,... | collective-permute-start | bytes 3145736 | tf_op jit(solution)/shard_map/ppermute | solution.py:158
  381.5 37.5 %all-to-all-start.8 = ((bf16[8,32,4096]{2,1,0:T(8,128)(2,1)}), bf16[8,32,4096]{2,1,0:T(8,128)(2,1)}, u32[]{:S(2)}, u32[]{:S(2)}) async-start(bf16[8,32,4096]{2,1,0:T(8,128)(2,1)} %bitcast.122), calls=%async_computation.8 | async-start | bytes 4194304 | tf_op jit(solution)/shard_map/all_to_all | solution.py:279
  385.8 9.7 %copy-start.10 = (f32[128,2048]{1,0:T(8,128)S(1)}, f32[128,2048]{1,0:T(8,128)}, u32[]{:S(2)}) copy-start(f32[128,2048]{1,0:T(8,128)} %copy-done.9) | copy-start | bytes 3145732
  385.9 9.7 %copy-start.12 = (f32[128,2048]{1,0:T(8,128)S(1)}, f32[128,2048]{1,0:T(8,128)}, u32[]{:S(2)}) copy-start(f32[128,2048]{1,0:T(8,128)} %copy-done.11) | copy-start | bytes 3145732
  388.1 8.6 %collective-permute-start.28 = (bf16[128,4096]{1,0:T(8,128)(2,1)S(1)}, bf16[128,4096]{1,0:T(8,128)(2,1)S(1)}, u32[]{:S(2)}, u32[]{:S(2)}) collective-permute-start(bf16[128,4096]{1,0:T(8,128)(2,1)S(1)} %combine.10), channel_id=1, source_target_pairs={{2,4},{4,2},{3,5},{5,3},{10,12},{12,10},{11,13},{13,11},{18,20},{2... | collective-permute-start | bytes 3145736 | tf_op jit(solution)/shard_map/ppermute | solution.py:158
  388.9 30.1 %collective-permute-start.29 = (bf16[128,4096]{1,0:T(8,128)(2,1)S(1)}, bf16[128,4096]{1,0:T(8,128)(2,1)S(1)}, u32[]{:S(2)}, u32[]{:S(2)}) collective-permute-start(bf16[128,4096]{1,0:T(8,128)(2,1)S(1)} %copy-done.4), channel_id=1, source_target_pairs={{0,2},{2,0},{4,6},{6,4},{1,3},{3,1},{5,7},{7,5},{8,10},{10,8},{12,... | collective-permute-start | bytes 3145736 | tf_op jit(solution)/shard_map/ppermute | solution.py:158
  (21 other events, 55.3 us)

commit v4 on v3

--- a/solution.py
+++ b/solution.py
@@ -400,7 +400,7 @@
     out_ref[...] = total.astype(out_ref.dtype)
 
 
-def combine(share, rows, *added):
+def combine(share, rows, *added, cost=None, room=VMEM):
     slots = rows.shape[0]
     tokens = share.shape[0] // 2
     tile = D // 2
@@ -415,9 +415,9 @@
         ]
         + [block] * len(added),
         out_specs=block,
-        compiler_params=pltpu.CompilerParams(vmem_limit_bytes=VMEM),
+        compiler_params=pltpu.CompilerParams(vmem_limit_bytes=room),
         cost_estimate=pl.CostEstimate(
-            flops=tokens, bytes_accessed=tokens, transcendentals=0
+            flops=cost or tokens, bytes_accessed=tokens, transcendentals=0
         ),
         name="combine",
     )(share, rows, *added)
@@ -560,18 +560,16 @@
     middle_out, far, far_sum = together(middle_out, far, far_sum)
     middle = plane_exchange(middle_out)
     outer_far = along(far_sum, INWARD)
-    inner_sum = combine(shares[3], far, outer_far)
-    near_out, middle, inner_sum = together(near_out, middle, inner_sum)
+    near_out, middle, outer_far = together(near_out, middle, outer_far)
     near = plane_exchange(near_out)
-    inner_far = along(inner_sum, INNER)
-    outer_middle = along(combine(shares[2], middle), INWARD)
-    near_sum = combine(shares[1], near, inner_far)
-    own_out, near_sum = together(own_out, near_sum)
+    inner_far = along(combine(shares[3], far, outer_far), INNER)
+    outer_middle = along(combine(shares[2], middle, cost=COST), INWARD)
+    own_out, near = together(own_out, near)
     own = plane_exchange(own_out)
-    inner_middle = along(combine(shares[2], middle, outer_middle), INNER)
-    all_near = along(near_sum, OUTER)
+    all_near = along(combine(shares[1], near, inner_far), OUTER)
+    inner_middle = along(combine(shares[2], middle, outer_middle, cost=COST), INNER)
     layer_output = combine(
-        shares[0], own, after_attention, inner_middle, all_near
+        shares[0], own, after_attention, inner_middle, all_near, room=58 * 2**20
     )
     return (after_attention[None], layer_output[None])
 

time: 424 us -> 418 us (0.986)
  local copies, waits for them, and re-layouts: 33.1 us -> 28.2 us
    unnamed x76 -> x70, local copies, waits for them, and re-layouts: 22.5 us -> 18.7 us
  transfers between devices with their start and end apart: 39 -> 39, of which waited for: 22 -> 23; matrix products, arithmetic and copies ran while one was open for 9% -> 9% of each run, Pallas kernels for 14% -> 14%
where the time goes in v4:
time: 418 us; the launch traced here: 416 us
  waiting for transfers between devices  203 us (49%)
  starting transfers between devices  82.6 us (20%)
  Pallas kernels  77.3 us (18%)
  local copies, waits for them, and re-layouts  28.2 us (7%)
  other arithmetic  11 us (3%)
  matrix products  9.71 us (2%)
    ppermute x22, waiting for transfers between devices, along(): return lax.ppermute(value, 'z', pairs)  96.2 us
    all_to_all x8, waiting for transfers between devices, plane_exchange(): lax.all_to_all(blocks, PLANE, split_axis=0, concat_axis=0, tiled=True)  82.1 us
    ppermute x22, starting transfers between devices, along(): return lax.ppermute(value, 'z', pairs)  36.3 us
    all_to_all x8, starting transfers between devices, plane_exchange(): lax.all_to_all(blocks, PLANE, split_axis=0, concat_axis=0, tiled=True)  33.7 us
    pallas_call x2, Pallas kernels, expert(): pl.pallas_call(expert_kernel, grid=(hidden // tile,), out_shape=jax.Shape...  25.6 us
    ppermute x8, waiting for transfers between devices, swap(): return lax.ppermute(value, axis, [(0, 1), (1, 0)])  24.2 us
    unnamed x70, local copies, waits for them, and re-layouts  18.7 us
    pallas_call x1, Pallas kernels, experts(): pl.pallas_call(functools.partial(experts_kernel, blocks=len(blocks), step...  18.4 us
  transfers between devices with their start and end apart: 39, of which 23 were waited for; matrix products, arithmetic and copies ran while one was open for 9% of the time, Pallas kernels for 14%

profile of v4, /device:TPU:0, one launch (start us, length us, event | category | flops | bytes accessed | tf_op | source)
XLA Modules:
  0.0 416.2 jit_solution(13705779662445229237)
XLA Ops:
  0.6 3.1 collective-permute-start
  13.2 3.6 all-to-all-start
  20.8 2.3 constant_dynamic-update-slice_fusion.4
  23.1 4.1 collective-permute-done
  27.2 2.2 collective-permute-done.2
  33.8 2.3 constant_dynamic-update-slice_fusion.3
  36.8 10.7 %attention.1 = bf16[512,1024]{1,0:T(8,128)(2,1)S(1)} custom-call(bf16[4,128,1536]{2,1,0:T(8,128)(2,1)S(1)} %all-to-all-done.message_ref), custom_call_target="tpu_custom_call" | custom-call | flops 1744830464 | bytes 2621440 | tf_op jit(solution)/shard_map/attention/pallas_call | solution.py:230
  47.9 13.2 %collective-permute-done.3 = bf16[128,4096]{1,0:T(8,128)(2,1)} collective-permute-done((bf16[128,4096]{1,0:T(8,128)(2,1)}, bf16[128,4096]{1,0:T(8,128)(2,1)}, u32[]{:S(2)}, u32[]{:S(2)}) %collective-permute-start.3) | collective-permute-done | bytes 1048608 | tf_op jit(solution)/shard_map/ppermute | solution.py:158
  63.2 2.5 constant_dynamic-update-slice_fusion.2
  67.0 2.3 constant_dynamic-update-slice_fusion.1
  70.4 3.5 fusion.2
  75.9 3.5 fusion
  80.8 6.6 %collective-permute-done.17 = s32[128,8]{0,1:T(8,128)S(1)} collective-permute-done((s32[128,8]{0,1:T(8,128)S(1)}, s32[128,8]{0,1:T(8,128)S(1)}, u32[]{:S(2)}, u32[]{:S(2)}) %collective-permute-start.17) | collective-permute-done | bytes 4128 | tf_op jit(solution)/shard_map/ppermute | solution.py:158
  92.9 6.7 %collective-permute-done.9 = bf16[128,2048]{1,0:T(8,128)(2,1)S(1)} collective-permute-done((bf16[128,2048]{1,0:T(8,128)(2,1)S(1)}, bf16[128,2048]{1,0:T(8,128)(2,1)S(1)}, u32[]{:S(2)}, u32[]{:S(2)}) %collective-permute-start.9) | collective-permute-done | bytes 524320 | tf_op jit(solution)/shard_map/ppermute | solution.py:154
  99.5 2.8 collective-permute-done.10
  117.7 5.9 %collective-permute-done.14 = bf16[128,2048]{1,0:T(8,128)(2,1)} collective-permute-done((bf16[128,2048]{1,0:T(8,128)(2,1)S(1)}, bf16[128,2048]{1,0:T(8,128)(2,1)}, u32[]{:S(2)}, u32[]{:S(2)}) %collective-permute-start.14) | collective-permute-done | bytes 524320 | tf_op jit(solution)/shard_map/ppermute | solution.py:154
  124.7 9.1 %collective-permute-done.12 = bf16[128,2048]{1,0:T(8,128)(2,1)} collective-permute-done((bf16[128,2048]{1,0:T(8,128)(2,1)}, bf16[128,2048]{1,0:T(8,128)(2,1)}, u32[]{:S(2)}, u32[]{:S(2)}) %collective-permute-start.12) | collective-permute-done | bytes 524320 | tf_op jit(solution)/shard_map/ppermute | solution.py:154
  137.2 2.3 collective-permute-start.22
  142.6 4.4 %all-to-all-start.1 = ((bf16[8,32,4096]{2,1,0:T(8,128)(2,1)}), bf16[8,32,4096]{2,1,0:T(8,128)(2,1)}, u32[]{:S(2)}, u32[]{:S(2)}) async-start(bf16[8,32,4096]{2,1,0:T(8,128)(2,1)} %bitcast.37), calls=%async_computation.1 | async-start | bytes 4194304 | tf_op jit(solution)/shard_map/all_to_all | solution.py:279
  148.3 13.4 %collective-permute-done.22.refs_0_ = bf16[128,4096]{1,0:T(8,128)(2,1)S(1)} collective-permute-done((bf16[128,4096]{1,0:T(8,128)(2,1)S(1)}, bf16[128,4096]{1,0:T(8,128)(2,1)S(1)}, u32[]{:S(2)}, u32[]{:S(2)}) %collective-permute-start.22) | collective-permute-done | bytes 1048608 | tf_op jit(solution)/shard_map/ppermute | solution.py:158
  164.3 8.8 %all-to-all-done.1 = bf16[8,32,4096]{2,1,0:T(8,128)(2,1)} async-done(((bf16[8,32,4096]{2,1,0:T(8,128)(2,1)}), bf16[8,32,4096]{2,1,0:T(8,128)(2,1)}, u32[]{:S(2)}, u32[]{:S(2)}) %all-to-all-start.1) | async-done | bytes 2097184 | tf_op jit(solution)/shard_map/all_to_all | solution.py:279
  173.2 4.4 %all-to-all-start.2 = ((bf16[8,32,4096]{2,1,0:T(8,128)(2,1)}), bf16[8,32,4096]{2,1,0:T(8,128)(2,1)}, u32[]{:S(2)}, u32[]{:S(2)}) async-start(bf16[8,32,4096]{2,1,0:T(8,128)(2,1)} %bitcast.39), calls=%async_computation.2 | async-start | bytes 4194304 | tf_op jit(solution)/shard_map/all_to_all | solution.py:279
  177.5 7.6 %collective-permute-done.21.refs_1_ = bf16[128,4096]{1,0:T(8,128)(2,1)} collective-permute-done((bf16[128,4096]{1,0:T(8,128)(2,1)S(1)}, bf16[128,4096]{1,0:T(8,128)(2,1)}, u32[]{:S(2)}, u32[]{:S(2)}) %collective-permute-start.21) | collective-permute-done | bytes 1048608 | tf_op jit(solution)/shard_map/ppermute | solution.py:158
  185.2 3.0 slots.4
  188.2 15.6 %all-to-all-done.2 = bf16[8,32,4096]{2,1,0:T(8,128)(2,1)} async-done(((bf16[8,32,4096]{2,1,0:T(8,128)(2,1)}), bf16[8,32,4096]{2,1,0:T(8,128)(2,1)}, u32[]{:S(2)}, u32[]{:S(2)}) %all-to-all-start.2) | async-done | bytes 2097184 | tf_op jit(solution)/shard_map/all_to_all | solution.py:279
  205.0 4.6 %all-to-all-start.3 = ((bf16[8,32,4096]{2,1,0:T(8,128)(2,1)}), bf16[8,32,4096]{2,1,0:T(8,128)(2,1)}, u32[]{:S(2)}, u32[]{:S(2)}) async-start(bf16[8,32,4096]{2,1,0:T(8,128)(2,1)} %bitcast.48), calls=%async_computation.3 | async-start | bytes 4194304 | tf_op jit(solution)/shard_map/all_to_all | solution.py:279
  209.6 18.4 %experts.1 = (bf16[256,4096]{1,0:T(8,128)(2,1)}, bf16[256,4096]{1,0:T(8,128)(2,1)}) custom-call(bf16[256,4096]{1,0:T(8,128)(2,1)} %bitcast.38.refs_0_, bf16[256,4096]{1,0:T(8,128)(2,1)} %bitcast.40.refs_1_, bf16[1,4096,768]{2,1,0:T(8,128)(2,1)} %gate_ref.3, bf16[1,4096,768]{2,1,0:T(8,128)(2,1)} %up_ref.3, bf16[1,768,4096]{2,1,0:T(8,128)(2,1)} %down_ref.3), custom_call_target="tpu_custom_call" | custom-call | flops 512 | bytes 512 | tf_op jit(solution)/shard_map/experts/pallas_call | solution.py:328
  228.0 2.4 collective-permute-done.24.refs_1_
  232.4 3.2 all-to-all-done.3
  235.5 3.6 all-to-all-start.4
  239.1 12.8 %expert.2 = bf16[256,4096]{1,0:T(8,128)(2,1)} custom-call(bf16[256,4096]{1,0:T(8,128)(2,1)} %bitcast.49.rows_ref, bf16[1,4096,768]{2,1,0:T(8,128)(2,1)} %gate_ref.3, bf16[1,4096,768]{2,1,0:T(8,128)(2,1)} %up_ref.3, bf16[1,768,4096]{2,1,0:T(8,128)(2,1)} %down_ref.3), custom_call_target="tpu_custom_call" | custom-call | flops 4831838208 | bytes 23068672 | tf_op jit(solution)/shard_map/expert/pallas_call | solution.py:371
  251.9 13.3 %all-to-all-done.4 = bf16[8,32,4096]{2,1,0:T(8,128)(2,1)S(1)} async-done(((bf16[8,32,4096]{2,1,0:T(8,128)(2,1)}), bf16[8,32,4096]{2,1,0:T(8,128)(2,1)S(1)}, u32[]{:S(2)}, u32[]{:S(2)}) %all-to-all-start.4) | async-done | bytes 2097184 | tf_op jit(solution)/shard_map/all_to_all | solution.py:279
  266.5 12.8 %expert.3 = bf16[256,4096]{1,0:T(8,128)(2,1)} custom-call(bf16[256,4096]{1,0:T(8,128)(2,1)} %bitcast.117, bf16[1,4096,768]{2,1,0:T(8,128)(2,1)} %gate_ref.3, bf16[1,4096,768]{2,1,0:T(8,128)(2,1)} %up_ref.3, bf16[1,768,4096]{2,1,0:T(8,128)(2,1)} %down_ref.3), custom_call_target="tpu_custom_call" | custom-call | flops 4831838208 | bytes 23068672 | tf_op jit(solution)/shard_map/expert/pallas_call | solution.py:371
  279.4 3.7 all-to-all-start.5
  283.8 25.4 %all-to-all-done.5 = bf16[8,32,4096]{2,1,0:T(8,128)(2,1)S(1)} async-done(((bf16[8,32,4096]{2,1,0:T(8,128)(2,1)}), bf16[8,32,4096]{2,1,0:T(8,128)(2,1)S(1)}, u32[]{:S(2)}, u32[]{:S(2)}) %all-to-all-start.5) | async-done | bytes 2097184 | tf_op jit(solution)/shard_map/all_to_all | solution.py:279
  310.3 4.3 %all-to-all-start.6 = ((bf16[8,32,4096]{2,1,0:T(8,128)(2,1)}), bf16[8,32,4096]{2,1,0:T(8,128)(2,1)}, u32[]{:S(2)}, u32[]{:S(2)}) async-start(bf16[8,32,4096]{2,1,0:T(8,128)(2,1)} %bitcast.116), calls=%async_computation.6 | async-start | bytes 4194304 | tf_op jit(solution)/shard_map/all_to_all | solution.py:279
  314.7 4.7 %collective-permute-start.25 = (bf16[128,4096]{1,0:T(8,128)(2,1)S(1)}, bf16[128,4096]{1,0:T(8,128)(2,1)S(1)}, u32[]{:S(2)}, u32[]{:S(2)}) collective-permute-start(bf16[128,4096]{1,0:T(8,128)(2,1)S(1)} %combine.6), channel_id=1, source_target_pairs={{0,2},{6,4},{1,3},{7,5},{8,10},{14,12},{9,11},{15,13},{16,18},{22,... | collective-permute-start | bytes 3145736 | tf_op jit(solution)/shard_map/ppermute | solution.py:158
  319.4 22.9 %collective-permute-done.25.refs_0_ = bf16[128,4096]{1,0:T(8,128)(2,1)S(1)} collective-permute-done((bf16[128,4096]{1,0:T(8,128)(2,1)S(1)}, bf16[128,4096]{1,0:T(8,128)(2,1)S(1)}, u32[]{:S(2)}, u32[]{:S(2)}) %collective-permute-start.25) | collective-permute-done | bytes 1048608 | tf_op jit(solution)/shard_map/ppermute | solution.py:158
  343.2 4.4 %all-to-all-start.7 = ((bf16[8,32,4096]{2,1,0:T(8,128)(2,1)}), bf16[8,32,4096]{2,1,0:T(8,128)(2,1)}, u32[]{:S(2)}, u32[]{:S(2)}) async-start(bf16[8,32,4096]{2,1,0:T(8,128)(2,1)} %bitcast.121), calls=%async_computation.7 | async-start | bytes 4194304 | tf_op jit(solution)/shard_map/all_to_all | solution.py:279
  347.6 3.0 combine.7
  350.6 5.4 %collective-permute-start.26 = (bf16[128,4096]{1,0:T(8,128)(2,1)}, bf16[128,4096]{1,0:T(8,128)(2,1)}, u32[]{:S(2)}, u32[]{:S(2)}) collective-permute-start(bf16[128,4096]{1,0:T(8,128)(2,1)} %combine.7), channel_id=1, source_target_pairs={{0,2},{6,4},{1,3},{7,5},{8,10},{14,12},{9,11},{15,13},{16,18},{22,... | collective-permute-start | bytes 3145736 | tf_op jit(solution)/shard_map/ppermute | solution.py:158
  357.9 15.8 %all-to-all-done.7 = bf16[8,32,4096]{2,1,0:T(8,128)(2,1)} async-done(((bf16[8,32,4096]{2,1,0:T(8,128)(2,1)}), bf16[8,32,4096]{2,1,0:T(8,128)(2,1)}, u32[]{:S(2)}, u32[]{:S(2)}) %all-to-all-start.7) | async-done | bytes 2097184 | tf_op jit(solution)/shard_map/all_to_all | solution.py:279
  373.8 4.4 %all-to-all-start.8 = ((bf16[8,32,4096]{2,1,0:T(8,128)(2,1)}), bf16[8,32,4096]{2,1,0:T(8,128)(2,1)}, u32[]{:S(2)}, u32[]{:S(2)}) async-start(bf16[8,32,4096]{2,1,0:T(8,128)(2,1)} %bitcast.120), calls=%async_computation.8 | async-start | bytes 4194304 | tf_op jit(solution)/shard_map/all_to_all | solution.py:279
  378.3 2.3 combine.8
  381.4 2.4 combine.10
  383.7 4.3 %collective-permute-start.29 = (bf16[128,4096]{1,0:T(8,128)(2,1)S(1)}, bf16[128,4096]{1,0:T(8,128)(2,1)S(1)}, u32[]{:S(2)}, u32[]{:S(2)}) collective-permute-start(bf16[128,4096]{1,0:T(8,128)(2,1)S(1)} %combine.10), channel_id=1, source_target_pairs={{0,2},{2,0},{4,6},{6,4},{1,3},{3,1},{5,7},{7,5},{8,10},{10,8},{12,... | collective-permute-start | bytes 3145736 | tf_op jit(solution)/shard_map/ppermute | solution.py:158
  390.3 21.1 %collective-permute-done.29.refs_2_ = bf16[128,4096]{1,0:T(8,128)(2,1)S(1)} collective-permute-done((bf16[128,4096]{1,0:T(8,128)(2,1)S(1)}, bf16[128,4096]{1,0:T(8,128)(2,1)S(1)}, u32[]{:S(2)}, u32[]{:S(2)}) %collective-permute-start.29) | collective-permute-done | bytes 1048608 | tf_op jit(solution)/shard_map/ppermute | solution.py:158
  412.3 3.8 combine.11
  (175 shorter events, 69.5 us)
Async XLA Ops:
  0.6 26.6 %collective-permute-start = (bf16[128,4096]{1,0:T(8,128)(2,1)}, bf16[128,4096]{1,0:T(8,128)(2,1)}, u32[]{:S(2)}, u32[]{:S(2)}) collective-permute-start(bf16[128,4096]{1,0:T(8,128)(2,1)} %param.20), channel_id=1, source_target_pairs={{0,2},{2,0},{4,6},{6,4},{1,3},{3,1},{5,7},{7,5},{8,10},{10,8},{12,... | collective-permute-start | bytes 3145736 | tf_op jit(solution)/shard_map/ppermute | solution.py:158
  3.7 23.5 %collective-permute-start.1 = (bf16[128,4096]{1,0:T(8,128)(2,1)}, bf16[128,4096]{1,0:T(8,128)(2,1)S(1)}, u32[]{:S(2)}, u32[]{:S(2)}) collective-permute-start(bf16[128,4096]{1,0:T(8,128)(2,1)} %param.20), channel_id=1, source_target_pairs={{2,4},{4,2},{3,5},{5,3},{10,12},{12,10},{11,13},{13,11},{18,20},{2... | collective-permute-start | bytes 3145736 | tf_op jit(solution)/shard_map/ppermute | solution.py:158
  4.4 25.0 %collective-permute-start.2 = (bf16[128,4096]{1,0:T(8,128)(2,1)}, bf16[128,4096]{1,0:T(8,128)(2,1)}, u32[]{:S(2)}, u32[]{:S(2)}) collective-permute-start(bf16[128,4096]{1,0:T(8,128)(2,1)} %param.20), channel_id=1, source_target_pairs={{0,1},{1,0},{2,3},{3,2},{4,5},{5,4},{6,7},{7,6},{8,9},{9,8},{10,11... | collective-permute-start | bytes 3145736 | tf_op jit(solution)/shard_map/ppermute | solution.py:154
  12.3 8.5 %copy-start.24 = (bf16[4096]{0:T(1024)(128)(2,1)S(1)}, bf16[4096]{0:T(1024)(128)(2,1)}, u32[]{:S(2)}) copy-start(bf16[4096]{0:T(1024)(128)(2,1)} %param.21) | copy-start | bytes 24580
  13.2 23.6 %all-to-all-start = ((bf16[4,128,1536]{2,1,0:T(8,128)(2,1)}), bf16[4,128,1536]{2,1,0:T(8,128)(2,1)S(1)}, u32[]{:S(2)}, u32[]{:S(2)}) async-start(bf16[4,128,1536]{2,1,0:T(8,128)(2,1)} %bitcast_dynamic-update-slice_fusion.1), calls=%async_computation | async-start | bytes 3145728 | tf_op jit(solution)/shard_map/all_to_all | solution.py:483
  29.4 31.7 %collective-permute-start.4 = (bf16[128,4096]{1,0:T(8,128)(2,1)}, bf16[128,4096]{1,0:T(8,128)(2,1)}, u32[]{:S(2)}, u32[]{:S(2)}) collective-permute-start(bf16[128,4096]{1,0:T(8,128)(2,1)} %collective-permute-done), channel_id=1, source_target_pairs={{2,4},{4,2},{3,5},{5,3},{10,12},{12,10},{11,13},{13,11},{18,20},{2... | collective-permute-start | bytes 3145736 | tf_op jit(solution)/shard_map/ppermute | solution.py:158
  31.1 30.1 %collective-permute-start.5 = (bf16[128,4096]{1,0:T(8,128)(2,1)}, bf16[128,4096]{1,0:T(8,128)(2,1)S(1)}, u32[]{:S(2)}, u32[]{:S(2)}) collective-permute-start(bf16[128,4096]{1,0:T(8,128)(2,1)} %collective-permute-done), channel_id=1, source_target_pairs={{0,1},{1,0},{2,3},{3,2},{4,5},{5,4},{6,7},{7,6},{8,9},{9,8},{10,11... | collective-permute-start | bytes 3145736 | tf_op jit(solution)/shard_map/ppermute | solution.py:154
  32.6 28.6 %collective-permute-start.3 = (bf16[128,4096]{1,0:T(8,128)(2,1)}, bf16[128,4096]{1,0:T(8,128)(2,1)}, u32[]{:S(2)}, u32[]{:S(2)}) collective-permute-start(bf16[128,4096]{1,0:T(8,128)(2,1)} %copy-done.14), channel_id=1, source_target_pairs={{2,0},{4,6},{3,1},{5,7},{10,8},{12,14},{11,9},{13,15},{18,16},{20,... | collective-permute-start | bytes 3145736 | tf_op jit(solution)/shard_map/ppermute | solution.py:158
  47.5 13.6 %copy-start.25 = (s32[1,128,4]{1,2,0:T(4,128)S(1)}, s32[1,128,4]{1,2,0:T(4,128)}, u32[]{:S(2)}) copy-start(s32[1,128,4]{1,2,0:T(4,128)} %param.26) | copy-start | bytes 6148
  47.5 13.6 %copy-start.26 = (s32[1,128,4]{1,2,0:T(4,128)S(1)}, s32[1,128,4]{1,2,0:T(4,128)}, u32[]{:S(2)}) copy-start(s32[1,128,4]{1,2,0:T(4,128)} %param.25) | copy-start | bytes 6148
  47.5 15.7 %copy-start.15 = (bf16[128,4096]{1,0:T(8,128)(2,1)S(1)}, bf16[128,4096]{1,0:T(8,128)(2,1)}, u32[]{:S(2)}) copy-start(bf16[128,4096]{1,0:T(8,128)(2,1)} %copy-done.14) | copy-start | bytes 3145732
  61.1 12.8 %collective-permute-start.15 = (s32[128,8]{0,1:T(8,128)S(1)}, s32[128,8]{0,1:T(8,128)S(1)}, u32[]{:S(2)}, u32[]{:S(2)}) collective-permute-start(s32[128,8]{0,1:T(8,128)S(1)} %get-tuple-element.103), channel_id=1, source_target_pairs={{0,2},{2,0},{4,6},{6,4},{1,3},{3,1},{5,7},{7,5},{8,10},{10,8},{12,... | collective-permute-start | bytes 12296 | tf_op jit(solution)/shard_map/ppermute | solution.py:158
  61.2 13.4 %collective-permute-start.16 = (s32[128,8]{0,1:T(8,128)S(1)}, s32[128,8]{0,1:T(8,128)S(1)}, u32[]{:S(2)}, u32[]{:S(2)}) collective-permute-start(s32[128,8]{0,1:T(8,128)S(1)} %get-tuple-element.103), channel_id=1, source_target_pairs={{2,4},{4,2},{3,5},{5,3},{10,12},{12,10},{11,13},{13,11},{18,20},{2... | collective-permute-start | bytes 12296 | tf_op jit(solution)/shard_map/ppermute | solution.py:158
  61.9 27.6 %collective-permute-start.6 = (bf16[128,4096]{1,0:T(8,128)(2,1)}, bf16[128,4096]{1,0:T(8,128)(2,1)S(1)}, u32[]{:S(2)}, u32[]{:S(2)}) collective-permute-start(bf16[128,4096]{1,0:T(8,128)(2,1)} %collective-permute-done.4), channel_id=1, source_target_pairs={{2,0},{4,6},{3,1},{5,7},{10,8},{12,14},{11,9},{13,15},{18,16},{20,... | collective-permute-start | bytes 3145736 | tf_op jit(solution)/shard_map/ppermute | solution.py:158
  65.7 23.8 %collective-permute-start.7 = (bf16[128,4096]{1,0:T(8,128)(2,1)S(1)}, bf16[128,4096]{1,0:T(8,128)(2,1)S(1)}, u32[]{:S(2)}, u32[]{:S(2)}) collective-permute-start(bf16[128,4096]{1,0:T(8,128)(2,1)S(1)} %get-tuple-element.81), channel_id=1, source_target_pairs={{0,1},{1,0},{2,3},{3,2},{4,5},{5,4},{6,7},{7,6},{8,9},{9,8},{10,11... | collective-permute-start | bytes 3145736 | tf_op jit(solution)/shard_map/ppermute | solution.py:154
  66.3 23.1 %collective-permute-start.8 = (bf16[128,2048]{1,0:T(8,128)(2,1)S(1)}, bf16[128,2048]{1,0:T(8,128)(2,1)S(1)}, u32[]{:S(2)}, u32[]{:S(2)}) collective-permute-start(bf16[128,2048]{1,0:T(8,128)(2,1)S(1)} %slice.84), channel_id=1, source_target_pairs={{2,4},{4,2},{3,5},{5,3},{10,12},{12,10},{11,13},{13,11},{18,20},{2... | collective-permute-start | bytes 1572872 | tf_op jit(solution)/shard_map/ppermute | solution.py:158
  73.9 5.5 %collective-permute-start.18 = (s32[128,8]{0,1:T(8,128)S(1)}, s32[128,8]{0,1:T(8,128)S(1)}, u32[]{:S(2)}, u32[]{:S(2)}) collective-permute-start(s32[128,8]{0,1:T(8,128)S(1)} %collective-permute-done.15), channel_id=1, source_target_pairs={{2,4},{4,2},{3,5},{5,3},{10,12},{12,10},{11,13},{13,11},{18,20},{2... | collective-permute-start | bytes 12296 | tf_op jit(solution)/shard_map/ppermute | solution.py:158
  74.6 12.8 %collective-permute-start.17 = (s32[128,8]{0,1:T(8,128)S(1)}, s32[128,8]{0,1:T(8,128)S(1)}, u32[]{:S(2)}, u32[]{:S(2)}) collective-permute-start(s32[128,8]{0,1:T(8,128)S(1)} %collective-permute-done.16), channel_id=1, source_target_pairs={{2,0},{4,6},{3,1},{5,7},{10,8},{12,14},{11,9},{13,15},{18,16},{20,... | collective-permute-start | bytes 12296 | tf_op jit(solution)/shard_map/ppermute | solution.py:158
  79.5 10.0 %collective-permute-start.19 = (s32[128,8]{0,1:T(8,128)S(1)}, s32[128,8]{0,1:T(8,128)S(1)}, u32[]{:S(2)}, u32[]{:S(2)}) collective-permute-start(s32[128,8]{0,1:T(8,128)S(1)} %collective-permute-done.18), channel_id=1, source_target_pairs={{2,0},{4,6},{3,1},{5,7},{10,8},{12,14},{11,9},{13,15},{18,16},{20,... | collective-permute-start | bytes 12296 | tf_op jit(solution)/shard_map/ppermute | solution.py:158
  89.7 9.8 %collective-permute-start.9 = (bf16[128,2048]{1,0:T(8,128)(2,1)S(1)}, bf16[128,2048]{1,0:T(8,128)(2,1)S(1)}, u32[]{:S(2)}, u32[]{:S(2)}) collective-permute-start(bf16[128,2048]{1,0:T(8,128)(2,1)S(1)} %get-tuple-element.89), channel_id=1, source_target_pairs={{0,1},{1,0},{2,3},{3,2},{4,5},{5,4},{6,7},{7,6},{8,9},{9,8},{10,11... | collective-permute-start | bytes 1572872 | tf_op jit(solution)/shard_map/ppermute | solution.py:154
  91.3 11.1 %collective-permute-start.10 = (bf16[128,2048]{1,0:T(8,128)(2,1)S(1)}, bf16[128,2048]{1,0:T(8,128)(2,1)S(1)}, u32[]{:S(2)}, u32[]{:S(2)}) collective-permute-start(bf16[128,2048]{1,0:T(8,128)(2,1)S(1)} %collective-permute-done.8), channel_id=1, source_target_pairs={{2,0},{4,6},{3,1},{5,7},{10,8},{12,14},{11,9},{13,15},{18,16},{20,... | collective-permute-start | bytes 1572872 | tf_op jit(solution)/shard_map/ppermute | solution.py:158
  104.9 3.3 collective-permute-start.13
  107.6 2.8 collective-permute-start.11
  108.6 15.0 %collective-permute-start.14 = (bf16[128,2048]{1,0:T(8,128)(2,1)S(1)}, bf16[128,2048]{1,0:T(8,128)(2,1)}, u32[]{:S(2)}, u32[]{:S(2)}) collective-permute-start(bf16[128,2048]{1,0:T(8,128)(2,1)S(1)} %fusion.25), channel_id=1, source_target_pairs={{0,16},{16,0},{1,17},{17,1},{2,18},{18,2},{3,19},{19,3},{4,20},{20... | collective-permute-start | bytes 1572872 | tf_op jit(solution)/shard_map/ppermute | solution.py:154
  112.9 20.9 %collective-permute-start.12 = (bf16[128,2048]{1,0:T(8,128)(2,1)}, bf16[128,2048]{1,0:T(8,128)(2,1)}, u32[]{:S(2)}, u32[]{:S(2)}) collective-permute-start(bf16[128,2048]{1,0:T(8,128)(2,1)} %fusion.24), channel_id=1, source_target_pairs={{0,16},{16,0},{1,17},{17,1},{2,18},{18,2},{3,19},{19,3},{4,20},{20... | collective-permute-start | bytes 1572872 | tf_op jit(solution)/shard_map/ppermute | solution.py:154
  117.6 16.2 %copy-start.9 = (f32[2,128,2048]{2,1,0:T(8,128)S(1)}, f32[2,128,2048]{2,1,0:T(8,128)}, u32[]{:S(2)}) copy-start(f32[2,128,2048]{2,1,0:T(8,128)} %copy-done.8) | copy-start | bytes 6291460
  117.6 17.3 %copy-start.10 = (bf16[1,128,4096]{2,1,0:T(8,128)(2,1)S(1)}, bf16[1,128,4096]{2,1,0:T(8,128)(2,1)}, u32[]{:S(2)}) copy-start(bf16[1,128,4096]{2,1,0:T(8,128)(2,1)} %param.14) | copy-start | bytes 3145732
  124.7 10.7 %copy-start.3 = (f32[128,2048]{1,0:T(8,128)}, f32[128,2048]{1,0:T(8,128)S(1)}, u32[]{:S(2)}) copy-start(f32[128,2048]{1,0:T(8,128)S(1)} %bitcast_add_fusion.2) | copy-start | bytes 3145732
  136.3 10.7 %collective-permute-start.20 = (bf16[128,4096]{1,0:T(8,128)(2,1)S(1)}, bf16[128,4096]{1,0:T(8,128)(2,1)S(1)}, u32[]{:S(2)}, u32[]{:S(2)}) collective-permute-start(bf16[128,4096]{1,0:T(8,128)(2,1)S(1)} %fusion.9.refs_0_), channel_id=1, source_target_pairs={{2,4},{4,2},{3,5},{5,3},{10,12},{12,10},{11,13},{13,11},{18,20},{2... | collective-permute-start | bytes 3145736 | tf_op jit(solution)/shard_map/ppermute | solution.py:158
  137.2 24.5 %collective-permute-start.22 = (bf16[128,4096]{1,0:T(8,128)(2,1)S(1)}, bf16[128,4096]{1,0:T(8,128)(2,1)S(1)}, u32[]{:S(2)}, u32[]{:S(2)}) collective-permute-start(bf16[128,4096]{1,0:T(8,128)(2,1)S(1)} %fusion.9.refs_0_), channel_id=1, source_target_pairs={{0,2},{2,0},{4,6},{6,4},{1,3},{3,1},{5,7},{7,5},{8,10},{10,8},{12,... | collective-permute-start | bytes 3145736 | tf_op jit(solution)/shard_map/ppermute | solution.py:158
  142.6 30.5 %all-to-all-start.1 = ((bf16[8,32,4096]{2,1,0:T(8,128)(2,1)}), bf16[8,32,4096]{2,1,0:T(8,128)(2,1)}, u32[]{:S(2)}, u32[]{:S(2)}) async-start(bf16[8,32,4096]{2,1,0:T(8,128)(2,1)} %bitcast.37), calls=%async_computation.1 | async-start | bytes 4194304 | tf_op jit(solution)/shard_map/all_to_all | solution.py:279
  147.0 38.2 %collective-permute-start.21 = (bf16[128,4096]{1,0:T(8,128)(2,1)S(1)}, bf16[128,4096]{1,0:T(8,128)(2,1)}, u32[]{:S(2)}, u32[]{:S(2)}) collective-permute-start(bf16[128,4096]{1,0:T(8,128)(2,1)S(1)} %collective-permute-done.20.refs_0_), channel_id=1, source_target_pairs={{2,0},{4,6},{3,1},{5,7},{10,8},{12,14},{11,9},{13,15},{18,16},{20,... | collective-permute-start | bytes 3145736 | tf_op jit(solution)/shard_map/ppermute | solution.py:158
  161.7 26.5 %collective-permute-start.23 = (bf16[128,4096]{1,0:T(8,128)(2,1)S(1)}, bf16[128,4096]{1,0:T(8,128)(2,1)S(1)}, u32[]{:S(2)}, u32[]{:S(2)}) collective-permute-start(bf16[128,4096]{1,0:T(8,128)(2,1)S(1)} %collective-permute-done.22.refs_0_), channel_id=1, source_target_pairs={{2,4},{4,2},{3,5},{5,3},{10,12},{12,10},{11,13},{13,11},{18,20},{2... | collective-permute-start | bytes 3145736 | tf_op jit(solution)/shard_map/ppermute | solution.py:158
  173.2 30.5 %all-to-all-start.2 = ((bf16[8,32,4096]{2,1,0:T(8,128)(2,1)}), bf16[8,32,4096]{2,1,0:T(8,128)(2,1)}, u32[]{:S(2)}, u32[]{:S(2)}) async-start(bf16[8,32,4096]{2,1,0:T(8,128)(2,1)} %bitcast.39), calls=%async_computation.2 | async-start | bytes 4194304 | tf_op jit(solution)/shard_map/all_to_all | solution.py:279
  203.7 26.6 %collective-permute-start.24 = (bf16[128,4096]{1,0:T(8,128)(2,1)S(1)}, bf16[128,4096]{1,0:T(8,128)(2,1)S(1)}, u32[]{:S(2)}, u32[]{:S(2)}) collective-permute-start(bf16[128,4096]{1,0:T(8,128)(2,1)S(1)} %collective-permute-done.23.refs_0_), channel_id=1, source_target_pairs={{2,0},{4,6},{3,1},{5,7},{10,8},{12,14},{11,9},{13,15},{18,16},{20,... | collective-permute-start | bytes 3145736 | tf_op jit(solution)/shard_map/ppermute | solution.py:158
  205.0 30.5 %all-to-all-start.3 = ((bf16[8,32,4096]{2,1,0:T(8,128)(2,1)}), bf16[8,32,4096]{2,1,0:T(8,128)(2,1)}, u32[]{:S(2)}, u32[]{:S(2)}) async-start(bf16[8,32,4096]{2,1,0:T(8,128)(2,1)} %bitcast.48), calls=%async_computation.3 | async-start | bytes 4194304 | tf_op jit(solution)/shard_map/all_to_all | solution.py:279
  235.5 29.7 %all-to-all-start.4 = ((bf16[8,32,4096]{2,1,0:T(8,128)(2,1)}), bf16[8,32,4096]{2,1,0:T(8,128)(2,1)S(1)}, u32[]{:S(2)}, u32[]{:S(2)}) async-start(bf16[8,32,4096]{2,1,0:T(8,128)(2,1)} %bitcast.50), calls=%async_computation.4 | async-start | bytes 4194304 | tf_op jit(solution)/shard_map/all_to_all | solution.py:279
  279.4 29.8 %all-to-all-start.5 = ((bf16[8,32,4096]{2,1,0:T(8,128)(2,1)}), bf16[8,32,4096]{2,1,0:T(8,128)(2,1)S(1)}, u32[]{:S(2)}, u32[]{:S(2)}) async-start(bf16[8,32,4096]{2,1,0:T(8,128)(2,1)} %bitcast.118), calls=%async_computation.5 | async-start | bytes 4194304 | tf_op jit(solution)/shard_map/all_to_all | solution.py:279
  310.3 32.9 %all-to-all-start.6 = ((bf16[8,32,4096]{2,1,0:T(8,128)(2,1)}), bf16[8,32,4096]{2,1,0:T(8,128)(2,1)}, u32[]{:S(2)}, u32[]{:S(2)}) async-start(bf16[8,32,4096]{2,1,0:T(8,128)(2,1)} %bitcast.116), calls=%async_computation.6 | async-start | bytes 4194304 | tf_op jit(solution)/shard_map/all_to_all | solution.py:279
  314.7 27.5 %collective-permute-start.25 = (bf16[128,4096]{1,0:T(8,128)(2,1)S(1)}, bf16[128,4096]{1,0:T(8,128)(2,1)S(1)}, u32[]{:S(2)}, u32[]{:S(2)}) collective-permute-start(bf16[128,4096]{1,0:T(8,128)(2,1)S(1)} %combine.6), channel_id=1, source_target_pairs={{0,2},{6,4},{1,3},{7,5},{8,10},{14,12},{9,11},{15,13},{16,18},{22,... | collective-permute-start | bytes 3145736 | tf_op jit(solution)/shard_map/ppermute | solution.py:158
  343.2 30.5 %all-to-all-start.7 = ((bf16[8,32,4096]{2,1,0:T(8,128)(2,1)}), bf16[8,32,4096]{2,1,0:T(8,128)(2,1)}, u32[]{:S(2)}, u32[]{:S(2)}) async-start(bf16[8,32,4096]{2,1,0:T(8,128)(2,1)} %bitcast.121), calls=%async_computation.7 | async-start | bytes 4194304 | tf_op jit(solution)/shard_map/all_to_all | solution.py:279
  347.6 8.4 %copy-start.1 = (bf16[128,4096]{1,0:T(8,128)(2,1)S(1)}, bf16[128,4096]{1,0:T(8,128)(2,1)}, u32[]{:S(2)}) copy-start(bf16[128,4096]{1,0:T(8,128)(2,1)} %copy-done) | copy-start | bytes 3145732
  350.6 27.6 %collective-permute-start.26 = (bf16[128,4096]{1,0:T(8,128)(2,1)}, bf16[128,4096]{1,0:T(8,128)(2,1)}, u32[]{:S(2)}, u32[]{:S(2)}) collective-permute-start(bf16[128,4096]{1,0:T(8,128)(2,1)} %combine.7), channel_id=1, source_target_pairs={{0,2},{6,4},{1,3},{7,5},{8,10},{14,12},{9,11},{15,13},{16,18},{22,... | collective-permute-start | bytes 3145736 | tf_op jit(solution)/shard_map/ppermute | solution.py:158
  357.2 24.1 %collective-permute-start.28 = (bf16[128,4096]{1,0:T(8,128)(2,1)S(1)}, bf16[128,4096]{1,0:T(8,128)(2,1)S(1)}, u32[]{:S(2)}, u32[]{:S(2)}) collective-permute-start(bf16[128,4096]{1,0:T(8,128)(2,1)S(1)} %combine.9), channel_id=1, source_target_pairs={{2,4},{4,2},{3,5},{5,3},{10,12},{12,10},{11,13},{13,11},{18,20},{2... | collective-permute-start | bytes 3145736 | tf_op jit(solution)/shard_map/ppermute | solution.py:158
  373.8 37.6 %all-to-all-start.8 = ((bf16[8,32,4096]{2,1,0:T(8,128)(2,1)}), bf16[8,32,4096]{2,1,0:T(8,128)(2,1)}, u32[]{:S(2)}, u32[]{:S(2)}) async-start(bf16[8,32,4096]{2,1,0:T(8,128)(2,1)} %bitcast.120), calls=%async_computation.8 | async-start | bytes 4194304 | tf_op jit(solution)/shard_map/all_to_all | solution.py:279
  380.6 8.6 %collective-permute-start.27 = (bf16[128,4096]{1,0:T(8,128)(2,1)S(1)}, bf16[128,4096]{1,0:T(8,128)(2,1)S(1)}, u32[]{:S(2)}, u32[]{:S(2)}) collective-permute-start(bf16[128,4096]{1,0:T(8,128)(2,1)S(1)} %combine.8), channel_id=1, source_target_pairs={{2,4},{4,2},{3,5},{5,3},{10,12},{12,10},{11,13},{13,11},{18,20},{2... | collective-permute-start | bytes 3145736 | tf_op jit(solution)/shard_map/ppermute | solution.py:158
  381.3 6.7 %copy-start.4 = (f32[128,2048]{1,0:T(8,128)S(1)}, f32[128,2048]{1,0:T(8,128)}, u32[]{:S(2)}) copy-start(f32[128,2048]{1,0:T(8,128)} %copy-done.3) | copy-start | bytes 3145732
  383.7 27.6 %collective-permute-start.29 = (bf16[128,4096]{1,0:T(8,128)(2,1)S(1)}, bf16[128,4096]{1,0:T(8,128)(2,1)S(1)}, u32[]{:S(2)}, u32[]{:S(2)}) collective-permute-start(bf16[128,4096]{1,0:T(8,128)(2,1)S(1)} %combine.10), channel_id=1, source_target_pairs={{0,2},{2,0},{4,6},{6,4},{1,3},{3,1},{5,7},{7,5},{8,10},{10,8},{12,... | collective-permute-start | bytes 3145736 | tf_op jit(solution)/shard_map/ppermute | solution.py:158
  (18 other events, 50.4 us)
